TPU v7x, 128 devices: a whole 4x4x4 slice. The times are simulated.
128 devices in a mesh: lat: 16 (over y, z), lon: 8 (over x, core).
Axes of the slice: x: 4, y: 4, z: 4, core: 2. Of those that a mesh axis runs over, the one named last changes fastest.
Arguments:
- coarse_field: bfloat16 [96, 720, 1440], P(None, 'lat', 'lon'), may hold values from -6 to 6
- forward_table: bfloat16 [368, 720, 720], P('lon', 'lat'), as said below
- degree_mixing_weight: bfloat16 [720, 96, 192], P('lat'), may hold values from -0.4375 to 0.4375
- synthesis_weight_table: bfloat16 [368, 720, 1024], P('lon', None, 'lat'), as said below
Outputs:
- upsampled: bfloat16 [96, 1024, 3600], P(None, 'lat', 'lon')
Inputs may be any that keep to these rules, and one draw needn't show every extreme that they name: forward_table[m, l, q] is zero wherever l < m. synthesis_weight_table[m, l, o] is zero wherever l < m.
All inputs are finite; a program needn't handle non-finite values.
Results may differ from a plain program's by a relative error of at most 0.012.
Values may be sent and summed in bfloat16 or wider, within the bound.
No kernel may reach another device: no remote copies, remote signals or barrier semaphores. Data moves between devices by JAX's collectives and lax.ppermute only.
A program may use at most 128 MiB of HBM per device.

v0:
```python
import math

import jax
import jax.numpy as jnp
from jax import lax
from jax.sharding import PartitionSpec as P

KEPT_ORDERS = 368
LON_IN = 1440
LON_OUT = 3600


def phase_table(order_ids, points, modulus, factor):
    phases = order_ids[:, None] * points[None, :] % modulus
    angles = 2.0 * math.pi / modulus * phases.astype(jnp.float32)
    return jnp.stack([jnp.cos(angles) * factor, -jnp.sin(angles) * factor], axis=1)


def local(coarse_field, forward_table, degree_mixing_weight, synthesis_weight_table):
    channels = coarse_field.shape[0]
    order_count = forward_table.shape[0]
    degree_count = forward_table.shape[1]
    out_rows = synthesis_weight_table.shape[2]
    widened = lax.all_to_all(coarse_field, "lon", split_axis=0, concat_axis=2, tiled=True)
    order_ids = jnp.arange(KEPT_ORDERS, dtype=jnp.int32)
    analysis = phase_table(order_ids, jnp.arange(LON_IN, dtype=jnp.int32), LON_IN, LON_IN ** (-0.5))
    analysis = (
        jnp.transpose(analysis, (2, 0, 1)).reshape(LON_IN, 2 * KEPT_ORDERS).astype(jnp.bfloat16)
    )
    spectrum = jnp.dot(
        widened.reshape(-1, LON_IN), analysis, preferred_element_type=jnp.float32
    ).astype(jnp.bfloat16)
    spectrum = spectrum.reshape(widened.shape[0], widened.shape[1], 2 * KEPT_ORDERS)
    per_order_values = lax.all_to_all(spectrum, "lon", split_axis=2, concat_axis=0, tiled=True)
    shard_rows = lax.all_gather(per_order_values, "lat", axis=1, tiled=True)
    row_count = shard_rows.shape[1]
    tab_slice = forward_table
    arranged = shard_rows.reshape(channels, row_count, order_count, 2)
    contrib = lax.dot_general(
        tab_slice, arranged, (((2,), (1,)), ((0,), (2,))), preferred_element_type=jnp.float32
    )
    coefficients = contrib.reshape(order_count, degree_count, 2 * channels).astype(jnp.bfloat16)
    real_imaginary_pair = coefficients.reshape(order_count, degree_count, channels, 2)
    with_real = jnp.einsum(
        "ynt,ntu->ynu",
        real_imaginary_pair[..., 0],
        degree_mixing_weight,
        preferred_element_type=jnp.float32,
    )
    with_imag = jnp.einsum(
        "ynt,ntu->ynu",
        real_imaginary_pair[..., 1],
        degree_mixing_weight,
        preferred_element_type=jnp.float32,
    )
    real_out = with_real[..., :channels] - with_imag[..., channels:]
    imag_out = with_real[..., channels:] + with_imag[..., :channels]
    mixed_coef = (
        jnp.stack([real_out, imag_out], axis=-1)
        .reshape(order_count, degree_count, 2 * channels)
        .astype(jnp.bfloat16)
    )
    shard_rows = lax.all_gather(mixed_coef, "lat", axis=1, tiled=True)
    tab_slice = synthesis_weight_table
    contrib = lax.dot_general(
        tab_slice, shard_rows, (((1,), (1,)), ((0,), (0,))), preferred_element_type=jnp.float32
    )
    grid_orders = contrib.astype(jnp.bfloat16)
    grid_split = grid_orders.reshape(order_count, out_rows, channels, 2)
    all_orders = lax.all_to_all(grid_split, "lon", split_axis=2, concat_axis=0, tiled=True)
    synth_tab = phase_table(
        order_ids, jnp.arange(LON_OUT, dtype=jnp.int32), LON_OUT, KEPT_ORDERS ** (-0.5)
    ).astype(jnp.bfloat16)
    waves_out = lax.dot_general(
        all_orders, synth_tab, (((0, 3), (0, 1)), ((), ())), preferred_element_type=jnp.float32
    ).astype(jnp.bfloat16)
    result = lax.all_to_all(waves_out, "lon", split_axis=2, concat_axis=1, tiled=True)
    return jnp.transpose(result, (1, 0, 2))


def solution(mesh):
    in_specs = (
        P(None, "lat", "lon"),
        P("lon", "lat", None),
        P("lat", None, None),
        P("lon", None, "lat"),
    )
    out_specs = P(None, "lat", "lon")
    return jax.shard_map(local, mesh=mesh, in_specs=in_specs, out_specs=out_specs, check_vma=False)
```

profile of v0, /device:TPU:1, one launch (start us, length us, event | category | flops | bytes accessed | tf_op | source)
XLA Modules:
  0.0 601.7 jit_solution(16734790631742257504)
XLA Ops:
  6.5 0.0 copy-start
  6.5 5.7 copy.56
  12.3 5.8 all-to-all-start
  18.1 0.0 all-gather.3.cloned.1.call-start
  18.1 9.7 %multiply_convert_fusion.2 = (bf16[368,1,1440]{0,2,1:T(8,128)(2,1)S(1)}, bf16[368,1,1440]{0,2,1:T(8,128)(2,1)S(1)}) fusion(), kind=kLoop, calls=%fused_computation.21 | loop fusion | flops 7418880 | bytes 2119680 | tf_op jit(solution)/shard_map/convert.7
  27.8 1.8 maximum_bitcast_fusion.2
  29.6 6.8 %copy.55 = bf16[1440,368,2]{0,2,1:T(2,128)(2,1)} copy(bf16[1440,368,2]{1,0,2:T(8,128)(2,1)} %maximum_bitcast_fusion.2) | data formatting | bytes 4239360 | tf_op jit(solution)/shard_map/convert_element_type | solution.py:28
  36.4 5.7 convert_element_type.68
  42.1 5.2 all-to-all-done
  47.3 4.3 copy.57
  51.6 4.7 reshape.139
  56.3 4.5 fusion.28
  60.8 2.3 reshape.140
  63.1 4.9 copy.58
  68.0 6.0 %reshape.146 = bf16[8,2,24840]{2,1,0:T(2,128)(2,1)} reshape(bf16[736,12,45]{2,1,0:T(8,128)(2,1)} %bitcast.75) | data formatting | bytes 1589760
  74.0 18.0 %all_to_all.69 = bf16[8,2,24840]{2,1,0:T(2,128)(2,1)} all-to-all(bf16[8,2,24840]{2,1,0:T(2,128)(2,1)} %reshape.146), channel_id=1, replica_groups=mesh['lat'=16,'lon'=8] {'lon'}, dimensions={0} | all-to-all | bytes 1589760 | tf_op jit(solution)/shard_map/all_to_all | solution.py:34
  92.0 6.2 %reshape.147 = bf16[736,12,45]{2,1,0:T(8,128)(2,1)} reshape(bf16[8,2,24840]{2,1,0:T(2,128)(2,1)} %all_to_all.69) | data formatting | bytes 1589760
  98.2 4.7 copy.60
  102.9 2.5 copy.61
  105.5 0.0 all-gather.3.cloned.1.call-update
  105.5 0.2 all-gather.5.cloned.1.call-start
  105.7 116.4 %all-gather.3.cloned.1.call-done = bf16[96,720,92]{2,0,1:T(8,128)(2,1)} async-done(((bf16[96,45,92]{2,0,1:T(8,128)(2,1)}), bf16[96,720,92]{2,0,1:T(8,128)(2,1)}) %all-gather.3.cloned.1.call-update) | async-done | bytes 12718096 | tf_op jit(solution)/shard_map/all_gather | solution.py:35
  222.1 25.6 %copy.62 = bf16[96,720,92]{1,0,2:T(8,128)(2,1)} copy(bf16[96,720,92]{2,0,1:T(8,128)(2,1)} %all-gather.3.cloned.1.call-done) | data formatting | bytes 25436160 | tf_op jit(solution)/shard_map/all_gather | solution.py:35
  247.7 0.0 copy-done
  247.7 9.8 %fusion.25 = bf16[46,45,96,2]{2,1,3,0:T(8,128)(2,1)S(1)} fusion(bf16[96,720,46,2]{1,0,3,2:T(8,128)(2,1)} %bitcast.73, bf16[46,45,720,1]{2,0,1,3:T(8,128)(2,1)S(1)} %bitcast.70), kind=kOutput, calls=%fused_computation.33 | convolution fusion | flops 572711040 | bytes 16493760 | tf_op jit(solution)/shard_map/dot_general | solution.py:39
  257.5 0.0 copy-start.2
  257.5 0.1 slice_bitcast_fusion.1
  257.6 1.5 copy-done.2
  259.1 0.4 convolution_bitcast_fusion.1
  259.6 0.4 convolution_bitcast_fusion
  260.0 0.6 fusion.31
  260.7 0.3 pad_maximum_fusion
  260.9 3.4 copy.66
  264.4 2.4 copy.67
  266.7 0.0 all-gather.5.cloned.1.call-update
  266.8 115.9 %all-gather.5.cloned.1.call-done = bf16[46,720,192]{2,0,1:T(8,128)(2,1)} async-done(((bf16[46,45,192]{2,0,1:T(8,128)(2,1)}), bf16[46,720,192]{2,0,1:T(8,128)(2,1)}) %all-gather.5.cloned.1.call-update) | async-done | bytes 12718096 | tf_op jit(solution)/shard_map/all_gather | solution.py:63
  382.7 13.7 %fusion.22 = bf16[46,64,192]{2,1,0:T(8,128)(2,1)} fusion(bf16[46,720,64]{1,2,0:T(8,128)(2,1)} %param.7, bf16[46,720,192]{2,0,1:T(8,128)(2,1)} %all-gather.5.cloned.1.call-done), kind=kOutput, calls=%fused_computation.31 | convolution fusion | flops 814522368 | bytes 18087936 | tf_op jit(solution)/shard_map/dot_general | solution.py:65
  396.3 3.3 copy.69
  399.6 2.9 copy.98
  402.5 4.3 reshape.148
  406.8 5.0 all-to-all-start.2
  411.8 23.9 %multiply_convert_fusion = (bf16[368,1,3600]{2,0,1:T(8,128)(2,1)}, bf16[368,1,3600]{2,0,1:T(8,128)(2,1)}) fusion(), kind=kLoop, calls=%fused_computation.9 | loop fusion | flops 18547200 | bytes 5299200 | tf_op jit(solution)/shard_map/convert.1
  435.7 0.0 all-to-all-done.2
  435.7 3.2 reshape.149
  438.9 1.8 copy.71
  440.7 3.7 copy.72
  444.4 3.1 all_to_all.60
  447.5 10.3 %bitcast_convert_fusion = bf16[64,12,3600]{2,0,1:T(8,128)(2,1)} fusion(bf16[368,64,12,2]{0,1,3,2:T(8,128)(2,1)} %all_to_all.60, bf16[368,1,3600]{2,0,1:T(8,128)(2,1)} %get-tuple-element.11, bf16[368,1,3600]{2,0,1:T(8,128)(2,1)} %get-tuple-element.12), kind=kOutput, calls=%fused_computation.2 | convolution fusion | flops 4075200000 | bytes 11959296 | tf_op jit(solution)/shard_map/dot_general | solution.py:74
  457.8 17.9 %copy.73 = bf16[64,12,3600]{0,1,2:T(8,128)(2,1)} copy(bf16[64,12,3600]{2,0,1:T(8,128)(2,1)} %bitcast_convert_fusion) | data formatting | bytes 11059200 | tf_op jit(solution)/shard_map/convert_element_type | solution.py:76
  475.7 15.6 %reshape.150 = bf16[8,2,172800]{2,1,0:T(2,128)(2,1)} reshape(bf16[3600,12,64]{2,1,0:T(8,128)(2,1)} %bitcast.71) | data formatting | bytes 11059200
  491.3 69.5 %all_to_all.70 = bf16[8,2,172800]{2,1,0:T(2,128)(2,1)} all-to-all(bf16[8,2,172800]{2,1,0:T(2,128)(2,1)} %reshape.150), channel_id=1, replica_groups=mesh['lat'=16,'lon'=8] {'lon'}, dimensions={0} | all-to-all | bytes 11059200 | tf_op jit(solution)/shard_map/all_to_all | solution.py:77
  560.8 16.4 %reshape.151 = bf16[3600,12,64]{2,1,0:T(8,128)(2,1)} reshape(bf16[8,2,172800]{2,1,0:T(2,128)(2,1)} %all_to_all.70) | data formatting | bytes 11059200
  577.2 0.0 copy-start.1
  577.2 17.3 %copy.74 = bf16[64,8,12,450]{3,0,2,1:T(8,128)(2,1)} copy(bf16[64,8,12,450]{0,2,3,1:T(8,128)(2,1)} %bitcast.72) | data formatting | bytes 11059200 | tf_op jit(solution)/shard_map/all_to_all | solution.py:77
  594.4 0.0 copy-done.1
Async XLA Ops:
  6.5 241.1 %copy-start = (bf16[46,45,720]{2,0,1:T(8,128)(2,1)S(1)}, bf16[46,45,720]{2,0,1:T(8,128)(2,1)}, u32[]{:S(2)}) copy-start(bf16[46,45,720]{2,0,1:T(8,128)(2,1)} %param.5) | copy-start | bytes 8942404
  12.3 35.0 %all-to-all-start = ((bf16[96,45,180]{2,1,0:T(8,128)(2,1)}), bf16[96,45,180]{2,1,0:T(8,128)(2,1)}, u32[]{:S(2)}, u32[]{:S(2)}) async-start(bf16[96,45,180]{2,1,0:T(8,128)(2,1)} %copy.56), calls=%async_computation | async-start | bytes 4718592 | tf_op jit(solution)/shard_map/all_to_all | solution.py:24
  18.1 204.0 %all-gather.3.cloned.1.call-start = ((), (), s32[]{:S(2)}) async-start(), calls=%async_computation.4 | async-start | bytes 18800640 | tf_op jit(solution)/shard_map/all_gather | solution.py:35
  105.5 277.2 %all-gather.5.cloned.1.call-start = ((), (), s32[]{:S(2)}) async-start(), calls=%async_computation.5 | async-start | bytes 18800640 | tf_op jit(solution)/shard_map/all_gather | solution.py:63
  257.5 1.6 copy-start.2
  406.8 28.9 %all-to-all-start.2 = ((bf16[8,2,35328]{2,1,0:T(2,128)(2,1)}), bf16[8,2,35328]{2,1,0:T(2,128)(2,1)}, u32[]{:S(2)}, u32[]{:S(2)}) async-start(bf16[8,2,35328]{2,1,0:T(2,128)(2,1)} %reshape.148), calls=%async_computation.2 | async-start | bytes 2260992 | tf_op jit(solution)/shard_map/all_to_all | solution.py:70
  577.2 17.3 %copy-start.1 = (bf16[46,45,720]{2,0,1:T(8,128)(2,1)S(1)}, bf16[46,45,720]{2,0,1:T(8,128)(2,1)}, u32[]{:S(2)}) copy-start(bf16[46,45,720]{2,0,1:T(8,128)(2,1)} %param.5) | copy-start | bytes 8942404
Sparse Core Ops, SparseCore 0:
  105.6 116.4 all-gather.2
  266.9 115.7 all-gather.4
where the time goes:
time: 613 us; the launch traced here: 602 us
  waiting for transfers between devices  237 us (39%)
  local copies, waits for them, and re-layouts  176 us (29%)
  blocking collectives  87.5 us (14%)
  matrix products  39.1 us (6%)
  other arithmetic  36.3 us (6%)
  between operations  13.9 us (2%)
  starting transfers between devices  11 us (2%)
    all_gather x1, waiting for transfers between devices, local(): shard_rows = lax.all_gather(per_order_values, 'lat', axis=1, tiled=True)  116 us
    all_gather x1, waiting for transfers between devices, local(): shard_rows = lax.all_gather(mixed_coef, 'lat', axis=1, tiled=True)  116 us
    all_to_all x1, blocking collectives, local(): lax.all_to_all(waves_out, 'lon', split_axis=2, concat_axis=1, tiled=True)  69.5 us
    unnamed x13, local copies, waits for them, and re-layouts  58.9 us
    another operation x2, other arithmetic  33.6 us
    all_gather x1, local copies, waits for them, and re-layouts, local(): shard_rows = lax.all_gather(per_order_values, 'lat', axis=1, tiled=True)  25.6 us
    all_to_all x1, blocking collectives, local(): lax.all_to_all(spectrum, 'lon', split_axis=2, concat_axis=0, tiled=True)  18 us
    convert_element_type x1, local copies, waits for them, and re-layouts, local(): waves_out = lax.dot_general(all_orders, synth_tab, (((0, 3), (0, 1)), (()...  17.9 us
  transfers between devices with their start and end apart: 4, of which 3 were waited for; matrix products, arithmetic and copies ran while one was open for 8% of the time, Pallas kernels for 0%

commit v1 on v0

v1 whole, which is shorter than its diff:
```python
import math

import jax
import jax.numpy as jnp
from jax import lax
from jax.sharding import PartitionSpec as P

CHAN = 96
KEPT_ORDERS = 368
LON_IN = 1440
LON_OUT = 3600
LATS = 16
LONS = 8
OWN = 46
SLOTS = 48
EACH = 3
ROWS = 45
QPAD = 48
QEACH = 6
BF = jnp.bfloat16


def waves(order_ids, valid, points, modulus, factor):
    phases = order_ids * points % modulus
    angles = 2.0 * math.pi / modulus * phases.astype(jnp.float32)
    scale = jnp.where(valid, factor, 0.0)
    return (jnp.cos(angles) * scale).astype(BF), (-jnp.sin(angles) * scale).astype(BF)


def swap(x, axis):
    return lax.all_to_all(x, axis, split_axis=0, concat_axis=0, tiled=True)


def local(coarse_field, forward_table, degree_mixing_weight, synthesis_weight_table):
    ftab = jnp.pad(forward_table, ((0, SLOTS - OWN), (0, 0), (0, 0)))
    ftab = swap(ftab.reshape(LATS, EACH, ROWS, 720), "lat")
    wtab = jnp.transpose(synthesis_weight_table, (0, 2, 1))
    wtab = jnp.pad(wtab, ((0, SLOTS - OWN), (0, 0), (0, 0)))
    wtab = swap(wtab.reshape(LATS, EACH, 64, 720), "lat")

    field = jnp.pad(jnp.transpose(coarse_field, (1, 2, 0)), ((0, QPAD - ROWS), (0, 0), (0, 0)))
    field = swap(field.reshape(LONS, QEACH, 180, CHAN), "lon")

    a = jnp.arange(LATS * LONS * EACH, dtype=jnp.int32)
    slot = (a // (LONS * EACH)) * EACH + a % EACH
    column = (a // EACH) % LONS
    valid = (slot < OWN)[:, None]
    ids = (column * OWN + jnp.minimum(slot, OWN - 1))[:, None]
    points = jnp.arange(LON_IN, dtype=jnp.int32)[None, :]
    cos_in, sin_in = waves(ids, valid, points, LON_IN, LON_IN ** (-0.5))
    field = jnp.transpose(field, (1, 0, 2, 3)).reshape(QEACH, LON_IN, CHAN)
    parts = [
        jnp.einsum("np,qpc->nqc", t, field, preferred_element_type=jnp.float32).astype(BF)
        for t in (cos_in, sin_in)
    ]
    spectrum = jnp.concatenate(parts, axis=-1)
    spectrum = spectrum.reshape(LATS * LONS, EACH, QEACH, 2 * CHAN)
    spectrum = swap(spectrum, ("lat", "lon")).reshape(LATS, LONS, EACH, QEACH, 2 * CHAN)
    spectrum = jnp.transpose(spectrum, (2, 0, 1, 3, 4)).reshape(EACH, LATS, QPAD, 2 * CHAN)
    spectrum = spectrum[:, :, :ROWS].reshape(EACH, 720, 2 * CHAN)

    coef = jnp.einsum("ajlq,jqn->ajln", ftab, spectrum, preferred_element_type=jnp.float32)
    coef = swap(coef.astype(BF), "lat").reshape(SLOTS, ROWS, 2 * CHAN)

    w = degree_mixing_weight
    turned = jnp.concatenate([-w[..., CHAN:], w[..., :CHAN]], axis=-1)
    both = jnp.concatenate([w, turned], axis=1)
    mixed = jnp.einsum("mlt,ltu->mlu", coef, both, preferred_element_type=jnp.float32)
    mixed = swap(mixed.astype(BF).reshape(LATS, EACH, ROWS, 2 * CHAN), "lat")
    mixed = jnp.transpose(mixed, (1, 0, 2, 3)).reshape(EACH, 720, 2 * CHAN)

    rows = jnp.einsum("ajol,jln->ajon", wtab, mixed, preferred_element_type=jnp.float32)
    rows = swap(rows.astype(BF), "lat").reshape(SLOTS, 64, 2, CHAN)

    every = lax.all_gather(rows, "lon", axis=0, tiled=True)
    b = jnp.arange(LONS * SLOTS, dtype=jnp.int32)
    slot = b % SLOTS
    ids = ((b // SLOTS) * OWN + jnp.minimum(slot, OWN - 1))[:, None]
    points = (lax.axis_index("lon") * 450 + jnp.arange(450, dtype=jnp.int32))[None, :]
    cos_out, sin_out = waves(ids, (slot < OWN)[:, None], points, LON_OUT, KEPT_ORDERS ** (-0.5))
    table = jnp.stack([cos_out, sin_out], axis=1)
    out = jnp.einsum("norc,nrp->cop", every, table, preferred_element_type=jnp.float32)
    return out.astype(BF)


def solution(mesh):
    in_specs = (
        P(None, "lat", "lon"),
        P("lon", "lat", None),
        P("lat", None, None),
        P("lon", None, "lat"),
    )
    out_specs = P(None, "lat", "lon")
    return jax.shard_map(local, mesh=mesh, in_specs=in_specs, out_specs=out_specs, check_vma=False)
```

time: 613 us -> 405 us (0.66); the launches traced: 602 us -> 402 us
  local copies, waits for them, and re-layouts: 176 us -> 41.1 us
  blocking collectives: 87.5 us -> 23.5 us
  other arithmetic: 36.3 us -> 5.4 us
  starting transfers between devices: 11 us -> 40.8 us
    all_to_all x2 -> x6, waiting for transfers between devices: 5.2 us -> 172 us  [swap(): return lax.all_to_all(x, axis, split_axis=0, concat_axis=0, tiled=True)]
    all_gather x2 -> x1, waiting for transfers between devices: 232 us -> 65.4 us  [local(): every = lax.all_gather(rows, 'lon', axis=0, tiled=True)]
    all_to_all x2 -> x1, blocking collectives: 87.5 us -> 23.5 us  [swap(): return lax.all_to_all(x, axis, split_axis=0, concat_axis=0, tiled=True)]
    unnamed x13 -> x7, local copies, waits for them, and re-layouts: 58.9 us -> 4.43 us
    all_to_all x7 -> x1, local copies, waits for them, and re-layouts: 37.4 us -> 0.3 us  [swap(): return lax.all_to_all(x, axis, split_axis=0, concat_axis=0, tiled=True)]
    another operation x4 -> x0, other arithmetic: 34.5 us -> none
    all_to_all x2 -> x6, starting transfers between devices: 10.8 us -> 40.7 us  [swap(): return lax.all_to_all(x, axis, split_axis=0, concat_axis=0, tiled=True)]
    convert_element_type x5 -> x4, local copies, waits for them, and re-layouts: 36.1 us -> 8.99 us  [the longest x1 6.29 us: local(): return out.astype(BF)]
  transfers between devices with their start and end apart: 4 -> 7, of which waited for: 3 -> 7; matrix products, arithmetic and copies ran while one was open for 8% -> 4% of each run, Pallas kernels for 0% -> 0%
where the time goes in v1:
time: 405 us; the launch traced here: 402 us
  waiting for transfers between devices  238 us (59%)
  local copies, waits for them, and re-layouts  41.1 us (10%)
  starting transfers between devices  40.8 us (10%)
  matrix products  39.3 us (10%)
  blocking collectives  23.5 us (6%)
  between operations  13.9 us (3%)
  other arithmetic  5.4 us (1%)
    all_to_all x6, waiting for transfers between devices, swap(): return lax.all_to_all(x, axis, split_axis=0, concat_axis=0, tiled=True)  172 us
    all_gather x1, waiting for transfers between devices, local(): every = lax.all_gather(rows, 'lon', axis=0, tiled=True)  65.4 us
    all_to_all x6, starting transfers between devices, swap(): return lax.all_to_all(x, axis, split_axis=0, concat_axis=0, tiled=True)  40.7 us
    all_to_all x1, blocking collectives, swap(): return lax.all_to_all(x, axis, split_axis=0, concat_axis=0, tiled=True)  23.5 us
    unnamed x2, matrix products  20.9 us
    dot_general x1, matrix products, local(): jnp.einsum('norc,nrp->cop', every, table, preferred_element_type=jnp.floa...  8.65 us
  transfers between devices with their start and end apart: 7, of which 7 were waited for; matrix products, arithmetic and copies ran while one was open for 4% of the time, Pallas kernels for 0%

profile of v1, /device:TPU:1, one launch (start us, length us, event | category | flops | bytes accessed | tf_op | source)
XLA Modules:
  0.0 401.7 jit_solution(15868297208371770868)
XLA Ops:
  6.5 3.4 pad.12
  9.9 5.8 %all-to-all-start = ((bf16[8,6,180,96]{3,2,1,0:T(8,128)(2,1)}), bf16[8,6,180,96]{3,2,1,0:T(8,128)(2,1)S(1)}, u32[]{:S(2)}, u32[]{:S(2)}) async-start(bf16[8,6,180,96]{3,2,1,0:T(8,128)(2,1)} %bitcast.54), calls=%async_computation | async-start | bytes 4521984 | tf_op jit(solution)/shard_map/all_to_all | solution.py:31
  15.8 28.1 %all-to-all-done = bf16[8,6,180,96]{3,2,1,0:T(8,128)(2,1)S(1)} async-done(((bf16[8,6,180,96]{3,2,1,0:T(8,128)(2,1)}), bf16[8,6,180,96]{3,2,1,0:T(8,128)(2,1)S(1)}, u32[]{:S(2)}, u32[]{:S(2)}) %all-to-all-start) | async-done | bytes 1658912 | tf_op jit(solution)/shard_map/all_to_all | solution.py:31
  43.8 0.0 copy-start
  43.8 1.4 copy-done
  45.2 3.5 copy.41
  48.7 4.2 %reshape.269 = bf16[6,1440,96]{1,2,0:T(8,128)(2,1)} reshape(bf16[6,8,180,96]{2,1,3,0:T(8,128)(2,1)S(1)} %copy.41) | data formatting | bytes 3317760 | tf_op jit(solution)/shard_map/reshape | solution.py:51
  52.9 0.0 copy-start.2
  52.9 11.1 %fusion.35 = f32[384,576]{0,1:S(1)} fusion(bf16[1440,576]{0,1:T(8,128)(2,1)} %bitcast.60, f32[384]{0:T(512)S(1)} %compare_select_fusion, s32[384]{0:T(512)S(1)} %fusion.68), kind=kOutput, calls=%fused_computation.29 | convolution fusion | flops 643092480 | bytes 2546688
  64.1 0.0 copy-done.2
  64.1 9.8 %fusion.34 = f32[384,576]{0,1:S(1)} fusion(bf16[1440,576]{0,1:T(8,128)(2,1)S(1)} %bitcast.61, f32[384]{0:T(512)S(1)} %compare_select_fusion, s32[384]{0:T(512)S(1)} %fusion.68), kind=kOutput, calls=%fused_computation.28 | convolution fusion | flops 643645440 | bytes 2546688
  73.8 0.1 convert_element_type.88
  73.9 0.1 convert_element_type.86
  74.0 0.1 pad_maximum_fusion
  74.1 0.6 copy.42
  74.7 0.7 reshape.270
  75.4 1.7 copy.43
  77.1 9.0 %all-to-all-start.1 = ((bf16[128,3,6,192]{3,1,2,0:T(4,128)(2,1)}), bf16[128,3,6,192]{3,1,2,0:T(4,128)(2,1)S(1)}, u32[]{:S(2)}, u32[]{:S(2)}) async-start(bf16[128,3,6,192]{3,1,2,0:T(4,128)(2,1)} %copy.43), calls=%async_computation.1 | async-start | bytes 3145728 | tf_op jit(solution)/shard_map/all_to_all | solution.py:31
  86.1 3.0 copy.64
  89.2 2.2 pad.13.clone
  91.3 19.7 %all-to-all-done.1 = bf16[128,3,6,192]{3,1,2,0:T(4,128)(2,1)S(1)} async-done(((bf16[128,3,6,192]{3,1,2,0:T(4,128)(2,1)}), bf16[128,3,6,192]{3,1,2,0:T(4,128)(2,1)S(1)}, u32[]{:S(2)}, u32[]{:S(2)}) %all-to-all-start.1) | async-done | bytes 884768 | tf_op jit(solution)/shard_map/all_to_all | solution.py:31
  111.0 4.7 %all-to-all-start.2 = ((bf16[16,3,45,720]{3,2,1,0:T(8,128)(2,1)}), bf16[16,3,45,720]{3,2,1,0:T(8,128)(2,1)}, u32[]{:S(2)}, u32[]{:S(2)}) async-start(bf16[16,3,45,720]{3,2,1,0:T(8,128)(2,1)} %bitcast.12), calls=%async_computation.2 | async-start | bytes 7077888 | tf_op jit(solution)/shard_map/all_to_all | solution.py:31
  115.7 0.3 copy.80
  116.1 0.3 copy.45
  116.3 0.1 slice.12
  116.4 0.4 copy.46
  116.8 0.6 reshape.290
  117.4 44.0 %all-to-all-done.2 = bf16[16,3,45,720]{3,2,1,0:T(8,128)(2,1)} async-done(((bf16[16,3,45,720]{3,2,1,0:T(8,128)(2,1)}), bf16[16,3,45,720]{3,2,1,0:T(8,128)(2,1)}, u32[]{:S(2)}, u32[]{:S(2)}) %all-to-all-start.2) | async-done | bytes 3110432 | tf_op jit(solution)/shard_map/all_to_all | solution.py:31
  161.3 3.1 fusion.28
  164.4 0.0 copy-start.1
  164.4 1.1 copy.50
  165.5 11.7 %all-to-all-start.3 = ((bf16[16,3,45,192]{3,2,1,0:T(8,128)(2,1)}), bf16[16,3,45,192]{3,2,1,0:T(8,128)(2,1)S(1)}, u32[]{:S(2)}, u32[]{:S(2)}) async-start(bf16[16,3,45,192]{3,2,1,0:T(8,128)(2,1)} %copy.50), calls=%async_computation.3 | async-start | bytes 2359296 | tf_op jit(solution)/shard_map/all_to_all | solution.py:31
  177.2 0.0 copy-done.1
  177.2 1.9 slice_negate_fusion
  179.1 14.3 %all-to-all-done.3 = bf16[16,3,45,192]{3,2,1,0:T(8,128)(2,1)S(1)} async-done(((bf16[16,3,45,192]{3,2,1,0:T(8,128)(2,1)}), bf16[16,3,45,192]{3,2,1,0:T(8,128)(2,1)S(1)}, u32[]{:S(2)}, u32[]{:S(2)}) %all-to-all-start.3) | async-done | bytes 829472 | tf_op jit(solution)/shard_map/all_to_all | solution.py:31
  193.4 3.0 fusion.31
  196.4 1.4 copy.52
  197.8 4.3 %all-to-all-start.4 = ((bf16[16,3,45,192]{3,2,1,0:T(8,128)(2,1)}), bf16[16,3,45,192]{3,2,1,0:T(8,128)(2,1)S(1)}, u32[]{:S(2)}, u32[]{:S(2)}) async-start(bf16[16,3,45,192]{3,2,1,0:T(8,128)(2,1)} %bitcast.16), calls=%async_computation.4 | async-start | bytes 2359296 | tf_op jit(solution)/shard_map/all_to_all | solution.py:31
  202.1 5.3 %pad.14 = bf16[48,64,720]{2,1,0:T(8,128)(2,1)} pad(bf16[46,64,720]{2,1,0:T(8,128)(2,1)} %bitcast.57, bf16[]{:T(256)} %constant.94.clone.1), padding=0_2x0_0x0_0 | pad | bytes 8663042 | tf_op jit(solution)/shard_map/jit(_pad)/pad | solution.py:38
  207.4 10.5 %all-to-all-done.4 = bf16[16,3,45,192]{3,2,1,0:T(8,128)(2,1)S(1)} async-done(((bf16[16,3,45,192]{3,2,1,0:T(8,128)(2,1)}), bf16[16,3,45,192]{3,2,1,0:T(8,128)(2,1)S(1)}, u32[]{:S(2)}, u32[]{:S(2)}) %all-to-all-start.4) | async-done | bytes 829472 | tf_op jit(solution)/shard_map/all_to_all | solution.py:31
  218.0 5.2 %all-to-all-start.5 = ((bf16[16,3,64,720]{3,2,1,0:T(8,128)(2,1)}), bf16[16,3,64,720]{3,2,1,0:T(8,128)(2,1)}, u32[]{:S(2)}, u32[]{:S(2)}) async-start(bf16[16,3,64,720]{3,2,1,0:T(8,128)(2,1)} %bitcast.52), calls=%async_computation.5 | async-start | bytes 9437184 | tf_op jit(solution)/shard_map/all_to_all | solution.py:31
  223.2 0.0 all-gather.2.cloned.1.call-start
  223.3 0.1 copy.53
  223.4 0.6 reshape.293
  223.9 55.6 %all-to-all-done.5 = bf16[16,3,64,720]{3,2,1,0:T(8,128)(2,1)} async-done(((bf16[16,3,64,720]{3,2,1,0:T(8,128)(2,1)}), bf16[16,3,64,720]{3,2,1,0:T(8,128)(2,1)}, u32[]{:S(2)}, u32[]{:S(2)}) %all-to-all-start.5) | async-done | bytes 4423712 | tf_op jit(solution)/shard_map/all_to_all | solution.py:31
  279.6 3.7 fusion.25
  283.3 0.2 copy.56
  283.5 23.5 %all_to_all.35 = bf16[16,3,64,192]{3,2,1,0:T(8,128)(2,1)S(1)} all-to-all(bf16[16,3,64,192]{3,2,1,0:T(8,128)(2,1)S(1)} %copy.56), channel_id=1, replica_groups=mesh['lat'=16,'lon'=8] {'lat'}, dimensions={0} | all-to-all | bytes 2359296 | tf_op jit(solution)/shard_map/all_to_all | solution.py:31
  307.0 0.9 reshape.279
  307.9 3.0 copy.57
  310.9 0.0 all-gather.2.cloned.1.call-update
  310.9 3.3 multiply_convert_fusion.5
  314.2 65.4 %all-gather.2.cloned.1.call-done = bf16[384,64,2,96]{3,0,2,1:T(8,128)(2,1)} async-done(((bf16[48,64,2,96]{3,0,2,1:T(8,128)(2,1)}), bf16[384,64,2,96]{3,0,2,1:T(8,128)(2,1)}) %all-gather.2.cloned.1.call-update) | async-done | bytes 9437200 | tf_op jit(solution)/shard_map/all_gather | solution.py:75
  379.6 8.7 %fusion = bf16[96,64,450]{2,0,1:T(8,128)(2,1)S(1)} fusion(bf16[384,64,2,96]{3,0,2,1:T(8,128)(2,1)} %all-gather.2.cloned.1.call-done, bf16[384,1,450]{0,2,1:T(8,128)(2,1)S(1)} %get-tuple-element.8, bf16[384,1,450]{0,2,1:T(8,128)(2,1)S(1)} %get-tuple-element.7), kind=kOutput, calls=%fused_computation.1 | convolution fusion | flops 4250880000 | bytes 15657984 | tf_op jit(solution)/shard_map/norc,nrp->cop/dot_general | solution.py:82
  388.3 6.3 %copy.58 = bf16[96,64,450]{2,1,0:T(8,128)(2,1)} copy(bf16[96,64,450]{2,0,1:T(8,128)(2,1)S(1)} %fusion) | data formatting | bytes 11059200 | tf_op jit(solution)/shard_map/convert_element_type | solution.py:83
  (5 shorter events, 0.1 us)
Async XLA Ops:
  9.9 33.9 %all-to-all-start = ((bf16[8,6,180,96]{3,2,1,0:T(8,128)(2,1)}), bf16[8,6,180,96]{3,2,1,0:T(8,128)(2,1)S(1)}, u32[]{:S(2)}, u32[]{:S(2)}) async-start(bf16[8,6,180,96]{3,2,1,0:T(8,128)(2,1)} %bitcast.54), calls=%async_computation | async-start | bytes 4521984 | tf_op jit(solution)/shard_map/all_to_all | solution.py:31
  43.8 1.4 copy-start
  52.9 11.1 %copy-start.2 = (bf16[6,1440,96]{1,2,0:T(8,128)(2,1)S(1)}, bf16[6,1440,96]{1,2,0:T(8,128)(2,1)}, u32[]{:S(2)}) copy-start(bf16[6,1440,96]{1,2,0:T(8,128)(2,1)} %reshape.269) | copy-start | bytes 4976644
  77.1 33.9 %all-to-all-start.1 = ((bf16[128,3,6,192]{3,1,2,0:T(4,128)(2,1)}), bf16[128,3,6,192]{3,1,2,0:T(4,128)(2,1)S(1)}, u32[]{:S(2)}, u32[]{:S(2)}) async-start(bf16[128,3,6,192]{3,1,2,0:T(4,128)(2,1)} %copy.43), calls=%async_computation.1 | async-start | bytes 3145728 | tf_op jit(solution)/shard_map/all_to_all | solution.py:31
  111.0 50.3 %all-to-all-start.2 = ((bf16[16,3,45,720]{3,2,1,0:T(8,128)(2,1)}), bf16[16,3,45,720]{3,2,1,0:T(8,128)(2,1)}, u32[]{:S(2)}, u32[]{:S(2)}) async-start(bf16[16,3,45,720]{3,2,1,0:T(8,128)(2,1)} %bitcast.12), calls=%async_computation.2 | async-start | bytes 7077888 | tf_op jit(solution)/shard_map/all_to_all | solution.py:31
  164.4 12.8 %copy-start.1 = (bf16[45,96,192]{2,1,0:T(8,128)(2,1)S(1)}, bf16[45,96,192]{2,1,0:T(8,128)(2,1)}, u32[]{:S(2)}) copy-start(bf16[45,96,192]{2,1,0:T(8,128)(2,1)} %param.6) | copy-start | bytes 4976644
  165.5 27.9 %all-to-all-start.3 = ((bf16[16,3,45,192]{3,2,1,0:T(8,128)(2,1)}), bf16[16,3,45,192]{3,2,1,0:T(8,128)(2,1)S(1)}, u32[]{:S(2)}, u32[]{:S(2)}) async-start(bf16[16,3,45,192]{3,2,1,0:T(8,128)(2,1)} %copy.50), calls=%async_computation.3 | async-start | bytes 2359296 | tf_op jit(solution)/shard_map/all_to_all | solution.py:31
  197.8 20.2 %all-to-all-start.4 = ((bf16[16,3,45,192]{3,2,1,0:T(8,128)(2,1)}), bf16[16,3,45,192]{3,2,1,0:T(8,128)(2,1)S(1)}, u32[]{:S(2)}, u32[]{:S(2)}) async-start(bf16[16,3,45,192]{3,2,1,0:T(8,128)(2,1)} %bitcast.16), calls=%async_computation.4 | async-start | bytes 2359296 | tf_op jit(solution)/shard_map/all_to_all | solution.py:31
  218.0 61.6 %all-to-all-start.5 = ((bf16[16,3,64,720]{3,2,1,0:T(8,128)(2,1)}), bf16[16,3,64,720]{3,2,1,0:T(8,128)(2,1)}, u32[]{:S(2)}, u32[]{:S(2)}) async-start(bf16[16,3,64,720]{3,2,1,0:T(8,128)(2,1)} %bitcast.52), calls=%async_computation.5 | async-start | bytes 9437184 | tf_op jit(solution)/shard_map/all_to_all | solution.py:31
  223.2 156.4 %all-gather.2.cloned.1.call-start = ((), (), s32[]{:S(2)}) async-start(), calls=%async_computation.7 | async-start | bytes 14155776 | tf_op jit(solution)/shard_map/all_gather | solution.py:75
Sparse Core Ops, SparseCore 0:
  311.0 68.5 all-gather.1

commit v2 on v1

v2 whole, which is shorter than its diff:
```python
import math

import jax
import jax.numpy as jnp
from jax import lax
from jax.experimental import pallas as pl
from jax.experimental.pallas import tpu as pltpu
from jax.sharding import PartitionSpec as P

CHAN = 96
KEPT_ORDERS = 368
LON_IN = 1440
LON_OUT = 3600
LATS = 16
LONS = 8
OWN = 46
SLOTS = 48
EACH = 3
ROWS = 45
QPAD = 48
PAIRS = 23
OUT_ROWS = 64
OUT_COLS = 450
WIDE = 512
LANES = 128
STEP = 16
VMEM = 56 * 1024 * 1024
QEACH = 6
BF = jnp.bfloat16


def waves(order_ids, valid, points, modulus, factor):
    phases = order_ids * points % modulus
    angles = 2.0 * math.pi / modulus * phases.astype(jnp.float32)
    scale = jnp.where(valid, factor, 0.0)
    return (jnp.cos(angles) * scale).astype(BF), (-jnp.sin(angles) * scale).astype(BF)


def swap(x, axis):
    return lax.all_to_all(x, axis, split_axis=0, concat_axis=0, tiled=True)


def synthesis_kernel(table, mixed, rows):
    m = mixed[:, 0].reshape(LATS * QPAD, 4 * CHAN)
    t = table[:, 0].reshape(2 * OUT_ROWS, LATS * QPAD)
    both = jnp.dot(t, m, preferred_element_type=jnp.float32)
    lane = lax.broadcasted_iota(jnp.int32, (OUT_ROWS, 4 * CHAN), 1)
    rows[0] = jnp.where(lane < 2 * CHAN, both[:OUT_ROWS], both[OUT_ROWS:]).astype(BF)


def synthesise(table, mixed):
    return pl.pallas_call(
        synthesis_kernel,
        grid=(PAIRS,),
        in_specs=[
            pl.BlockSpec((2, 1, OUT_ROWS, LATS * QPAD), lambda p: (0, p, 0, 0)),
            pl.BlockSpec((LATS, 1, QPAD, 4 * CHAN), lambda p: (0, p, 0, 0)),
        ],
        out_specs=pl.BlockSpec((1, OUT_ROWS, 4 * CHAN), lambda p: (p, 0, 0)),
        out_shape=jax.ShapeDtypeStruct((PAIRS, OUT_ROWS, 4 * CHAN), BF),
        compiler_params=pltpu.CompilerParams(vmem_limit_bytes=VMEM),
    )(table, mixed)


def output_kernel(rows, table, out, wide, turned, total):
    count = LONS * PAIRS
    for k in range(3):
        some = rows[:, :, k * LANES : (k + 1) * LANES].astype(jnp.float32)
        wide[k] = some.reshape(count * STEP, LANES)
    for o in range(STEP):
        one = [wide[k, pl.ds(o, count, stride=STEP), :].T for k in range(3)]
        one = jnp.concatenate(one, axis=0).astype(BF)
        for part in range(4):
            turned[part, o * CHAN : (o + 1) * CHAN, :] = one[part * CHAN : (part + 1) * CHAN]
    acc = jnp.dot(turned[0], table[0], preferred_element_type=jnp.float32)
    for part in range(1, 4):
        acc += jnp.dot(turned[part], table[part], preferred_element_type=jnp.float32)
    for k in range(4):
        total[k] = acc[:, k * LANES : (k + 1) * LANES]
    for c in range(CHAN):
        one = [total[k, pl.ds(c, STEP, stride=CHAN), :] for k in range(4)]
        out[c] = jnp.concatenate(one, axis=1)[:, :OUT_COLS].astype(BF)


def to_longitudes(rows, table):
    count = LONS * PAIRS
    return pl.pallas_call(
        output_kernel,
        grid=(OUT_ROWS // STEP,),
        in_specs=[
            pl.BlockSpec((count, STEP, 4 * CHAN), lambda s: (0, s, 0)),
            pl.BlockSpec((4, count, WIDE), lambda s: (0, 0, 0)),
        ],
        out_specs=pl.BlockSpec((CHAN, STEP, OUT_COLS), lambda s: (0, s, 0)),
        out_shape=jax.ShapeDtypeStruct((CHAN, OUT_ROWS, OUT_COLS), BF),
        scratch_shapes=[
            pltpu.VMEM((3, count * STEP, LANES), jnp.float32),
            pltpu.VMEM((4, STEP * CHAN, count), BF),
            pltpu.VMEM((4, STEP * CHAN, LANES), jnp.float32),
        ],
        compiler_params=pltpu.CompilerParams(vmem_limit_bytes=VMEM),
    )(rows, table)


def pick(x, index):
    return lax.dynamic_index_in_dim(x, index, 0, keepdims=False)


def local(coarse_field, forward_table, degree_mixing_weight, synthesis_weight_table):
    ftab = jnp.pad(forward_table, ((0, SLOTS - OWN), (0, 0), (0, 0)))
    ftab = swap(ftab.reshape(LATS, EACH, ROWS, 720), "lat")
    wtab = jnp.transpose(synthesis_weight_table, (0, 2, 1))
    place = jnp.arange(LATS * QPAD, dtype=jnp.int32)
    home = jnp.where(place % QPAD < ROWS, place // QPAD * ROWS + place % QPAD, -1)
    spread = (jnp.arange(720, dtype=jnp.int32)[:, None] == home[None, :]).astype(BF)
    wtab = jnp.einsum("mol,lk->mok", wtab, spread, preferred_element_type=jnp.float32)
    wtab = wtab.astype(BF).reshape(2, PAIRS, OUT_ROWS, LATS * QPAD)

    field = jnp.pad(jnp.transpose(coarse_field, (1, 2, 0)), ((0, QPAD - ROWS), (0, 0), (0, 0)))
    field = field.reshape(LONS, QEACH, 180, CHAN)
    lon = lax.axis_index("lon")
    x, core = lon // 2, lon % 2
    pieces, held = [], []
    for dx, dc in ((2, 0), (2, 1), (1, 0), (3, 0), (1, 1), (3, 1), (0, 1), (0, 0)):
        part = pick(field, (x + dx) % 4 * 2 + (core + dc) % 2)
        if dx or dc:
            pairs = [(i, (i // 2 + dx) % 4 * 2 + (i + dc) % 2) for i in range(LONS)]
            part = lax.ppermute(part, "lon", pairs)
        pieces.append(part)
        held.append((x + 4 - dx) % 4 * 2 + (core + dc) % 2)

    a = jnp.arange(LATS * LONS * EACH, dtype=jnp.int32)
    slot = (a // (LONS * EACH)) * EACH + a % EACH
    column = (a // EACH) % LONS
    valid = (slot < OWN)[:, None]
    ids = (column * OWN + jnp.minimum(slot, OWN - 1))[:, None]
    points = jnp.stack(held)[:, None] * 180 + jnp.arange(180, dtype=jnp.int32)[None, :]
    points = points.reshape(1, LON_IN)
    cos_in, sin_in = lax.optimization_barrier(waves(ids, valid, points, LON_IN, LON_IN ** (-0.5)))
    field = jnp.concatenate(pieces, axis=1)
    parts = [
        jnp.einsum("np,qpc->nqc", t, field, preferred_element_type=jnp.float32).astype(BF)
        for t in (cos_in, sin_in)
    ]
    spectrum = jnp.concatenate(parts, axis=-1)
    spectrum = spectrum.reshape(LATS * LONS, EACH, QEACH, 2 * CHAN)
    spectrum, ftab = lax.optimization_barrier((spectrum, ftab))
    spectrum = swap(spectrum, ("lat", "lon")).reshape(LATS, LONS, EACH, QEACH, 2 * CHAN)
    spectrum = jnp.transpose(spectrum, (2, 0, 1, 3, 4)).reshape(EACH, LATS, QPAD, 2 * CHAN)
    spectrum = spectrum[:, :, :ROWS].reshape(EACH, 720, 2 * CHAN)

    coef = jnp.einsum("ajlq,jqn->ajln", ftab, spectrum, preferred_element_type=jnp.float32)
    coef = swap(coef.astype(BF), "lat").reshape(SLOTS, ROWS, 2 * CHAN)

    w = degree_mixing_weight
    turned = jnp.concatenate([-w[..., CHAN:], w[..., :CHAN]], axis=-1)
    both = jnp.concatenate([w, turned], axis=1)
    mixed = jnp.einsum("mlt,ltu->mlu", coef, both, preferred_element_type=jnp.float32)
    mixed = mixed.astype(BF)[:OWN].reshape(2, PAIRS, ROWS, 2 * CHAN)
    mixed = jnp.transpose(mixed, (1, 2, 0, 3)).reshape(PAIRS, ROWS, 4 * CHAN)
    mixed = jnp.pad(mixed, ((0, 0), (0, QPAD - ROWS), (0, 0)))
    mixed = lax.all_gather(mixed, "lat", axis=0)
    rows = synthesise(wtab, mixed)

    every = lax.all_gather(rows, "lon", axis=0, tiled=True)
    b = jnp.arange(LONS * PAIRS, dtype=jnp.int32)
    ids = b // PAIRS * OWN + b % PAIRS
    ids = jnp.stack([ids, ids + PAIRS])[:, :, None]
    t = jnp.arange(WIDE, dtype=jnp.int32)
    points = (lon * OUT_COLS + t)[None, None, :]
    cos_out, sin_out = waves(ids, t < OUT_COLS, points, LON_OUT, KEPT_ORDERS ** (-0.5))
    table = jnp.stack([cos_out, sin_out], axis=1).reshape(4, LONS * PAIRS, WIDE)
    table = lax.optimization_barrier(table)
    return to_longitudes(every, table)


def solution(mesh):
    in_specs = (
        P(None, "lat", "lon"),
        P("lon", "lat", None),
        P("lat", None, None),
        P("lon", None, "lat"),
    )
    out_specs = P(None, "lat", "lon")
    return jax.shard_map(local, mesh=mesh, in_specs=in_specs, out_specs=out_specs, check_vma=False)
```

time: 405 us -> 339 us (0.84)
  waiting for transfers between devices: 238 us -> 150 us
  Pallas kernels: 0 us -> 45.7 us
  matrix products: 39.3 us -> 17.6 us
  starting transfers between devices: 40.8 us -> 22.8 us
  blocking collectives: 23.5 us -> 40.5 us
  other arithmetic: 5.4 us -> 17.7 us
  local copies, waits for them, and re-layouts: 41.1 us -> 30.2 us
    all_to_all x6 -> x2, waiting for transfers between devices: 172 us -> 16.6 us  [swap(): return lax.all_to_all(x, axis, split_axis=0, concat_axis=0, tiled=True)]
    all_gather x0 -> x1, waiting for transfers between devices: none -> 84.6 us  [local(): mixed = lax.all_gather(mixed, 'lat', axis=0)]
    pallas_call x0 -> x2, Pallas kernels: none -> 45.7 us  [the longest x1 27.3 us: to_longitudes(): pl.pallas_call(output_kernel, grid=(OUT_ROWS // STEP,), in_specs=[pl.Bloc...]
    all_to_all x6 -> x2, starting transfers between devices: 40.7 us -> 12.3 us  [swap(): return lax.all_to_all(x, axis, split_axis=0, concat_axis=0, tiled=True)]
    unnamed x2, matrix products: 20.9 us -> 3.4 us
    all_gather x1, waiting for transfers between devices: 65.4 us -> 48.2 us  [local(): every = lax.all_gather(rows, 'lon', axis=0, tiled=True)]
    all_to_all x1, blocking collectives: 23.5 us -> 40.5 us  [swap(): return lax.all_to_all(x, axis, split_axis=0, concat_axis=0, tiled=True)]
    convert_element_type x0 -> x1, other arithmetic: none -> 11.2 us  [waves(): (-jnp.sin(angles) * scale).astype(BF)]
  transfers between devices with their start and end apart: 7 -> 11, of which waited for: 7 -> 5; matrix products, arithmetic and copies ran while one was open for 4% -> 14% of each run, Pallas kernels for 0% -> 0%
where the time goes in v2:
time: 339 us; the launch traced here: 338 us
  waiting for transfers between devices  150 us (44%)
  Pallas kernels  45.7 us (13%)
  blocking collectives  40.5 us (12%)
  local copies, waits for them, and re-layouts  30.2 us (9%)
  starting transfers between devices  22.8 us (7%)
  other arithmetic  17.7 us (5%)
  matrix products  17.6 us (5%)
  between operations  13.9 us (4%)
    all_gather x1, waiting for transfers between devices, local(): mixed = lax.all_gather(mixed, 'lat', axis=0)  84.6 us
    all_gather x1, waiting for transfers between devices, local(): every = lax.all_gather(rows, 'lon', axis=0, tiled=True)  48.2 us
    all_to_all x1, blocking collectives, swap(): return lax.all_to_all(x, axis, split_axis=0, concat_axis=0, tiled=True)  40.5 us
    pallas_call x1, Pallas kernels, to_longitudes(): pl.pallas_call(output_kernel, grid=(OUT_ROWS // STEP,), in_specs=[pl.Bloc...  27.3 us
    pallas_call x1, Pallas kernels, synthesise(): pl.pallas_call(synthesis_kernel, grid=(PAIRS,), in_specs=[pl.BlockSpec((2...  18.4 us
    all_to_all x2, waiting for transfers between devices, swap(): return lax.all_to_all(x, axis, split_axis=0, concat_axis=0, tiled=True)  16.6 us
    unnamed x23, local copies, waits for them, and re-layouts  15.6 us
    all_to_all x2, starting transfers between devices, swap(): return lax.all_to_all(x, axis, split_axis=0, concat_axis=0, tiled=True)  12.3 us
  transfers between devices with their start and end apart: 11, of which 5 were waited for; matrix products, arithmetic and copies ran while one was open for 14% of the time, Pallas kernels for 0%

profile of v2, /device:TPU:1, one launch (start us, length us, event | category | flops | bytes accessed | tf_op | source)
XLA Modules:
  0.0 338.2 jit_solution(17887941504958028864)
XLA Ops:
  6.5 3.0 copy.85
  9.6 2.2 pad.13.clone
  11.8 8.6 %all-to-all-start = ((bf16[16,3,45,720]{3,2,1,0:T(8,128)(2,1)}), bf16[16,3,45,720]{3,2,1,0:T(8,128)(2,1)}, u32[]{:S(2)}, u32[]{:S(2)}) async-start(bf16[16,3,45,720]{3,2,1,0:T(8,128)(2,1)} %bitcast.28), calls=%async_computation | async-start | bytes 7077888 | tf_op jit(solution)/shard_map/all_to_all | solution.py:40
  20.5 2.0 pad.12
  22.6 1.1 constant_dynamic-slice_fusion
  23.7 1.1 copy.77
  24.9 2.8 collective-permute-start
  27.7 1.1 copy.78
  28.9 1.4 collective-permute-start.1
  30.3 1.9 copy.79
  32.2 1.2 collective-permute-start.2
  33.4 1.9 copy.80
  35.3 1.5 collective-permute-start.3
  36.7 0.9 copy.81
  37.7 0.1 stack.45
  37.7 0.1 iota_add_fusion
  37.8 0.1 add.373
  37.9 0.9 copy.82
  38.8 0.9 copy.83
  39.8 3.0 collective-permute-start.5
  42.8 0.3 collective-permute-done.1
  43.1 0.2 collective-permute-start.6
  43.3 11.2 %multiply_convert_fusion = (bf16[384,1440]{0,1:T(8,128)(2,1)S(1)}, bf16[384,1440]{0,1:T(8,128)(2,1)}) fusion(f32[384]{0:T(512)S(1)} %compare_select_fusion, s32[1440]{0:T(1024)S(1)} %add.373, s32[384]{0:T(512)S(1)} %fusion.58), kind=kLoop, calls=%fused_computation.14 | loop fusion | flops 7741440 | bytes 2220672 | tf_op jit(solution)/shard_map/convert_element_type | solution.py:36
  54.5 0.2 copy.84
  54.8 0.6 copy-done.3
  55.4 0.1 copy-done.4
  55.6 0.1 copy-done.5
  55.7 3.1 concatenate.18
  58.8 2.3 fusion.67
  61.2 0.1 convert_element_type.79
  61.2 1.1 fusion.68
  62.3 0.1 convert_element_type.80
  62.4 0.1 pad_maximum_fusion
  62.5 0.6 copy.62
  63.1 0.7 reshape.297
  63.8 1.6 all-to-all-done
  65.4 0.5 copy.64
  65.9 40.5 %all_to_all.15 = bf16[128,3,6,192]{3,1,2,0:T(4,128)(2,1)S(1)} all-to-all(bf16[128,3,6,192]{3,1,2,0:T(4,128)(2,1)S(1)} %copy.64), channel_id=1, replica_groups=mesh['lat'=16,'lon'=8] {'lat','lon'}, dimensions={0} | all-to-all | bytes 1769472 | tf_op jit(solution)/shard_map/all_to_all | solution.py:40
  106.4 0.3 copy.98
  106.7 0.3 copy.66
  107.0 0.1 slice.16
  107.1 0.4 copy.67
  107.5 0.6 reshape.315
  108.1 3.1 fusion.26
  111.2 1.1 copy.70
  112.3 3.7 %all-to-all-start.2 = ((bf16[16,3,45,192]{3,2,1,0:T(8,128)(2,1)}), bf16[16,3,45,192]{3,2,1,0:T(8,128)(2,1)S(1)}, u32[]{:S(2)}, u32[]{:S(2)}) async-start(bf16[16,3,45,192]{3,2,1,0:T(8,128)(2,1)} %copy.70), calls=%async_computation.2 | async-start | bytes 2359296 | tf_op jit(solution)/shard_map/all_to_all | solution.py:40
  116.0 0.0 all-gather.6.cloned.1.call-start
  116.0 1.9 slice_negate_fusion
  117.9 15.0 %all-to-all-done.2 = bf16[16,3,45,192]{3,2,1,0:T(8,128)(2,1)S(1)} async-done(((bf16[16,3,45,192]{3,2,1,0:T(8,128)(2,1)}), bf16[16,3,45,192]{3,2,1,0:T(8,128)(2,1)S(1)}, u32[]{:S(2)}, u32[]{:S(2)}) %all-to-all-start.2) | async-done | bytes 829472 | tf_op jit(solution)/shard_map/all_to_all | solution.py:40
  132.9 3.0 fusion.29
  135.9 0.4 copy.72
  136.3 0.8 copy.87
  137.1 1.8 reshape.316
  139.0 1.0 pad.14.clone
  140.0 0.0 all-gather.6.cloned.1.call-update
  140.0 0.3 all-gather.4.cloned.1.call-start
  140.3 8.1 %fusion.10 = bf16[768,46,64]{0,2,1:T(8,128)(2,1)} fusion(bf16[46,720,64]{1,2,0:T(8,128)(2,1)} %param.7, s32[768]{0:T(1024)S(1)} %fusion.51), kind=kOutput, calls=%fused_computation.11 | convolution fusion | flops 3258642432 | bytes 8764416 | tf_op jit(solution)/shard_map/mol,lk->mok/dot_general | solution.py:116
  148.4 84.6 %all-gather.6.cloned.1.call-done = bf16[368,48,384]{2,1,0:T(8,128)(2,1)} async-done(((bf16[23,48,384]{2,1,0:T(8,128)(2,1)}), bf16[368,48,384]{2,1,0:T(8,128)(2,1)}) %all-gather.6.cloned.1.call-update) | async-done | bytes 13565968 | tf_op jit(solution)/shard_map/all_gather | solution.py:162
  233.0 18.4 %shard_map.46 = bf16[23,64,384]{2,1,0:T(8,128)(2,1)} custom-call(bf16[2,23,64,768]{3,2,1,0:T(8,128)(2,1)} %bitcast.64, bf16[16,23,48,384]{3,2,1,0:T(8,128)(2,1)} %bitcast.61), custom_call_target="tpu_custom_call" | custom-call | tf_op jit(solution)/shard_map/pallas_call | solution.py:52
  251.4 0.0 all-gather.4.cloned.1.call-update
  251.4 3.4 multiply_convert_fusion.3
  254.8 0.9 pad_maximum_fusion.1
  255.8 48.2 %all-gather.4.cloned.1.call-done.rows = bf16[184,64,384]{2,1,0:T(8,128)(2,1)} async-done(((bf16[23,64,384]{2,1,0:T(8,128)(2,1)}), bf16[184,64,384]{2,1,0:T(8,128)(2,1)}) %all-gather.4.cloned.1.call-update) | async-done | bytes 9043984 | tf_op jit(solution)/shard_map/all_gather | solution.py:165
  304.0 27.3 %shard_map.47 = bf16[96,64,450]{2,1,0:T(8,128)(2,1)} custom-call(bf16[184,64,384]{2,1,0:T(8,128)(2,1)} %all-gather.4.cloned.1.call-done.rows, bf16[4,184,512]{2,1,0:T(8,128)(2,1)} %bitcast.67), custom_call_target="tpu_custom_call" | custom-call | tf_op jit(solution)/shard_map/pallas_call | solution.py:87
  (24 shorter events, 0.1 us)
Async XLA Ops:
  11.8 53.6 %all-to-all-start = ((bf16[16,3,45,720]{3,2,1,0:T(8,128)(2,1)}), bf16[16,3,45,720]{3,2,1,0:T(8,128)(2,1)}, u32[]{:S(2)}, u32[]{:S(2)}) async-start(bf16[16,3,45,720]{3,2,1,0:T(8,128)(2,1)} %bitcast.28), calls=%async_computation | async-start | bytes 7077888 | tf_op jit(solution)/shard_map/all_to_all | solution.py:40
  24.9 14.9 %collective-permute-start = (bf16[6,180,96]{1,2,0:T(8,128)(2,1)S(1)}, bf16[6,180,96]{1,2,0:T(8,128)(2,1)S(1)}, u32[]{:S(2)}, u32[]{:S(2)}) collective-permute-start(bf16[6,180,96]{1,2,0:T(8,128)(2,1)S(1)} %bitcast.77), channel_id=1, source_target_pairs={{0,4},{1,5},{2,6},{3,7},{4,0},{5,1},{6,2},{7,3},{8,12},{9,13},{10,... | collective-permute-start | bytes 622088 | tf_op jit(solution)/shard_map/ppermute | solution.py:128
  28.9 14.3 %collective-permute-start.1 = (bf16[6,180,96]{1,2,0:T(8,128)(2,1)S(1)}, bf16[6,180,96]{1,2,0:T(8,128)(2,1)S(1)}, u32[]{:S(2)}, u32[]{:S(2)}) collective-permute-start(bf16[6,180,96]{1,2,0:T(8,128)(2,1)S(1)} %bitcast.76), channel_id=1, source_target_pairs={{0,5},{1,4},{2,7},{3,6},{4,1},{5,0},{6,3},{7,2},{8,13},{9,12},{10,... | collective-permute-start | bytes 622088 | tf_op jit(solution)/shard_map/ppermute | solution.py:128
  32.2 22.5 %collective-permute-start.2 = (bf16[6,180,96]{1,2,0:T(8,128)(2,1)}, bf16[6,180,96]{1,2,0:T(8,128)(2,1)S(1)}, u32[]{:S(2)}, u32[]{:S(2)}) collective-permute-start(bf16[6,180,96]{1,2,0:T(8,128)(2,1)} %bitcast.16), channel_id=1, source_target_pairs={{0,2},{1,3},{2,4},{3,5},{4,6},{5,7},{6,0},{7,1},{8,10},{9,11},{10,... | collective-permute-start | bytes 622088 | tf_op jit(solution)/shard_map/ppermute | solution.py:128
  35.3 19.5 %collective-permute-start.3 = (bf16[6,180,96]{1,2,0:T(8,128)(2,1)}, bf16[6,180,96]{1,2,0:T(8,128)(2,1)S(1)}, u32[]{:S(2)}, u32[]{:S(2)}) collective-permute-start(bf16[6,180,96]{1,2,0:T(8,128)(2,1)} %bitcast.17), channel_id=1, source_target_pairs={{0,6},{1,7},{2,0},{3,1},{4,2},{5,3},{6,4},{7,5},{8,14},{9,15},{10,... | collective-permute-start | bytes 622088 | tf_op jit(solution)/shard_map/ppermute | solution.py:128
  37.7 17.1 %collective-permute-start.4 = (bf16[6,180,96]{1,2,0:T(8,128)(2,1)}, bf16[6,180,96]{1,2,0:T(8,128)(2,1)}, u32[]{:S(2)}, u32[]{:S(2)}) collective-permute-start(bf16[6,180,96]{1,2,0:T(8,128)(2,1)} %bitcast.18), channel_id=1, source_target_pairs={{0,3},{1,2},{2,5},{3,4},{4,7},{5,6},{6,1},{7,0},{8,11},{9,10},{10,... | collective-permute-start | bytes 622088 | tf_op jit(solution)/shard_map/ppermute | solution.py:128
  39.8 15.0 %copy-start.1 = (bf16[6,180,96]{1,2,0:T(8,128)(2,1)}, bf16[6,180,96]{1,2,0:T(8,128)(2,1)S(1)}, u32[]{:S(2)}) copy-start(bf16[6,180,96]{1,2,0:T(8,128)(2,1)S(1)} %collective-permute-done) | copy-start | bytes 622084
  39.8 14.9 %collective-permute-start.5 = (bf16[6,180,96]{1,2,0:T(8,128)(2,1)}, bf16[6,180,96]{1,2,0:T(8,128)(2,1)S(1)}, u32[]{:S(2)}, u32[]{:S(2)}) collective-permute-start(bf16[6,180,96]{1,2,0:T(8,128)(2,1)} %bitcast.19), channel_id=1, source_target_pairs={{0,7},{1,6},{2,1},{3,0},{4,3},{5,2},{6,5},{7,4},{8,15},{9,14},{10,... | collective-permute-start | bytes 622088 | tf_op jit(solution)/shard_map/ppermute | solution.py:128
  43.1 11.7 %copy-start.2 = (bf16[6,180,96]{1,2,0:T(8,128)(2,1)}, bf16[6,180,96]{1,2,0:T(8,128)(2,1)S(1)}, u32[]{:S(2)}) copy-start(bf16[6,180,96]{1,2,0:T(8,128)(2,1)S(1)} %collective-permute-done.1) | copy-start | bytes 622084
  43.1 11.6 %collective-permute-start.6 = (bf16[6,180,96]{1,2,0:T(8,128)(2,1)}, bf16[6,180,96]{1,2,0:T(8,128)(2,1)}, u32[]{:S(2)}, u32[]{:S(2)}) collective-permute-start(bf16[6,180,96]{1,2,0:T(8,128)(2,1)} %bitcast.20), channel_id=1, source_target_pairs={{0,1},{1,0},{2,3},{3,2},{4,5},{5,4},{6,7},{7,6},{8,9},{9,8},{10,11... | collective-permute-start | bytes 622088 | tf_op jit(solution)/shard_map/ppermute | solution.py:128
  54.7 0.7 copy-start.3
  54.7 0.8 copy-start.4
  54.8 0.9 copy-start.5
  111.2 4.9 %copy-start = (bf16[45,96,192]{2,1,0:T(8,128)(2,1)S(1)}, bf16[45,96,192]{2,1,0:T(8,128)(2,1)}, u32[]{:S(2)}) copy-start(bf16[45,96,192]{2,1,0:T(8,128)(2,1)} %param.6) | copy-start | bytes 4976644
  112.3 20.7 %all-to-all-start.2 = ((bf16[16,3,45,192]{3,2,1,0:T(8,128)(2,1)}), bf16[16,3,45,192]{3,2,1,0:T(8,128)(2,1)S(1)}, u32[]{:S(2)}, u32[]{:S(2)}) async-start(bf16[16,3,45,192]{3,2,1,0:T(8,128)(2,1)} %copy.70), calls=%async_computation.2 | async-start | bytes 2359296 | tf_op jit(solution)/shard_map/all_to_all | solution.py:40
  116.0 117.0 %all-gather.6.cloned.1.call-start = ((), (), s32[]{:S(2)}) async-start(), calls=%async_computation.4 | async-start | bytes 14413824 | tf_op jit(solution)/shard_map/all_gather | solution.py:162
  140.0 164.0 %all-gather.4.cloned.1.call-start = ((), (), s32[]{:S(2)}) async-start(), calls=%async_computation.3 | async-start | bytes 10174464 | tf_op jit(solution)/shard_map/all_gather | solution.py:165
Sparse Core Ops, SparseCore 0:
  140.1 92.8 all-gather.5
  251.5 52.4 all-gather.3

commit v3 on v1

v3 whole, which is shorter than its diff:
```python
import math

import jax
import jax.numpy as jnp
from jax import lax
from jax.experimental import pallas as pl
from jax.experimental.pallas import tpu as pltpu
from jax.sharding import PartitionSpec as P

CHAN = 96
KEPT_ORDERS = 368
LON_IN = 1440
LON_OUT = 3600
LATS = 16
LONS = 8
OWN = 46
SLOTS = 48
EACH = 3
ROWS = 45
LINES = 2 * EACH
SPLIT = 64
HALF = 48
OUT_ROWS = 64
OUT_COLS = 450
WIDE = 464
LANES = 128
STEP = 8
VMEM = 56 * 1024 * 1024
BF = jnp.bfloat16


def waves(order_ids, turn, valid, points, modulus, factor):
    phases = (order_ids * points + turn * (modulus // 4)) % modulus
    angles = 2.0 * math.pi / modulus * phases.astype(jnp.float32)
    return (jnp.cos(angles) * jnp.where(valid, factor, 0.0)).astype(BF)


def swap(x, axis):
    return lax.all_to_all(x, axis, split_axis=0, concat_axis=0, tiled=True)


def share_kernel(waves_in, field, out):
    for q in range(0, field.shape[0], 2):
        some = [field[k] for k in range(q, min(q + 2, field.shape[0]))]
        some = jnp.concatenate([jnp.pad(v, ((0, 0), (0, LANES - CHAN))) for v in some], axis=1)
        made = jnp.dot(waves_in[...], some, preferred_element_type=jnp.float32).astype(BF)
        for k in range(some.shape[1] // LANES):
            one = made[:, k * LANES : k * LANES + CHAN].reshape(2, LONS, SLOTS, CHAN)
            for r in range(2):
                out[:, q + k, r * SLOTS : (r + 1) * SLOTS] = one[r]


def shares(waves_in, field):
    step = 9
    return pl.pallas_call(
        share_kernel,
        grid=(ROWS // step,),
        in_specs=[
            pl.BlockSpec(waves_in.shape, lambda s: (0, 0)),
            pl.BlockSpec((step, 180, CHAN), lambda s: (s, 0, 0)),
        ],
        out_specs=pl.BlockSpec((LONS, step, 2 * SLOTS, CHAN), lambda s: (0, s, 0, 0)),
        out_shape=jax.ShapeDtypeStruct((LONS, ROWS, 2 * SLOTS, CHAN), BF),
        compiler_params=pltpu.CompilerParams(vmem_limit_bytes=VMEM),
    )(waves_in, field)


def synthesis_kernel(mixed, table, rows, lines):
    made = []
    for k in range(EACH):
        t = table[:, k].reshape(LATS * OUT_ROWS, 720)
        made.append(jnp.dot(t, mixed[k], preferred_element_type=jnp.float32))
    for b in range(LATS):
        for k in range(EACH):
            one = made[k][b * OUT_ROWS : (b + 1) * OUT_ROWS].T
            for r in range(2):
                low, high = one[r * CHAN : r * CHAN + HALF], one[r * CHAN + HALF : (r + 1) * CHAN]
                side = jnp.concatenate([low, high], axis=1)
                lines[pl.ds(2 * k + r, HALF, stride=LINES), :] = side
        rows[b] = lines[...].astype(BF)


def synthesise(mixed, table):
    return pl.pallas_call(
        synthesis_kernel,
        out_shape=jax.ShapeDtypeStruct((LATS, HALF * LINES, LANES), BF),
        scratch_shapes=[pltpu.VMEM((HALF * LINES, LANES), jnp.float32)],
        compiler_params=pltpu.CompilerParams(vmem_limit_bytes=VMEM),
        cost_estimate=pl.CostEstimate(
            flops=2 * EACH * 1024 * 720 * 192, bytes_accessed=6000000, transcendentals=0
        ),
    )(mixed, table)


def joining_kernel(rows, out, rest, wide, lines):
    for a in range(LATS):
        wide[...] = rows[a].astype(jnp.float32)
        for k in range(LINES):
            one = wide[pl.ds(k, HALF, stride=LINES), :]
            lines[pl.ds(a * LINES + k, HALF, stride=LATS * LINES), :] = one
    made = lines[...].reshape(HALF, LATS * LINES, LANES).astype(BF)
    out[...] = made[:, :SPLIT]
    rest[...] = made[:, SPLIT:]


def join(rows):
    return pl.pallas_call(
        joining_kernel,
        out_shape=[
            jax.ShapeDtypeStruct((HALF, SPLIT, LANES), BF),
            jax.ShapeDtypeStruct((HALF, LATS * LINES - SPLIT, LANES), BF),
        ],
        scratch_shapes=[
            pltpu.VMEM((HALF * LINES, LANES), jnp.float32),
            pltpu.VMEM((HALF * LATS * LINES, LANES), jnp.float32),
        ],
        compiler_params=pltpu.CompilerParams(vmem_limit_bytes=VMEM),
    )(rows)


def output_kernel(table, *refs):
    out = refs[-1]

    def line(r, at):
        return r[at] if len(r.shape) == 3 else r[:, at].reshape(-1, LANES)

    for i in range(0, STEP, 2):
        both = [jnp.concatenate([line(r, i + k) for r in refs[:-1]], axis=0) for k in range(2)]
        both = jnp.concatenate(both, axis=1)
        made = jnp.dot(table[...], both, preferred_element_type=jnp.float32)
        made = made.astype(BF).T[:, :OUT_COLS]
        for k in range(2):
            for half in range(2):
                at = (2 * k + half) * OUT_ROWS
                out[half, i + k] = made[at : at + OUT_ROWS]


def to_longitudes(table, pieces):
    def spec(v):
        if v.ndim == 4:
            return pl.BlockSpec((v.shape[0], STEP, v.shape[2], LANES), lambda s: (0, s, 0, 0))
        return pl.BlockSpec((STEP, v.shape[1], LANES), lambda s: (s, 0, 0))

    out = pl.pallas_call(
        output_kernel,
        grid=(HALF // STEP,),
        in_specs=[pl.BlockSpec(table.shape, lambda s: (0, 0))] + [spec(v) for v in pieces],
        out_specs=pl.BlockSpec((2, STEP, OUT_ROWS, OUT_COLS), lambda s: (0, s, 0, 0)),
        out_shape=jax.ShapeDtypeStruct((2, HALF, OUT_ROWS, OUT_COLS), BF),
        compiler_params=pltpu.CompilerParams(vmem_limit_bytes=VMEM),
    )(table, *pieces)
    return out.reshape(CHAN, OUT_ROWS, OUT_COLS)


def lon_order():
    lon = lax.axis_index("lon")
    columns = [lon, (lon + 6) % 8, (lon + 2) % 8, (lon + 4) % 8]
    return columns + [c ^ 1 for c in columns]


def gather_lon(v):
    def along(u, d):
        return lax.ppermute(u, "lon", [(i, (i + 2 * d) % 8) for i in range(8)])

    def across(u):
        return lax.ppermute(u, "lon", [(i, i ^ 1) for i in range(8)])

    pieces = [v, along(v, 1), along(v, -1), along(v, 2)]
    return pieces + [across(u) for u in pieces]


def local(coarse_field, forward_table, degree_mixing_weight, synthesis_weight_table):
    ftab = jnp.pad(forward_table, ((0, SLOTS - OWN), (0, 0), (0, 0)))
    ftab = ftab.reshape(LATS, EACH, ROWS, 720)
    ftab, coarse_field = lax.optimization_barrier((ftab, coarse_field))
    ftab = swap(ftab, "lat")

    lon = lax.axis_index("lon")
    row = jnp.arange(2 * LONS * SLOTS, dtype=jnp.int32)[:, None]
    slot = row % SLOTS
    ids = row // SLOTS % LONS * OWN + jnp.minimum(slot, OWN - 1)
    points = (lon * 180 + jnp.arange(180, dtype=jnp.int32))[None, :]
    factor = LON_IN ** (-0.5)
    waves_in = waves(ids, row // (SLOTS * LONS), slot < OWN, points, LON_IN, factor)
    spectrum = shares(waves_in, jnp.transpose(coarse_field, (1, 2, 0)))

    wtab = jnp.transpose(synthesis_weight_table, (0, 2, 1))
    wtab = jnp.pad(wtab, ((0, SLOTS - OWN), (0, 0), (0, 0))).reshape(LATS, EACH, OUT_ROWS, 720)
    spectrum, ftab, wtab, lon = lax.optimization_barrier((spectrum, ftab, wtab, lon))
    spectrum = lax.psum_scatter(spectrum, "lon", scatter_dimension=0)
    wtab = swap(wtab, "lat")
    spectrum, wtab, lon = lax.optimization_barrier((spectrum, wtab, lon))
    spectrum = spectrum.reshape(ROWS, 2, LATS, EACH, CHAN)
    spectrum = jnp.transpose(spectrum, (2, 3, 0, 1, 4)).reshape(LATS, EACH, ROWS, 2 * CHAN)
    spectrum = swap(spectrum, "lat")
    spectrum = jnp.transpose(spectrum, (1, 0, 2, 3)).reshape(EACH, 720, 2 * CHAN)

    coef = jnp.einsum("ajlq,jqn->ajln", ftab, spectrum, preferred_element_type=jnp.float32)
    coef = swap(coef.astype(BF), "lat").reshape(SLOTS, ROWS, 2 * CHAN)

    ids, turns, real = [], [], []
    orders = [(column, 0, SPLIT) for column in range(LONS)]
    orders += [(column, SPLIT, 2 * SLOTS) for column in lon_order()]
    for column, first, last in orders:
        line = jnp.arange(first, last, dtype=jnp.int32)
        ids.append(column * OWN + jnp.minimum(line // 2, OWN - 1))
        turns.append(line % 2)
        real.append(line // 2 < OWN)
    ids, turns, real = (jnp.concatenate(v)[None, :] for v in (ids, turns, real))
    points = (lon * OUT_COLS + jnp.arange(WIDE, dtype=jnp.int32))[:, None]
    table = waves(ids, turns, real, points, LON_OUT, KEPT_ORDERS ** (-0.5))
    coef, table = lax.optimization_barrier((coef, table))

    w = degree_mixing_weight
    turned = jnp.concatenate([-w[..., CHAN:], w[..., :CHAN]], axis=-1)
    both = jnp.concatenate([w, turned], axis=1)
    mixed = jnp.einsum("mlt,ltu->mlu", coef, both, preferred_element_type=jnp.float32)
    mixed = swap(mixed.astype(BF).reshape(LATS, EACH, ROWS, 2 * CHAN), "lat")
    mixed = jnp.transpose(mixed, (1, 0, 2, 3)).reshape(EACH, 720, 2 * CHAN)
    rows, rest = join(swap(synthesise(mixed, wtab), "lat"))
    pieces = [lax.all_gather(rows, "lon", axis=0)] + gather_lon(rest)

    return to_longitudes(table, pieces)


def solution(mesh):
    in_specs = (
        P(None, "lat", "lon"),
        P("lon", "lat", None),
        P("lat", None, None),
        P("lon", None, "lat"),
    )
    out_specs = P(None, "lat", "lon")
    return jax.shard_map(local, mesh=mesh, in_specs=in_specs, out_specs=out_specs, check_vma=False)
```

time: 405 us -> 301 us (0.74)
  waiting for transfers between devices: 238 us -> 125 us
  matrix products: 39.3 us -> 6.06 us
  Pallas kernels: 0 us -> 28.7 us
  local copies, waits for them, and re-layouts: 41.1 us -> 20.6 us
  starting transfers between devices: 40.8 us -> 60.8 us
  blocking collectives: 23.5 us -> 32.3 us
  other arithmetic: 5.4 us -> 12.8 us
    all_to_all x6 -> x4, waiting for transfers between devices: 172 us -> 102 us  [swap(): return lax.all_to_all(x, axis, split_axis=0, concat_axis=0, tiled=True)]
    all_gather x1, waiting for transfers between devices: 65.4 us -> 21 us  [local(): pieces = [lax.all_gather(rows, 'lon', axis=0)] + gather_lon(rest)]
    pallas_call x0 -> x4, Pallas kernels: none -> 28.7 us  [the longest x1 10.3 us: to_longitudes(): pl.pallas_call(output_kernel, grid=(HALF // STEP,), in_specs=[pl.BlockSpe...]
    ppermute x0 -> x7, starting transfers between devices: none -> 28 us  [the longest x4 23.8 us: across(): return lax.ppermute(u, 'lon', [(i, i ^ 1) for i in range(8)])]
    unnamed x2 -> x0, matrix products: 20.9 us -> none
    dot_general x2 -> x0, matrix products: 12.4 us -> none  [the longest x1 8.65 us: local(): jnp.einsum('norc,nrp->cop', every, table, preferred_element_type=jnp.floa...]
    all_to_all x1 -> x2, blocking collectives: 23.5 us -> 32.3 us  [swap(): return lax.all_to_all(x, axis, split_axis=0, concat_axis=0, tiled=True)]
    all_to_all x6 -> x4, starting transfers between devices: 40.7 us -> 32.5 us  [swap(): return lax.all_to_all(x, axis, split_axis=0, concat_axis=0, tiled=True)]
  transfers between devices with their start and end apart: 7 -> 13, of which waited for: 7 -> 6; matrix products, arithmetic and copies ran while one was open for 4% -> 6% of each run, Pallas kernels for 0% -> 2%
where the time goes in v3:
time: 301 us; the launch traced here: 300 us
  waiting for transfers between devices  125 us (42%)
  starting transfers between devices  60.8 us (20%)
  blocking collectives  32.3 us (11%)
  Pallas kernels  28.7 us (10%)
  local copies, waits for them, and re-layouts  20.6 us (7%)
  between operations  13.7 us (5%)
  other arithmetic  12.8 us (4%)
  matrix products  6.06 us (2%)
    all_to_all x4, waiting for transfers between devices, swap(): return lax.all_to_all(x, axis, split_axis=0, concat_axis=0, tiled=True)  102 us
    all_to_all x4, starting transfers between devices, swap(): return lax.all_to_all(x, axis, split_axis=0, concat_axis=0, tiled=True)  32.5 us
    all_to_all x2, blocking collectives, swap(): return lax.all_to_all(x, axis, split_axis=0, concat_axis=0, tiled=True)  32.3 us
    ppermute x4, starting transfers between devices, across(): return lax.ppermute(u, 'lon', [(i, i ^ 1) for i in range(8)])  23.8 us
    all_gather x1, waiting for transfers between devices, local(): pieces = [lax.all_gather(rows, 'lon', axis=0)] + gather_lon(rest)  21 us
    convert_element_type x2, other arithmetic, waves(): return (jnp.cos(angles) * jnp.where(valid, factor, 0.0)).astype(BF)  10.8 us
    pallas_call x1, Pallas kernels, to_longitudes(): pl.pallas_call(output_kernel, grid=(HALF // STEP,), in_specs=[pl.BlockSpe...  10.3 us
    pallas_call x1, Pallas kernels, shares(): pl.pallas_call(share_kernel, grid=(ROWS // step,), in_specs=[pl.BlockSpec...  7.04 us
  transfers between devices with their start and end apart: 13, of which 6 were waited for; matrix products, arithmetic and copies ran while one was open for 6% of the time, Pallas kernels for 2%

profile of v3, /device:TPU:1, one launch (start us, length us, event | category | flops | bytes accessed | tf_op | source)
XLA Modules:
  0.0 299.9 jit_solution(13612836412735215576)
XLA Ops:
  6.5 3.0 %copy.32 = bf16[46,45,720]{2,1,0:T(8,128)(2,1)S(1)} copy(bf16[46,45,720]{2,0,1:T(8,128)(2,1)} %param.5) | data formatting | bytes 5961600
  9.6 2.2 pad.8.clone
  11.7 8.6 %all-to-all-start = ((bf16[16,3,45,720]{3,2,1,0:T(8,128)(2,1)}), bf16[16,3,45,720]{3,2,1,0:T(8,128)(2,1)S(1)}, u32[]{:S(2)}, u32[]{:S(2)}) async-start(bf16[16,3,45,720]{3,2,1,0:T(8,128)(2,1)} %bitcast), calls=%async_computation | async-start | bytes 7077888 | tf_op jit(solution)/shard_map/all_to_all | solution.py:39
  20.4 0.0 reduce-scatter.2.cloned.1.call-start
  20.4 5.3 %pad.9 = bf16[48,64,720]{2,1,0:T(8,128)(2,1)} pad(bf16[46,64,720]{2,1,0:T(8,128)(2,1)} %bitcast.25, bf16[]{:T(256)} %constant.255.clone.1), padding=0_2x0_0x0_0 | pad | bytes 8663042 | tf_op jit(solution)/shard_map/jit(_pad)/pad | solution.py:188
  25.7 4.5 %fusion.33.waves_in = bf16[768,180]{1,0:T(8,128)(2,1)} fusion(f32[768]{0:T(1024)S(1)} %fusion.52, s32[768]{0:T(1024)S(1)} %get-tuple-element.33, s32[180]{0:T(256)S(1)} %iota_add_fusion.1, s32[768]{0:T(1024)S(1)} %get-tuple-element.34), kind=kLoop, calls=%fused_computation.29 | loop fusion | flops 1658880 | bytes 286416 | tf_op jit(solution)/shard_map/convert_element_type | solution.py:35
  30.2 7.0 %shard_map.46 = bf16[8,45,96,96]{3,2,1,0:T(8,128)(2,1)} custom-call(bf16[768,180]{1,0:T(8,128)(2,1)} %fusion.33.waves_in, bf16[45,180,96]{2,1,0:T(8,128)(2,1)} %bitcast.26), custom_call_target="tpu_custom_call" | custom-call | tf_op jit(solution)/shard_map/pallas_call | solution.py:55
  37.2 28.2 %all-to-all-done = bf16[16,3,45,720]{3,2,1,0:T(8,128)(2,1)S(1)} async-done(((bf16[16,3,45,720]{3,2,1,0:T(8,128)(2,1)}), bf16[16,3,45,720]{3,2,1,0:T(8,128)(2,1)S(1)}, u32[]{:S(2)}, u32[]{:S(2)}) %all-to-all-start) | async-done | bytes 3110432 | tf_op jit(solution)/shard_map/all_to_all | solution.py:39
  65.4 0.0 reduce-scatter.2.cloned.1.call-update
  65.4 1.7 copy-done
  67.1 11.6 %all-to-all-start.1 = ((bf16[16,3,64,720]{3,2,1,0:T(8,128)(2,1)}), bf16[16,3,64,720]{3,2,1,0:T(8,128)(2,1)}, u32[]{:S(2)}, u32[]{:S(2)}) async-start(bf16[16,3,64,720]{3,2,1,0:T(8,128)(2,1)} %bitcast.19), calls=%async_computation.2 | async-start | bytes 9437184 | tf_op jit(solution)/shard_map/all_to_all | solution.py:39
  78.8 0.1 concatenate.25
  78.9 0.1 concatenate.24
  79.1 57.2 %all-to-all-done.1.table = bf16[16,3,64,720]{3,2,1,0:T(8,128)(2,1)} async-done(((bf16[16,3,64,720]{3,2,1,0:T(8,128)(2,1)}), bf16[16,3,64,720]{3,2,1,0:T(8,128)(2,1)}, u32[]{:S(2)}, u32[]{:S(2)}) %all-to-all-start.1) | async-done | bytes 4423712 | tf_op jit(solution)/shard_map/all_to_all | solution.py:39
  136.3 1.7 copy.18
  137.9 1.2 copy.29
  139.1 1.7 reshape.297
  140.8 8.0 %all-to-all-start.2 = ((bf16[16,3,45,192]{3,2,1,0:T(8,128)(2,1)}), bf16[16,3,45,192]{3,2,1,0:T(8,128)(2,1)S(1)}, u32[]{:S(2)}, u32[]{:S(2)}) async-start(bf16[16,3,45,192]{3,2,1,0:T(8,128)(2,1)} %reshape.297), calls=%async_computation.3 | async-start | bytes 2359296 | tf_op jit(solution)/shard_map/all_to_all | solution.py:39
  148.9 0.1 concatenate.23
  149.0 12.9 %all-to-all-done.2 = bf16[16,3,45,192]{3,2,1,0:T(8,128)(2,1)S(1)} async-done(((bf16[16,3,45,192]{3,2,1,0:T(8,128)(2,1)}), bf16[16,3,45,192]{3,2,1,0:T(8,128)(2,1)S(1)}, u32[]{:S(2)}, u32[]{:S(2)}) %all-to-all-start.2) | async-done | bytes 829472 | tf_op jit(solution)/shard_map/all_to_all | solution.py:39
  161.9 0.1 copy.21
  162.0 0.6 reshape.300
  162.6 3.1 %fusion.22 = bf16[16,3,45,192]{3,2,0,1:T(8,128)(2,1)S(1)} fusion(bf16[3,720,192,1]{2,1,3,0:T(8,128)(2,1)S(1)} %reshape.300, bf16[16,3,45,720]{3,2,1,0:T(8,128)(2,1)} %copy-done), kind=kOutput, calls=%fused_computation.20 | convolution fusion | flops 597611520 | bytes 4769280 | tf_op jit(solution)/shard_map/ajlq,jqn->ajln/dot_general | solution.py:198
  165.7 1.1 copy.24
  166.7 4.3 %all-to-all-start.3 = ((bf16[16,3,45,192]{3,2,1,0:T(8,128)(2,1)}), bf16[16,3,45,192]{3,2,1,0:T(8,128)(2,1)S(1)}, u32[]{:S(2)}, u32[]{:S(2)}) async-start(bf16[16,3,45,192]{3,2,1,0:T(8,128)(2,1)} %copy.24), calls=%async_computation.4 | async-start | bytes 2359296 | tf_op jit(solution)/shard_map/all_to_all | solution.py:39
  171.1 0.2 all-gather.3.cloned.1.call-start
  171.3 0.0 copy-done.1
  171.3 1.9 slice_negate_fusion
  173.2 6.4 %fusion.18.table = bf16[464,768]{1,0:T(8,128)(2,1)} fusion(f32[768]{0:T(1024)S(1)} %broadcast_select_fusion, s32[768]{0:T(1024)S(1)} %broadcast_multiply_fusion, s32[464]{0:T(512)S(1)} %iota_add_fusion, s32[768]{0:T(1024)S(1)} %concatenate.23), kind=kLoop, calls=%fused_computation.15 | loop fusion | flops 4276224 | bytes 723776 | tf_op jit(solution)/shard_map/convert_element_type | solution.py:35
  179.6 4.1 %all-to-all-done.3 = bf16[16,3,45,192]{3,2,1,0:T(8,128)(2,1)S(1)} async-done(((bf16[16,3,45,192]{3,2,1,0:T(8,128)(2,1)}), bf16[16,3,45,192]{3,2,1,0:T(8,128)(2,1)S(1)}, u32[]{:S(2)}, u32[]{:S(2)}) %all-to-all-start.3) | async-done | bytes 829472 | tf_op jit(solution)/shard_map/all_to_all | solution.py:39
  183.6 3.0 fusion.25
  186.6 0.4 copy.26
  187.0 15.6 %all_to_all.30 = bf16[16,3,45,192]{3,2,1,0:T(8,128)(2,1)S(1)} all-to-all(bf16[16,3,45,192]{3,2,1,0:T(8,128)(2,1)S(1)} %bitcast.23), channel_id=1, replica_groups=mesh['lat'=16,'lon'=8] {'lat'}, dimensions={0} | all-to-all | bytes 1658880 | tf_op jit(solution)/shard_map/all_to_all | solution.py:39
  202.6 0.1 copy.27
  202.7 1.4 reshape.293.mixed
  204.1 6.7 %shard_map.47 = bf16[16,288,128]{2,1,0:T(8,128)(2,1)} custom-call(bf16[3,720,192]{2,1,0:T(8,128)(2,1)} %reshape.293.mixed, bf16[16,3,64,720]{3,2,1,0:T(8,128)(2,1)} %all-to-all-done.1.table), custom_call_target="tpu_custom_call" | custom-call | flops 849346560 | bytes 6000000 | tf_op jit(solution)/shard_map/pallas_call | solution.py:84
  210.7 16.7 %all_to_all.31.rows = bf16[16,288,128]{2,1,0:T(8,128)(2,1)} all-to-all(bf16[16,288,128]{2,1,0:T(8,128)(2,1)} %shard_map.47), channel_id=1, replica_groups=mesh['lat'=16,'lon'=8] {'lat'}, dimensions={0} | all-to-all | bytes 2359296 | tf_op jit(solution)/shard_map/all_to_all | solution.py:39
  227.4 4.8 %shard_map.48 = (bf16[48,64,128]{2,1,0:T(8,128)(2,1)}, bf16[48,32,128]{2,1,0:T(8,128)(2,1)}) custom-call(bf16[16,288,128]{2,1,0:T(8,128)(2,1)} %all_to_all.31.rows), custom_call_target="tpu_custom_call" | custom-call | tf_op jit(solution)/shard_map/pallas_call | solution.py:107
  232.2 0.0 all-gather.3.cloned.1.call-update
  232.2 1.3 collective-permute-start
  233.5 1.5 collective-permute-start.1
  234.9 1.5 collective-permute-start.2
  236.5 10.1 %collective-permute-start.3 = (bf16[48,32,128]{2,1,0:T(8,128)(2,1)}, bf16[48,32,128]{2,1,0:T(8,128)(2,1)S(1)}, u32[]{:S(2)}, u32[]{:S(2)}) collective-permute-start(bf16[48,32,128]{2,1,0:T(8,128)(2,1)} %get-tuple-element.30.refs_1_), channel_id=1, source_target_pairs={{0,1},{1,0},{2,3},{3,2},{4,5},{5,4},{6,7},{7,6},{8,9},{9,8},{10,11... | collective-permute-start | bytes 1179656 | tf_op jit(solution)/shard_map/ppermute | solution.py:166
  246.6 0.0 collective-permute-done.refs_2_
  246.6 4.1 %collective-permute-start.4 = (bf16[48,32,128]{2,1,0:T(8,128)(2,1)S(1)}, bf16[48,32,128]{2,1,0:T(8,128)(2,1)S(1)}, u32[]{:S(2)}, u32[]{:S(2)}) collective-permute-start(bf16[48,32,128]{2,1,0:T(8,128)(2,1)S(1)} %collective-permute-done.refs_2_), channel_id=1, source_target_pairs={{0,1},{1,0},{2,3},{3,2},{4,5},{5,4},{6,7},{7,6},{8,9},{9,8},{10,11... | collective-permute-start | bytes 1179656 | tf_op jit(solution)/shard_map/ppermute | solution.py:166
  250.8 0.0 collective-permute-done.1.refs_3_
  250.8 1.4 collective-permute-start.5
  252.2 0.0 collective-permute-done.2.refs_4_
  252.2 8.1 %collective-permute-start.6 = (bf16[48,32,128]{2,1,0:T(8,128)(2,1)S(1)}, bf16[48,32,128]{2,1,0:T(8,128)(2,1)S(1)}, u32[]{:S(2)}, u32[]{:S(2)}) collective-permute-start(bf16[48,32,128]{2,1,0:T(8,128)(2,1)S(1)} %collective-permute-done.2.refs_4_), channel_id=1, source_target_pairs={{0,1},{1,0},{2,3},{3,2},{4,5},{5,4},{6,7},{7,6},{8,9},{9,8},{10,11... | collective-permute-start | bytes 1179656 | tf_op jit(solution)/shard_map/ppermute | solution.py:166
  260.3 0.0 collective-permute-done.3.refs_5_
  260.3 0.0 collective-permute-done.4.refs_6_
  260.3 0.0 copy-start.6
  260.3 0.0 collective-permute-done.5.refs_7_
  260.3 0.0 copy-start.7
  260.3 1.4 collective-permute-done.6.refs_8_
  261.7 21.0 %all-gather.3.cloned.1.call-done = bf16[384,64,128]{2,1,0:T(8,128)(2,1)} async-done(((bf16[48,64,128]{2,1,0:T(8,128)(2,1)}), bf16[384,64,128]{2,1,0:T(8,128)(2,1)}) %all-gather.3.cloned.1.call-update) | async-done | bytes 6291472 | tf_op jit(solution)/shard_map/all_gather | solution.py:221
  282.7 0.0 copy-done.2
  282.7 0.0 copy-done.3
  282.7 0.0 copy-done.4
  282.8 0.0 copy-done.5
  282.8 0.0 copy-done.6
  282.8 0.0 copy-done.7
  282.8 0.0 copy-done.8
  282.8 10.3 %shard_map.49 = bf16[2,48,64,450]{3,2,1,0:T(8,128)(2,1)} custom-call(bf16[464,768]{1,0:T(8,128)(2,1)} %fusion.18.table, bf16[8,48,64,128]{3,2,1,0:T(8,128)(2,1)} %bitcast.20, bf16[48,32,128]{2,1,0:T(8,128)(2,1)} %get-tuple-element.30.refs_1_, bf16[48,32,128]{2,1,0:T(8,128)(2,1)} %copy-done.2, bf16[48,32,128]{2,1,0:T(8,128)(2,1)} %copy-done.3, ...), custom_call_target="tpu_custom_call" | custom-call | tf_op jit(solution)/shard_map/pallas_call | solution.py:144
  (27 shorter events, 0.1 us)
Async XLA Ops:
  11.7 53.6 %all-to-all-start = ((bf16[16,3,45,720]{3,2,1,0:T(8,128)(2,1)}), bf16[16,3,45,720]{3,2,1,0:T(8,128)(2,1)S(1)}, u32[]{:S(2)}, u32[]{:S(2)}) async-start(bf16[16,3,45,720]{3,2,1,0:T(8,128)(2,1)} %bitcast), calls=%async_computation | async-start | bytes 7077888 | tf_op jit(solution)/shard_map/all_to_all | solution.py:39
  20.4 115.9 %reduce-scatter.2.cloned.1.call-start = ((), (), s32[]{:S(2)}) async-start(), calls=%async_computation.7 | async-start | bytes 9953280 | tf_op jit(solution)/shard_map/reduce_scatter | solution.py:190
  65.4 1.7 copy-start
  67.1 69.1 %all-to-all-start.1 = ((bf16[16,3,64,720]{3,2,1,0:T(8,128)(2,1)}), bf16[16,3,64,720]{3,2,1,0:T(8,128)(2,1)}, u32[]{:S(2)}, u32[]{:S(2)}) async-start(bf16[16,3,64,720]{3,2,1,0:T(8,128)(2,1)} %bitcast.19), calls=%async_computation.2 | async-start | bytes 9437184 | tf_op jit(solution)/shard_map/all_to_all | solution.py:39
  140.8 21.1 %all-to-all-start.2 = ((bf16[16,3,45,192]{3,2,1,0:T(8,128)(2,1)}), bf16[16,3,45,192]{3,2,1,0:T(8,128)(2,1)S(1)}, u32[]{:S(2)}, u32[]{:S(2)}) async-start(bf16[16,3,45,192]{3,2,1,0:T(8,128)(2,1)} %reshape.297), calls=%async_computation.3 | async-start | bytes 2359296 | tf_op jit(solution)/shard_map/all_to_all | solution.py:39
  166.7 4.6 %copy-start.1 = (bf16[45,96,192]{2,1,0:T(8,128)(2,1)S(1)}, bf16[45,96,192]{2,1,0:T(8,128)(2,1)}, u32[]{:S(2)}) copy-start(bf16[45,96,192]{2,1,0:T(8,128)(2,1)} %param.6) | copy-start | bytes 4976644
  166.7 16.9 %all-to-all-start.3 = ((bf16[16,3,45,192]{3,2,1,0:T(8,128)(2,1)}), bf16[16,3,45,192]{3,2,1,0:T(8,128)(2,1)S(1)}, u32[]{:S(2)}, u32[]{:S(2)}) async-start(bf16[16,3,45,192]{3,2,1,0:T(8,128)(2,1)} %copy.24), calls=%async_computation.4 | async-start | bytes 2359296 | tf_op jit(solution)/shard_map/all_to_all | solution.py:39
  171.1 111.7 %all-gather.3.cloned.1.call-start = ((), (), s32[]{:S(2)}) async-start(), calls=%async_computation.8 | async-start | bytes 7077888 | tf_op jit(solution)/shard_map/all_gather | solution.py:221
  232.2 14.4 %collective-permute-start = (bf16[48,32,128]{2,1,0:T(8,128)(2,1)}, bf16[48,32,128]{2,1,0:T(8,128)(2,1)S(1)}, u32[]{:S(2)}, u32[]{:S(2)}) collective-permute-start(bf16[48,32,128]{2,1,0:T(8,128)(2,1)} %get-tuple-element.30.refs_1_), channel_id=1, source_target_pairs={{0,2},{1,3},{2,4},{3,5},{4,6},{5,7},{6,0},{7,1},{8,10},{9,11},{10,... | collective-permute-start | bytes 1179656 | tf_op jit(solution)/shard_map/ppermute | solution.py:163
  233.5 17.3 %collective-permute-start.1 = (bf16[48,32,128]{2,1,0:T(8,128)(2,1)}, bf16[48,32,128]{2,1,0:T(8,128)(2,1)S(1)}, u32[]{:S(2)}, u32[]{:S(2)}) collective-permute-start(bf16[48,32,128]{2,1,0:T(8,128)(2,1)} %get-tuple-element.30.refs_1_), channel_id=1, source_target_pairs={{0,6},{1,7},{2,0},{3,1},{4,2},{5,3},{6,4},{7,5},{8,14},{9,15},{10,... | collective-permute-start | bytes 1179656 | tf_op jit(solution)/shard_map/ppermute | solution.py:163
  234.9 17.3 %collective-permute-start.2 = (bf16[48,32,128]{2,1,0:T(8,128)(2,1)}, bf16[48,32,128]{2,1,0:T(8,128)(2,1)S(1)}, u32[]{:S(2)}, u32[]{:S(2)}) collective-permute-start(bf16[48,32,128]{2,1,0:T(8,128)(2,1)} %get-tuple-element.30.refs_1_), channel_id=1, source_target_pairs={{0,4},{1,5},{2,6},{3,7},{4,0},{5,1},{6,2},{7,3},{8,12},{9,13},{10,... | collective-permute-start | bytes 1179656 | tf_op jit(solution)/shard_map/ppermute | solution.py:163
  236.5 23.8 %collective-permute-start.3 = (bf16[48,32,128]{2,1,0:T(8,128)(2,1)}, bf16[48,32,128]{2,1,0:T(8,128)(2,1)S(1)}, u32[]{:S(2)}, u32[]{:S(2)}) collective-permute-start(bf16[48,32,128]{2,1,0:T(8,128)(2,1)} %get-tuple-element.30.refs_1_), channel_id=1, source_target_pairs={{0,1},{1,0},{2,3},{3,2},{4,5},{5,4},{6,7},{7,6},{8,9},{9,8},{10,11... | collective-permute-start | bytes 1179656 | tf_op jit(solution)/shard_map/ppermute | solution.py:166
  246.6 36.1 %copy-start.2 = (bf16[48,32,128]{2,1,0:T(8,128)(2,1)}, bf16[48,32,128]{2,1,0:T(8,128)(2,1)S(1)}, u32[]{:S(2)}) copy-start(bf16[48,32,128]{2,1,0:T(8,128)(2,1)S(1)} %collective-permute-done.refs_2_) | copy-start | bytes 1179652
  246.6 13.6 %collective-permute-start.4 = (bf16[48,32,128]{2,1,0:T(8,128)(2,1)S(1)}, bf16[48,32,128]{2,1,0:T(8,128)(2,1)S(1)}, u32[]{:S(2)}, u32[]{:S(2)}) collective-permute-start(bf16[48,32,128]{2,1,0:T(8,128)(2,1)S(1)} %collective-permute-done.refs_2_), channel_id=1, source_target_pairs={{0,1},{1,0},{2,3},{3,2},{4,5},{5,4},{6,7},{7,6},{8,9},{9,8},{10,11... | collective-permute-start | bytes 1179656 | tf_op jit(solution)/shard_map/ppermute | solution.py:166
  250.8 32.0 %copy-start.3 = (bf16[48,32,128]{2,1,0:T(8,128)(2,1)}, bf16[48,32,128]{2,1,0:T(8,128)(2,1)S(1)}, u32[]{:S(2)}) copy-start(bf16[48,32,128]{2,1,0:T(8,128)(2,1)S(1)} %collective-permute-done.1.refs_3_) | copy-start | bytes 1179652
  250.8 9.5 %collective-permute-start.5 = (bf16[48,32,128]{2,1,0:T(8,128)(2,1)S(1)}, bf16[48,32,128]{2,1,0:T(8,128)(2,1)S(1)}, u32[]{:S(2)}, u32[]{:S(2)}) collective-permute-start(bf16[48,32,128]{2,1,0:T(8,128)(2,1)S(1)} %collective-permute-done.1.refs_3_), channel_id=1, source_target_pairs={{0,1},{1,0},{2,3},{3,2},{4,5},{5,4},{6,7},{7,6},{8,9},{9,8},{10,11... | collective-permute-start | bytes 1179656 | tf_op jit(solution)/shard_map/ppermute | solution.py:166
  252.2 30.6 %copy-start.4 = (bf16[48,32,128]{2,1,0:T(8,128)(2,1)}, bf16[48,32,128]{2,1,0:T(8,128)(2,1)S(1)}, u32[]{:S(2)}) copy-start(bf16[48,32,128]{2,1,0:T(8,128)(2,1)S(1)} %collective-permute-done.2.refs_4_) | copy-start | bytes 1179652
  252.2 9.5 %collective-permute-start.6 = (bf16[48,32,128]{2,1,0:T(8,128)(2,1)S(1)}, bf16[48,32,128]{2,1,0:T(8,128)(2,1)S(1)}, u32[]{:S(2)}, u32[]{:S(2)}) collective-permute-start(bf16[48,32,128]{2,1,0:T(8,128)(2,1)S(1)} %collective-permute-done.2.refs_4_), channel_id=1, source_target_pairs={{0,1},{1,0},{2,3},{3,2},{4,5},{5,4},{6,7},{7,6},{8,9},{9,8},{10,11... | collective-permute-start | bytes 1179656 | tf_op jit(solution)/shard_map/ppermute | solution.py:166
  260.3 22.5 %copy-start.5 = (bf16[48,32,128]{2,1,0:T(8,128)(2,1)}, bf16[48,32,128]{2,1,0:T(8,128)(2,1)S(1)}, u32[]{:S(2)}) copy-start(bf16[48,32,128]{2,1,0:T(8,128)(2,1)S(1)} %collective-permute-done.3.refs_5_) | copy-start | bytes 1179652
  260.3 22.5 %copy-start.6 = (bf16[48,32,128]{2,1,0:T(8,128)(2,1)}, bf16[48,32,128]{2,1,0:T(8,128)(2,1)S(1)}, u32[]{:S(2)}) copy-start(bf16[48,32,128]{2,1,0:T(8,128)(2,1)S(1)} %collective-permute-done.4.refs_6_) | copy-start | bytes 1179652
  260.3 22.5 %copy-start.7 = (bf16[48,32,128]{2,1,0:T(8,128)(2,1)}, bf16[48,32,128]{2,1,0:T(8,128)(2,1)S(1)}, u32[]{:S(2)}) copy-start(bf16[48,32,128]{2,1,0:T(8,128)(2,1)S(1)} %collective-permute-done.5.refs_7_) | copy-start | bytes 1179652
  261.7 21.0 %copy-start.8 = (bf16[48,32,128]{2,1,0:T(8,128)(2,1)}, bf16[48,32,128]{2,1,0:T(8,128)(2,1)S(1)}, u32[]{:S(2)}) copy-start(bf16[48,32,128]{2,1,0:T(8,128)(2,1)S(1)} %collective-permute-done.6.refs_8_) | copy-start | bytes 1179652
Sparse Core Ops, SparseCore 0:
  65.5 61.3 reduce-scatter.1
  232.3 50.3 all-gather.2

commit v4 on v3

--- a/solution.py
+++ b/solution.py
@@ -25,7 +25,7 @@
 WIDE = 464
 LANES = 128
 STEP = 8
-VMEM = 56 * 1024 * 1024
+MIB = 1024 * 1024
 BF = jnp.bfloat16
 
 
@@ -61,7 +61,7 @@
         ],
         out_specs=pl.BlockSpec((LONS, step, 2 * SLOTS, CHAN), lambda s: (0, s, 0, 0)),
         out_shape=jax.ShapeDtypeStruct((LONS, ROWS, 2 * SLOTS, CHAN), BF),
-        compiler_params=pltpu.CompilerParams(vmem_limit_bytes=VMEM),
+        compiler_params=pltpu.CompilerParams(vmem_limit_bytes=16 * MIB),
     )(waves_in, field)
 
 
@@ -85,7 +85,7 @@
         synthesis_kernel,
         out_shape=jax.ShapeDtypeStruct((LATS, HALF * LINES, LANES), BF),
         scratch_shapes=[pltpu.VMEM((HALF * LINES, LANES), jnp.float32)],
-        compiler_params=pltpu.CompilerParams(vmem_limit_bytes=VMEM),
+        compiler_params=pltpu.CompilerParams(vmem_limit_bytes=20 * MIB),
         cost_estimate=pl.CostEstimate(
             flops=2 * EACH * 1024 * 720 * 192, bytes_accessed=6000000, transcendentals=0
         ),
@@ -114,7 +114,7 @@
             pltpu.VMEM((HALF * LINES, LANES), jnp.float32),
             pltpu.VMEM((HALF * LATS * LINES, LANES), jnp.float32),
         ],
-        compiler_params=pltpu.CompilerParams(vmem_limit_bytes=VMEM),
+        compiler_params=pltpu.CompilerParams(vmem_limit_bytes=10 * MIB),
     )(rows)
 
 
@@ -147,7 +147,7 @@
         in_specs=[pl.BlockSpec(table.shape, lambda s: (0, 0))] + [spec(v) for v in pieces],
         out_specs=pl.BlockSpec((2, STEP, OUT_ROWS, OUT_COLS), lambda s: (0, s, 0, 0)),
         out_shape=jax.ShapeDtypeStruct((2, HALF, OUT_ROWS, OUT_COLS), BF),
-        compiler_params=pltpu.CompilerParams(vmem_limit_bytes=VMEM),
+        compiler_params=pltpu.CompilerParams(vmem_limit_bytes=56 * MIB),
     )(table, *pieces)
     return out.reshape(CHAN, OUT_ROWS, OUT_COLS)
 
@@ -191,9 +191,9 @@
     wtab = swap(wtab, "lat")
     spectrum, wtab, lon = lax.optimization_barrier((spectrum, wtab, lon))
     spectrum = spectrum.reshape(ROWS, 2, LATS, EACH, CHAN)
-    spectrum = jnp.transpose(spectrum, (2, 3, 0, 1, 4)).reshape(LATS, EACH, ROWS, 2 * CHAN)
+    spectrum = jnp.transpose(spectrum, (2, 3, 1, 0, 4))
     spectrum = swap(spectrum, "lat")
-    spectrum = jnp.transpose(spectrum, (1, 0, 2, 3)).reshape(EACH, 720, 2 * CHAN)
+    spectrum = jnp.transpose(spectrum, (1, 0, 3, 2, 4)).reshape(EACH, 720, 2 * CHAN)
 
     coef = jnp.einsum("ajlq,jqn->ajln", ftab, spectrum, preferred_element_type=jnp.float32)
     coef = swap(coef.astype(BF), "lat").reshape(SLOTS, ROWS, 2 * CHAN)

time: 301 us -> 294 us (0.977)
  Pallas kernels: 28.7 us -> 22.8 us
    pallas_call x1, Pallas kernels: 7.04 us -> 3.94 us  [shares(): pl.pallas_call(share_kernel, grid=(ROWS // step,), in_specs=[pl.BlockSpec...]
    unnamed x19 -> x23, local copies, waits for them, and re-layouts: 4.78 us -> 6.52 us
  transfers between devices with their start and end apart: 13 -> 13, of which waited for: 6 -> 6; matrix products, arithmetic and copies ran while one was open for 6% -> 6% of each run, Pallas kernels for 2% -> 1%
where the time goes in v4:
time: 294 us; the launch traced here: 293 us
  waiting for transfers between devices  125 us (43%)
  starting transfers between devices  60.4 us (21%)
  blocking collectives  31.4 us (11%)
  Pallas kernels  22.8 us (8%)
  local copies, waits for them, and re-layouts  21.8 us (7%)
  between operations  13.7 us (5%)
  other arithmetic  12.2 us (4%)
  matrix products  6.05 us (2%)
    all_to_all x4, waiting for transfers between devices, swap(): return lax.all_to_all(x, axis, split_axis=0, concat_axis=0, tiled=True)  102 us
    all_to_all x4, starting transfers between devices, swap(): return lax.all_to_all(x, axis, split_axis=0, concat_axis=0, tiled=True)  32.7 us
    all_to_all x2, blocking collectives, swap(): return lax.all_to_all(x, axis, split_axis=0, concat_axis=0, tiled=True)  31.4 us
    ppermute x4, starting transfers between devices, across(): return lax.ppermute(u, 'lon', [(i, i ^ 1) for i in range(8)])  23.1 us
    all_gather x1, waiting for transfers between devices, local(): pieces = [lax.all_gather(rows, 'lon', axis=0)] + gather_lon(rest)  21.5 us
    pallas_call x1, Pallas kernels, to_longitudes(): pl.pallas_call(output_kernel, grid=(HALF // STEP,), in_specs=[pl.BlockSpe...  10.3 us
    convert_element_type x2, other arithmetic, waves(): return (jnp.cos(angles) * jnp.where(valid, factor, 0.0)).astype(BF)  10.2 us
    unnamed x23, local copies, waits for them, and re-layouts  6.52 us
  transfers between devices with their start and end apart: 13, of which 6 were waited for; matrix products, arithmetic and copies ran while one was open for 6% of the time, Pallas kernels for 1%

profile of v4, /device:TPU:1, one launch (start us, length us, event | category | flops | bytes accessed | tf_op | source)
XLA Modules:
  0.0 293.0 jit_solution(11637137734319342217)
XLA Ops:
  6.5 3.0 %copy.29 = bf16[46,45,720]{2,1,0:T(8,128)(2,1)S(1)} copy(bf16[46,45,720]{2,0,1:T(8,128)(2,1)} %param.5) | data formatting | bytes 5961600
  9.6 2.2 pad.8.clone
  11.7 8.6 %all-to-all-start = ((bf16[16,3,45,720]{3,2,1,0:T(8,128)(2,1)}), bf16[16,3,45,720]{3,2,1,0:T(8,128)(2,1)}, u32[]{:S(2)}, u32[]{:S(2)}) async-start(bf16[16,3,45,720]{3,2,1,0:T(8,128)(2,1)} %bitcast), calls=%async_computation | async-start | bytes 7077888 | tf_op jit(solution)/shard_map/all_to_all | solution.py:39
  20.4 0.0 reduce-scatter.2.cloned.1.call-start
  20.4 0.0 copy-start.1
  20.5 5.4 %pad.9 = bf16[48,64,720]{2,1,0:T(8,128)(2,1)} pad(bf16[46,64,720]{2,1,0:T(8,128)(2,1)} %bitcast.25, bf16[]{:T(256)} %constant.255.clone.1), padding=0_2x0_0x0_0 | pad | bytes 8663042 | tf_op jit(solution)/shard_map/jit(_pad)/pad | solution.py:188
  25.9 3.8 %fusion.33.waves_in = bf16[768,180]{1,0:T(8,128)(2,1)S(1)} fusion(f32[768]{0:T(1024)S(1)} %fusion.52, s32[768]{0:T(1024)S(1)} %get-tuple-element.33, s32[180]{0:T(256)S(1)} %iota_add_fusion.1, s32[768]{0:T(1024)S(1)} %get-tuple-element.34), kind=kLoop, calls=%fused_computation.29 | loop fusion | flops 1658880 | bytes 286416 | tf_op jit(solution)/shard_map/convert_element_type | solution.py:35
  29.8 0.0 copy-done.1
  29.8 3.9 %shard_map.46 = bf16[8,45,96,96]{3,2,1,0:T(8,128)(2,1)S(1)} custom-call(bf16[768,180]{1,0:T(8,128)(2,1)S(1)} %fusion.33.waves_in, bf16[45,180,96]{2,1,0:T(8,128)(2,1)S(1)} %bitcast.19), custom_call_target="tpu_custom_call" | custom-call | tf_op jit(solution)/shard_map/pallas_call | solution.py:55
  33.7 0.0 copy-start
  33.7 3.4 %copy-done = bf16[8,45,96,96]{3,2,1,0:T(8,128)(2,1)} copy-done((bf16[8,45,96,96]{3,2,1,0:T(8,128)(2,1)}, bf16[8,45,96,96]{3,2,1,0:T(8,128)(2,1)S(1)}, u32[]{:S(2)}) %copy-start) | copy-done | bytes 6635544
  37.2 28.2 %all-to-all-done = bf16[16,3,45,720]{3,2,1,0:T(8,128)(2,1)} async-done(((bf16[16,3,45,720]{3,2,1,0:T(8,128)(2,1)}), bf16[16,3,45,720]{3,2,1,0:T(8,128)(2,1)}, u32[]{:S(2)}, u32[]{:S(2)}) %all-to-all-start) | async-done | bytes 3110432 | tf_op jit(solution)/shard_map/all_to_all | solution.py:39
  65.4 0.0 reduce-scatter.2.cloned.1.call-update
  65.4 11.7 %all-to-all-start.1 = ((bf16[16,3,64,720]{3,2,1,0:T(8,128)(2,1)}), bf16[16,3,64,720]{3,2,1,0:T(8,128)(2,1)}, u32[]{:S(2)}, u32[]{:S(2)}) async-start(bf16[16,3,64,720]{3,2,1,0:T(8,128)(2,1)} %bitcast.20), calls=%async_computation.2 | async-start | bytes 9437184 | tf_op jit(solution)/shard_map/all_to_all | solution.py:39
  77.2 0.1 concatenate.25
  77.3 0.1 concatenate.24
  77.5 57.2 %all-to-all-done.1.table = bf16[16,3,64,720]{3,2,1,0:T(8,128)(2,1)} async-done(((bf16[16,3,64,720]{3,2,1,0:T(8,128)(2,1)}), bf16[16,3,64,720]{3,2,1,0:T(8,128)(2,1)}, u32[]{:S(2)}, u32[]{:S(2)}) %all-to-all-start.1) | async-done | bytes 4423712 | tf_op jit(solution)/shard_map/all_to_all | solution.py:39
  134.7 1.7 copy.18
  136.3 2.1 copy.19
  138.5 8.0 %all-to-all-start.2 = ((bf16[16,3,2,45,96]{4,2,3,1,0:T(2,128)(2,1)}), bf16[16,3,2,45,96]{4,2,3,1,0:T(2,128)(2,1)S(1)}, u32[]{:S(2)}, u32[]{:S(2)}) async-start(bf16[16,3,2,45,96]{4,2,3,1,0:T(2,128)(2,1)} %copy.19), calls=%async_computation.3 | async-start | bytes 2211840 | tf_op jit(solution)/shard_map/all_to_all | solution.py:39
  146.5 0.1 concatenate.23
  146.6 12.3 %all-to-all-done.2 = bf16[16,3,2,45,96]{4,2,3,1,0:T(2,128)(2,1)S(1)} async-done(((bf16[16,3,2,45,96]{4,2,3,1,0:T(2,128)(2,1)}), bf16[16,3,2,45,96]{4,2,3,1,0:T(2,128)(2,1)S(1)}, u32[]{:S(2)}, u32[]{:S(2)}) %all-to-all-start.2) | async-done | bytes 829472 | tf_op jit(solution)/shard_map/all_to_all | solution.py:39
  158.9 0.8 copy.20
  159.7 0.7 reshape.295
  160.4 3.1 %fusion.22 = bf16[16,3,45,192]{3,2,0,1:T(8,128)(2,1)S(1)} fusion(bf16[3,720,192,1]{2,1,3,0:T(8,128)(2,1)S(1)} %reshape.295, bf16[16,3,45,720]{3,2,1,0:T(8,128)(2,1)} %all-to-all-done), kind=kOutput, calls=%fused_computation.20 | convolution fusion | flops 597611520 | bytes 4769280 | tf_op jit(solution)/shard_map/ajlq,jqn->ajln/dot_general | solution.py:198
  163.5 1.1 copy.23
  164.6 4.4 %all-to-all-start.3 = ((bf16[16,3,45,192]{3,2,1,0:T(8,128)(2,1)}), bf16[16,3,45,192]{3,2,1,0:T(8,128)(2,1)S(1)}, u32[]{:S(2)}, u32[]{:S(2)}) async-start(bf16[16,3,45,192]{3,2,1,0:T(8,128)(2,1)} %copy.23), calls=%async_computation.4 | async-start | bytes 2359296 | tf_op jit(solution)/shard_map/all_to_all | solution.py:39
  169.0 0.2 all-gather.3.cloned.1.call-start
  169.3 0.0 copy-done.3
  169.3 1.9 slice_negate_fusion
  171.2 6.4 %fusion.18.table = bf16[464,768]{1,0:T(8,128)(2,1)} fusion(f32[768]{0:T(1024)S(1)} %broadcast_select_fusion, s32[768]{0:T(1024)S(1)} %broadcast_multiply_fusion, s32[464]{0:T(512)S(1)} %iota_add_fusion, s32[768]{0:T(1024)S(1)} %concatenate.23), kind=kLoop, calls=%fused_computation.15 | loop fusion | flops 4276224 | bytes 723776 | tf_op jit(solution)/shard_map/convert_element_type | solution.py:35
  177.5 4.1 %all-to-all-done.3 = bf16[16,3,45,192]{3,2,1,0:T(8,128)(2,1)S(1)} async-done(((bf16[16,3,45,192]{3,2,1,0:T(8,128)(2,1)}), bf16[16,3,45,192]{3,2,1,0:T(8,128)(2,1)S(1)}, u32[]{:S(2)}, u32[]{:S(2)}) %all-to-all-start.3) | async-done | bytes 829472 | tf_op jit(solution)/shard_map/all_to_all | solution.py:39
  181.7 3.0 %fusion.25 = bf16[48,45,192]{2,0,1:T(8,128)(2,1)S(1)} fusion(bf16[45,96,96]{2,1,0:T(8,128)(2,1)} %get-tuple-element.32, bf16[45,96,96]{2,1,0:T(8,128)(2,1)} %get-tuple-element.31, bf16[45,96,192]{2,1,0:T(8,128)(2,1)S(1)} %copy-done.3, bf16[48,45,192]{2,1,0:T(8,128)(2,1)S(1)} %bitcast.27), kind=kOutput, calls=%fused_computation.21 | convolution fusion | flops 169620480 | bytes 4976640 | tf_op jit(solution)/shard_map/mlt,ltu->mlu/dot_general | solution.py:217
  184.6 0.4 copy.25
  185.0 15.8 %all_to_all.30 = bf16[16,3,45,192]{3,2,1,0:T(8,128)(2,1)S(1)} all-to-all(bf16[16,3,45,192]{3,2,1,0:T(8,128)(2,1)S(1)} %bitcast.23), channel_id=1, replica_groups=mesh['lat'=16,'lon'=8] {'lat'}, dimensions={0} | all-to-all | bytes 1658880 | tf_op jit(solution)/shard_map/all_to_all | solution.py:39
  200.8 0.1 copy.26
  200.9 0.6 reshape.289.mixed
  201.4 5.3 %shard_map.47 = bf16[16,288,128]{2,1,0:T(8,128)(2,1)S(1)} custom-call(bf16[3,720,192]{2,1,0:T(8,128)(2,1)S(1)} %reshape.289.mixed, bf16[16,3,64,720]{3,2,1,0:T(8,128)(2,1)} %all-to-all-done.1.table), custom_call_target="tpu_custom_call" | custom-call | flops 849346560 | bytes 6000000 | tf_op jit(solution)/shard_map/pallas_call | solution.py:84
  206.7 15.6 %all_to_all.31.rows = bf16[16,288,128]{2,1,0:T(8,128)(2,1)S(1)} all-to-all(bf16[16,288,128]{2,1,0:T(8,128)(2,1)S(1)} %shard_map.47), channel_id=1, replica_groups=mesh['lat'=16,'lon'=8] {'lat'}, dimensions={0} | all-to-all | bytes 2359296 | tf_op jit(solution)/shard_map/all_to_all | solution.py:39
  222.4 3.3 %shard_map.48 = (bf16[48,64,128]{2,1,0:T(8,128)(2,1)}, bf16[48,32,128]{2,1,0:T(8,128)(2,1)S(1)}) custom-call(bf16[16,288,128]{2,1,0:T(8,128)(2,1)S(1)} %all_to_all.31.rows), custom_call_target="tpu_custom_call" | custom-call | tf_op jit(solution)/shard_map/pallas_call | solution.py:107
  225.7 0.0 all-gather.3.cloned.1.call-update
  225.7 1.3 collective-permute-start
  227.0 1.5 collective-permute-start.1
  228.4 1.5 collective-permute-start.2
  230.0 10.0 %collective-permute-start.3 = (bf16[48,32,128]{2,1,0:T(8,128)(2,1)S(1)}, bf16[48,32,128]{2,1,0:T(8,128)(2,1)S(1)}, u32[]{:S(2)}, u32[]{:S(2)}) collective-permute-start(bf16[48,32,128]{2,1,0:T(8,128)(2,1)S(1)} %get-tuple-element.30.refs_1_), channel_id=1, source_target_pairs={{0,1},{1,0},{2,3},{3,2},{4,5},{5,4},{6,7},{7,6},{8,9},{9,8},{10,11... | collective-permute-start | bytes 1179656 | tf_op jit(solution)/shard_map/ppermute | solution.py:166
  240.0 0.0 collective-permute-done.refs_2_
  240.0 3.9 %collective-permute-start.4 = (bf16[48,32,128]{2,1,0:T(8,128)(2,1)S(1)}, bf16[48,32,128]{2,1,0:T(8,128)(2,1)S(1)}, u32[]{:S(2)}, u32[]{:S(2)}) collective-permute-start(bf16[48,32,128]{2,1,0:T(8,128)(2,1)S(1)} %collective-permute-done.refs_2_), channel_id=1, source_target_pairs={{0,1},{1,0},{2,3},{3,2},{4,5},{5,4},{6,7},{7,6},{8,9},{9,8},{10,11... | collective-permute-start | bytes 1179656 | tf_op jit(solution)/shard_map/ppermute | solution.py:166
  243.9 0.0 collective-permute-done.1.refs_3_
  243.9 1.4 collective-permute-start.5
  245.4 0.0 collective-permute-done.2.refs_4_
  245.4 7.7 %collective-permute-start.6 = (bf16[48,32,128]{2,1,0:T(8,128)(2,1)S(1)}, bf16[48,32,128]{2,1,0:T(8,128)(2,1)S(1)}, u32[]{:S(2)}, u32[]{:S(2)}) collective-permute-start(bf16[48,32,128]{2,1,0:T(8,128)(2,1)S(1)} %collective-permute-done.2.refs_4_), channel_id=1, source_target_pairs={{0,1},{1,0},{2,3},{3,2},{4,5},{5,4},{6,7},{7,6},{8,9},{9,8},{10,11... | collective-permute-start | bytes 1179656 | tf_op jit(solution)/shard_map/ppermute | solution.py:166
  253.1 0.0 collective-permute-done.3.refs_5_
  253.1 0.0 collective-permute-done.4.refs_6_
  253.1 0.0 copy-start.8
  253.1 0.0 collective-permute-done.5.refs_7_
  253.1 0.0 copy-start.9
  253.1 1.3 collective-permute-done.6.refs_8_
  254.4 21.5 %all-gather.3.cloned.1.call-done = bf16[384,64,128]{2,1,0:T(8,128)(2,1)} async-done(((bf16[48,64,128]{2,1,0:T(8,128)(2,1)}), bf16[384,64,128]{2,1,0:T(8,128)(2,1)}) %all-gather.3.cloned.1.call-update) | async-done | bytes 6291472 | tf_op jit(solution)/shard_map/all_gather | solution.py:221
  275.9 0.0 copy-done.2
  275.9 0.0 copy-done.4
  275.9 0.0 copy-done.5
  275.9 0.0 copy-done.6
  275.9 0.0 copy-done.7
  276.0 10.3 %shard_map.49 = bf16[2,48,64,450]{3,2,1,0:T(8,128)(2,1)} custom-call(bf16[464,768]{1,0:T(8,128)(2,1)} %fusion.18.table, bf16[8,48,64,128]{3,2,1,0:T(8,128)(2,1)} %bitcast.21, bf16[48,32,128]{2,1,0:T(8,128)(2,1)} %copy-done.2, bf16[48,32,128]{2,1,0:T(8,128)(2,1)} %copy-done.4, bf16[48,32,128]{2,1,0:T(8,128)(2,1)} %copy-done.5, ...), custom_call_target="tpu_custom_call" | custom-call | tf_op jit(solution)/shard_map/pallas_call | solution.py:144
  (30 shorter events, 0.1 us)
Async XLA Ops:
  11.7 53.6 %all-to-all-start = ((bf16[16,3,45,720]{3,2,1,0:T(8,128)(2,1)}), bf16[16,3,45,720]{3,2,1,0:T(8,128)(2,1)}, u32[]{:S(2)}, u32[]{:S(2)}) async-start(bf16[16,3,45,720]{3,2,1,0:T(8,128)(2,1)} %bitcast), calls=%async_computation | async-start | bytes 7077888 | tf_op jit(solution)/shard_map/all_to_all | solution.py:39
  20.4 114.3 %reduce-scatter.2.cloned.1.call-start = ((), (), s32[]{:S(2)}) async-start(), calls=%async_computation.7 | async-start | bytes 9953280 | tf_op jit(solution)/shard_map/reduce_scatter | solution.py:190
  20.4 9.3 %copy-start.1 = (bf16[96,45,180]{0,2,1:T(8,128)(2,1)S(1)}, bf16[96,45,180]{0,2,1:T(8,128)(2,1)}, u32[]{:S(2)}) copy-start(bf16[96,45,180]{0,2,1:T(8,128)(2,1)} %param.4) | copy-start | bytes 4665604
  33.7 3.4 %copy-start = (bf16[8,45,96,96]{3,2,1,0:T(8,128)(2,1)}, bf16[8,45,96,96]{3,2,1,0:T(8,128)(2,1)S(1)}, u32[]{:S(2)}) copy-start(bf16[8,45,96,96]{3,2,1,0:T(8,128)(2,1)S(1)} %shard_map.46) | copy-start | bytes 19906564
  65.4 69.2 %all-to-all-start.1 = ((bf16[16,3,64,720]{3,2,1,0:T(8,128)(2,1)}), bf16[16,3,64,720]{3,2,1,0:T(8,128)(2,1)}, u32[]{:S(2)}, u32[]{:S(2)}) async-start(bf16[16,3,64,720]{3,2,1,0:T(8,128)(2,1)} %bitcast.20), calls=%async_computation.2 | async-start | bytes 9437184 | tf_op jit(solution)/shard_map/all_to_all | solution.py:39
  138.5 20.4 %all-to-all-start.2 = ((bf16[16,3,2,45,96]{4,2,3,1,0:T(2,128)(2,1)}), bf16[16,3,2,45,96]{4,2,3,1,0:T(2,128)(2,1)S(1)}, u32[]{:S(2)}, u32[]{:S(2)}) async-start(bf16[16,3,2,45,96]{4,2,3,1,0:T(2,128)(2,1)} %copy.19), calls=%async_computation.3 | async-start | bytes 2211840 | tf_op jit(solution)/shard_map/all_to_all | solution.py:39
  164.6 4.7 %copy-start.3 = (bf16[45,96,192]{2,1,0:T(8,128)(2,1)S(1)}, bf16[45,96,192]{2,1,0:T(8,128)(2,1)}, u32[]{:S(2)}) copy-start(bf16[45,96,192]{2,1,0:T(8,128)(2,1)} %param.6) | copy-start | bytes 4976644
  164.6 17.0 %all-to-all-start.3 = ((bf16[16,3,45,192]{3,2,1,0:T(8,128)(2,1)}), bf16[16,3,45,192]{3,2,1,0:T(8,128)(2,1)S(1)}, u32[]{:S(2)}, u32[]{:S(2)}) async-start(bf16[16,3,45,192]{3,2,1,0:T(8,128)(2,1)} %copy.23), calls=%async_computation.4 | async-start | bytes 2359296 | tf_op jit(solution)/shard_map/all_to_all | solution.py:39
  169.0 106.9 %all-gather.3.cloned.1.call-start = ((), (), s32[]{:S(2)}) async-start(), calls=%async_computation.8 | async-start | bytes 7077888 | tf_op jit(solution)/shard_map/all_gather | solution.py:221
  225.7 50.2 %copy-start.2 = (bf16[48,32,128]{2,1,0:T(8,128)(2,1)}, bf16[48,32,128]{2,1,0:T(8,128)(2,1)S(1)}, u32[]{:S(2)}) copy-start(bf16[48,32,128]{2,1,0:T(8,128)(2,1)S(1)} %get-tuple-element.30.refs_1_) | copy-start | bytes 1179652
  225.7 14.3 %collective-permute-start = (bf16[48,32,128]{2,1,0:T(8,128)(2,1)S(1)}, bf16[48,32,128]{2,1,0:T(8,128)(2,1)S(1)}, u32[]{:S(2)}, u32[]{:S(2)}) collective-permute-start(bf16[48,32,128]{2,1,0:T(8,128)(2,1)S(1)} %get-tuple-element.30.refs_1_), channel_id=1, source_target_pairs={{0,2},{1,3},{2,4},{3,5},{4,6},{5,7},{6,0},{7,1},{8,10},{9,11},{10,... | collective-permute-start | bytes 1179656 | tf_op jit(solution)/shard_map/ppermute | solution.py:163
  227.0 17.0 %collective-permute-start.1 = (bf16[48,32,128]{2,1,0:T(8,128)(2,1)S(1)}, bf16[48,32,128]{2,1,0:T(8,128)(2,1)S(1)}, u32[]{:S(2)}, u32[]{:S(2)}) collective-permute-start(bf16[48,32,128]{2,1,0:T(8,128)(2,1)S(1)} %get-tuple-element.30.refs_1_), channel_id=1, source_target_pairs={{0,6},{1,7},{2,0},{3,1},{4,2},{5,3},{6,4},{7,5},{8,14},{9,15},{10,... | collective-permute-start | bytes 1179656 | tf_op jit(solution)/shard_map/ppermute | solution.py:163
  228.4 16.9 %collective-permute-start.2 = (bf16[48,32,128]{2,1,0:T(8,128)(2,1)S(1)}, bf16[48,32,128]{2,1,0:T(8,128)(2,1)S(1)}, u32[]{:S(2)}, u32[]{:S(2)}) collective-permute-start(bf16[48,32,128]{2,1,0:T(8,128)(2,1)S(1)} %get-tuple-element.30.refs_1_), channel_id=1, source_target_pairs={{0,4},{1,5},{2,6},{3,7},{4,0},{5,1},{6,2},{7,3},{8,12},{9,13},{10,... | collective-permute-start | bytes 1179656 | tf_op jit(solution)/shard_map/ppermute | solution.py:163
  230.0 23.1 %collective-permute-start.3 = (bf16[48,32,128]{2,1,0:T(8,128)(2,1)S(1)}, bf16[48,32,128]{2,1,0:T(8,128)(2,1)S(1)}, u32[]{:S(2)}, u32[]{:S(2)}) collective-permute-start(bf16[48,32,128]{2,1,0:T(8,128)(2,1)S(1)} %get-tuple-element.30.refs_1_), channel_id=1, source_target_pairs={{0,1},{1,0},{2,3},{3,2},{4,5},{5,4},{6,7},{7,6},{8,9},{9,8},{10,11... | collective-permute-start | bytes 1179656 | tf_op jit(solution)/shard_map/ppermute | solution.py:166
  240.0 35.9 %copy-start.4 = (bf16[48,32,128]{2,1,0:T(8,128)(2,1)}, bf16[48,32,128]{2,1,0:T(8,128)(2,1)S(1)}, u32[]{:S(2)}) copy-start(bf16[48,32,128]{2,1,0:T(8,128)(2,1)S(1)} %collective-permute-done.refs_2_) | copy-start | bytes 1179652
  240.0 13.1 %collective-permute-start.4 = (bf16[48,32,128]{2,1,0:T(8,128)(2,1)S(1)}, bf16[48,32,128]{2,1,0:T(8,128)(2,1)S(1)}, u32[]{:S(2)}, u32[]{:S(2)}) collective-permute-start(bf16[48,32,128]{2,1,0:T(8,128)(2,1)S(1)} %collective-permute-done.refs_2_), channel_id=1, source_target_pairs={{0,1},{1,0},{2,3},{3,2},{4,5},{5,4},{6,7},{7,6},{8,9},{9,8},{10,11... | collective-permute-start | bytes 1179656 | tf_op jit(solution)/shard_map/ppermute | solution.py:166
  243.9 32.0 %copy-start.5 = (bf16[48,32,128]{2,1,0:T(8,128)(2,1)}, bf16[48,32,128]{2,1,0:T(8,128)(2,1)S(1)}, u32[]{:S(2)}) copy-start(bf16[48,32,128]{2,1,0:T(8,128)(2,1)S(1)} %collective-permute-done.1.refs_3_) | copy-start | bytes 1179652
  243.9 9.2 %collective-permute-start.5 = (bf16[48,32,128]{2,1,0:T(8,128)(2,1)S(1)}, bf16[48,32,128]{2,1,0:T(8,128)(2,1)S(1)}, u32[]{:S(2)}, u32[]{:S(2)}) collective-permute-start(bf16[48,32,128]{2,1,0:T(8,128)(2,1)S(1)} %collective-permute-done.1.refs_3_), channel_id=1, source_target_pairs={{0,1},{1,0},{2,3},{3,2},{4,5},{5,4},{6,7},{7,6},{8,9},{9,8},{10,11... | collective-permute-start | bytes 1179656 | tf_op jit(solution)/shard_map/ppermute | solution.py:166
  245.4 30.5 %copy-start.6 = (bf16[48,32,128]{2,1,0:T(8,128)(2,1)}, bf16[48,32,128]{2,1,0:T(8,128)(2,1)S(1)}, u32[]{:S(2)}) copy-start(bf16[48,32,128]{2,1,0:T(8,128)(2,1)S(1)} %collective-permute-done.2.refs_4_) | copy-start | bytes 1179652
  245.4 9.1 %collective-permute-start.6 = (bf16[48,32,128]{2,1,0:T(8,128)(2,1)S(1)}, bf16[48,32,128]{2,1,0:T(8,128)(2,1)S(1)}, u32[]{:S(2)}, u32[]{:S(2)}) collective-permute-start(bf16[48,32,128]{2,1,0:T(8,128)(2,1)S(1)} %collective-permute-done.2.refs_4_), channel_id=1, source_target_pairs={{0,1},{1,0},{2,3},{3,2},{4,5},{5,4},{6,7},{7,6},{8,9},{9,8},{10,11... | collective-permute-start | bytes 1179656 | tf_op jit(solution)/shard_map/ppermute | solution.py:166
  253.1 22.8 %copy-start.7 = (bf16[48,32,128]{2,1,0:T(8,128)(2,1)}, bf16[48,32,128]{2,1,0:T(8,128)(2,1)S(1)}, u32[]{:S(2)}) copy-start(bf16[48,32,128]{2,1,0:T(8,128)(2,1)S(1)} %collective-permute-done.3.refs_5_) | copy-start | bytes 1179652
  253.1 22.8 %copy-start.8 = (bf16[48,32,128]{2,1,0:T(8,128)(2,1)}, bf16[48,32,128]{2,1,0:T(8,128)(2,1)S(1)}, u32[]{:S(2)}) copy-start(bf16[48,32,128]{2,1,0:T(8,128)(2,1)S(1)} %collective-permute-done.4.refs_6_) | copy-start | bytes 1179652
  253.1 22.8 %copy-start.9 = (bf16[48,32,128]{2,1,0:T(8,128)(2,1)}, bf16[48,32,128]{2,1,0:T(8,128)(2,1)S(1)}, u32[]{:S(2)}) copy-start(bf16[48,32,128]{2,1,0:T(8,128)(2,1)S(1)} %collective-permute-done.5.refs_7_) | copy-start | bytes 1179652
  254.4 21.5 %copy-start.10 = (bf16[48,32,128]{2,1,0:T(8,128)(2,1)}, bf16[48,32,128]{2,1,0:T(8,128)(2,1)S(1)}, u32[]{:S(2)}) copy-start(bf16[48,32,128]{2,1,0:T(8,128)(2,1)S(1)} %collective-permute-done.6.refs_8_) | copy-start | bytes 1179652
Sparse Core Ops, SparseCore 0:
  65.5 61.4 reduce-scatter.1
  225.8 50.0 all-gather.2

commit v5 on v4

--- a/solution.py
+++ b/solution.py
@@ -24,7 +24,7 @@
 OUT_COLS = 450
 WIDE = 464
 LANES = 128
-STEP = 8
+STEP = 16
 MIB = 1024 * 1024
 BF = jnp.bfloat16
 
@@ -72,7 +72,7 @@
         made.append(jnp.dot(t, mixed[k], preferred_element_type=jnp.float32))
     for b in range(LATS):
         for k in range(EACH):
-            one = made[k][b * OUT_ROWS : (b + 1) * OUT_ROWS].T
+            one = made[k][b * OUT_ROWS : (b + 1) * OUT_ROWS].astype(BF).T.astype(jnp.float32)
             for r in range(2):
                 low, high = one[r * CHAN : r * CHAN + HALF], one[r * CHAN + HALF : (r + 1) * CHAN]
                 side = jnp.concatenate([low, high], axis=1)
@@ -152,10 +152,12 @@
     return out.reshape(CHAN, OUT_ROWS, OUT_COLS)
 
 
-def lon_order():
+def lon_order(first, last):
     lon = lax.axis_index("lon")
-    columns = [lon, (lon + 6) % 8, (lon + 2) % 8, (lon + 4) % 8]
-    return columns + [c ^ 1 for c in columns]
+    columns = [lon, (lon + 6) % 8, (lon + 2) % 8, (lon + 4) % 8, (lon + 4) % 8]
+    half = (first + last) // 2
+    ranges = [(first, last), (first, last), (first, last), (first, half), (half, last)]
+    return [(c, *r) for c, r in zip(columns + [c ^ 1 for c in columns], ranges * 2)]
 
 
 def gather_lon(v):
@@ -165,13 +167,16 @@
     def across(u):
         return lax.ppermute(u, "lon", [(i, i ^ 1) for i in range(8)])
 
-    pieces = [v, along(v, 1), along(v, -1), along(v, 2)]
+    half = v.shape[1] // 2
+    right, left = along(v, 1), along(v, -1)
+    far = [along(right[:, :half], 1), along(left[:, half:], -1)]
+    pieces = [v, right, left] + far
     return pieces + [across(u) for u in pieces]
 
 
 def local(coarse_field, forward_table, degree_mixing_weight, synthesis_weight_table):
     ftab = jnp.pad(forward_table, ((0, SLOTS - OWN), (0, 0), (0, 0)))
-    ftab = ftab.reshape(LATS, EACH, ROWS, 720)
+    ftab = ftab.reshape(LATS, EACH * ROWS, 720)
     ftab, coarse_field = lax.optimization_barrier((ftab, coarse_field))
     ftab = swap(ftab, "lat")
 
@@ -189,9 +194,10 @@
     spectrum, ftab, wtab, lon = lax.optimization_barrier((spectrum, ftab, wtab, lon))
     spectrum = lax.psum_scatter(spectrum, "lon", scatter_dimension=0)
     wtab = swap(wtab, "lat")
-    spectrum, wtab, lon = lax.optimization_barrier((spectrum, wtab, lon))
+    ftab = ftab.reshape(LATS, EACH, ROWS, 720)
     spectrum = spectrum.reshape(ROWS, 2, LATS, EACH, CHAN)
     spectrum = jnp.transpose(spectrum, (2, 3, 1, 0, 4))
+    spectrum, wtab, lon = lax.optimization_barrier((spectrum, wtab, lon))
     spectrum = swap(spectrum, "lat")
     spectrum = jnp.transpose(spectrum, (1, 0, 3, 2, 4)).reshape(EACH, 720, 2 * CHAN)
 
@@ -200,7 +206,7 @@
 
     ids, turns, real = [], [], []
     orders = [(column, 0, SPLIT) for column in range(LONS)]
-    orders += [(column, SPLIT, 2 * SLOTS) for column in lon_order()]
+    orders += lon_order(SPLIT, 2 * SLOTS)
     for column, first, last in orders:
         line = jnp.arange(first, last, dtype=jnp.int32)
         ids.append(column * OWN + jnp.minimum(line // 2, OWN - 1))

time: 294 us -> 288 us (0.980)
  waiting for transfers between devices: 125 us -> 112 us
  local copies, waits for them, and re-layouts: 21.8 us -> 27.4 us
    all_to_all x4, waiting for transfers between devices: 102 us -> 43.7 us  [swap(): return lax.all_to_all(x, axis, split_axis=0, concat_axis=0, tiled=True)]
    reduce_scatter x1, waiting for transfers between devices: 0.01 us -> 49.6 us  [local(): spectrum = lax.psum_scatter(spectrum, 'lon', scatter_dimension=0)]
    optimization_barrier x0 -> x1, local copies, waits for them, and re-layouts: none -> 4.31 us  [local(): lax.optimization_barrier((spectrum, ftab, wtab, lon))]
    all_gather x1, waiting for transfers between devices: 21.5 us -> 17.6 us  [local(): pieces = [lax.all_gather(rows, 'lon', axis=0)] + gather_lon(rest)]
    reshape x0 -> x1, local copies, waits for them, and re-layouts: none -> 2.96 us  [local(): ftab = ftab.reshape(LATS, EACH * ROWS, 720)]
    ppermute x4 -> x5, starting transfers between devices: 23.1 us -> 25.7 us  [across(): return lax.ppermute(u, 'lon', [(i, i ^ 1) for i in range(8)])]
    unnamed x23 -> x27, local copies, waits for them, and re-layouts: 6.52 us -> 6.55 us
  transfers between devices with their start and end apart: 13 -> 15, of which waited for: 6 -> 8; matrix products, arithmetic and copies ran while one was open for 6% -> 8% of each run, Pallas kernels for 1% -> 1%
where the time goes in v5:
time: 288 us; the launch traced here: 287 us
  waiting for transfers between devices  112 us (39%)
  starting transfers between devices  62.7 us (22%)
  blocking collectives  31.4 us (11%)
  local copies, waits for them, and re-layouts  27.4 us (10%)
  Pallas kernels  21.1 us (7%)
  between operations  13.8 us (5%)
  other arithmetic  12.3 us (4%)
  matrix products  6.17 us (2%)
    reduce_scatter x1, waiting for transfers between devices, local(): spectrum = lax.psum_scatter(spectrum, 'lon', scatter_dimension=0)  49.6 us
    all_to_all x4, waiting for transfers between devices, swap(): return lax.all_to_all(x, axis, split_axis=0, concat_axis=0, tiled=True)  43.7 us
    all_to_all x2, blocking collectives, swap(): return lax.all_to_all(x, axis, split_axis=0, concat_axis=0, tiled=True)  31.4 us
    all_to_all x4, starting transfers between devices, swap(): return lax.all_to_all(x, axis, split_axis=0, concat_axis=0, tiled=True)  31.2 us
    ppermute x5, starting transfers between devices, across(): return lax.ppermute(u, 'lon', [(i, i ^ 1) for i in range(8)])  25.7 us
    all_gather x1, waiting for transfers between devices, local(): pieces = [lax.all_gather(rows, 'lon', axis=0)] + gather_lon(rest)  17.6 us
    convert_element_type x2, other arithmetic, waves(): return (jnp.cos(angles) * jnp.where(valid, factor, 0.0)).astype(BF)  10.2 us
    pallas_call x1, Pallas kernels, to_longitudes(): pl.pallas_call(output_kernel, grid=(HALF // STEP,), in_specs=[pl.BlockSpe...  9.46 us
  transfers between devices with their start and end apart: 15, of which 8 were waited for; matrix products, arithmetic and copies ran while one was open for 8% of the time, Pallas kernels for 1%

profile of v5, /device:TPU:1, one launch (start us, length us, event | category | flops | bytes accessed | tf_op | source)
XLA Modules:
  0.0 286.8 jit_solution(16665756726626163032)
XLA Ops:
  6.5 3.0 %copy.30 = bf16[46,45,720]{2,1,0:T(8,128)(2,1)S(1)} copy(bf16[46,45,720]{2,0,1:T(8,128)(2,1)} %param.5) | data formatting | bytes 5961600
  9.6 0.4 pad.8.clone
  10.0 3.0 %reshape.307 = bf16[16,135,720]{2,1,0:T(8,128)(2,1)} reshape(bf16[48,45,720]{2,1,0:T(8,128)(2,1)S(1)} %pad.8.clone) | data formatting | bytes 6220800 | tf_op jit(solution)/shard_map/reshape | solution.py:179
  12.9 8.6 %all-to-all-start = ((bf16[16,135,720]{2,1,0:T(8,128)(2,1)}), bf16[16,135,720]{2,1,0:T(8,128)(2,1)}, u32[]{:S(2)}, u32[]{:S(2)}) async-start(bf16[16,135,720]{2,1,0:T(8,128)(2,1)} %reshape.307), calls=%async_computation | async-start | bytes 6684672 | tf_op jit(solution)/shard_map/all_to_all | solution.py:39
  21.6 0.0 reduce-scatter.2.cloned.1.call-start
  21.6 0.0 copy-start.1
  21.6 5.4 %pad.9 = bf16[48,64,720]{2,1,0:T(8,128)(2,1)} pad(bf16[46,64,720]{2,1,0:T(8,128)(2,1)} %bitcast.24, bf16[]{:T(256)} %constant.294.clone.1), padding=0_2x0_0x0_0 | pad | bytes 8663042 | tf_op jit(solution)/shard_map/jit(_pad)/pad | solution.py:193
  27.1 3.8 %fusion.33.waves_in = bf16[768,180]{1,0:T(8,128)(2,1)S(1)} fusion(f32[768]{0:T(1024)S(1)} %fusion.52, s32[768]{0:T(1024)S(1)} %get-tuple-element.33, s32[180]{0:T(256)S(1)} %iota_add_fusion.1, s32[768]{0:T(1024)S(1)} %get-tuple-element.34), kind=kLoop, calls=%fused_computation.29 | loop fusion | flops 1658880 | bytes 286416 | tf_op jit(solution)/shard_map/convert_element_type | solution.py:35
  30.9 0.0 copy-done.1
  31.0 3.9 %shard_map.46 = bf16[8,45,96,96]{3,2,1,0:T(8,128)(2,1)S(1)} custom-call(bf16[768,180]{1,0:T(8,128)(2,1)S(1)} %fusion.33.waves_in, bf16[45,180,96]{2,1,0:T(8,128)(2,1)S(1)} %bitcast.18), custom_call_target="tpu_custom_call" | custom-call | tf_op jit(solution)/shard_map/pallas_call | solution.py:55
  34.9 3.5 %copy-done = bf16[8,45,96,96]{3,2,1,0:T(8,128)(2,1)} copy-done((bf16[8,45,96,96]{3,2,1,0:T(8,128)(2,1)}, bf16[8,45,96,96]{3,2,1,0:T(8,128)(2,1)S(1)}, u32[]{:S(2)}) %copy-start) | copy-done | bytes 6635544
  38.4 25.8 %all-to-all-done = bf16[16,135,720]{2,1,0:T(8,128)(2,1)} async-done(((bf16[16,135,720]{2,1,0:T(8,128)(2,1)}), bf16[16,135,720]{2,1,0:T(8,128)(2,1)}, u32[]{:S(2)}, u32[]{:S(2)}) %all-to-all-start) | async-done | bytes 3110432 | tf_op jit(solution)/shard_map/all_to_all | solution.py:39
  64.1 0.0 reduce-scatter.2.cloned.1.call-update
  64.2 10.2 %all-to-all-start.1 = ((bf16[16,3,64,720]{3,2,1,0:T(8,128)(2,1)}), bf16[16,3,64,720]{3,2,1,0:T(8,128)(2,1)}, u32[]{:S(2)}, u32[]{:S(2)}) async-start(bf16[16,3,64,720]{3,2,1,0:T(8,128)(2,1)} %bitcast.19), calls=%async_computation.2 | async-start | bytes 9437184 | tf_op jit(solution)/shard_map/all_to_all | solution.py:39
  74.5 0.1 concatenate.25
  74.6 0.1 concatenate.24
  74.7 49.6 %reduce-scatter.2.cloned.1.call-done = bf16[1,45,96,96]{3,2,1,0:T(8,128)(2,1)} async-done(((bf16[8,45,96,96]{3,2,1,0:T(8,128)(2,1)}), bf16[1,45,96,96]{3,2,1,0:T(8,128)(2,1)}) %reduce-scatter.2.cloned.1.call-update) | async-done | bytes 829456 | tf_op jit(solution)/shard_map/reduce_scatter | solution.py:195
  124.3 1.7 copy.18
  126.0 5.9 %all-to-all-done.1.table = bf16[16,3,64,720]{3,2,1,0:T(8,128)(2,1)} async-done(((bf16[16,3,64,720]{3,2,1,0:T(8,128)(2,1)}), bf16[16,3,64,720]{3,2,1,0:T(8,128)(2,1)}, u32[]{:S(2)}, u32[]{:S(2)}) %all-to-all-start.1) | async-done | bytes 4423712 | tf_op jit(solution)/shard_map/all_to_all | solution.py:39
  131.9 2.2 copy.19
  134.1 8.0 %all-to-all-start.2 = ((bf16[16,3,2,45,96]{4,2,3,1,0:T(2,128)(2,1)}), bf16[16,3,2,45,96]{4,2,3,1,0:T(2,128)(2,1)S(1)}, u32[]{:S(2)}, u32[]{:S(2)}) async-start(bf16[16,3,2,45,96]{4,2,3,1,0:T(2,128)(2,1)} %copy.19), calls=%async_computation.3 | async-start | bytes 2211840 | tf_op jit(solution)/shard_map/all_to_all | solution.py:39
  142.1 0.1 concatenate.23
  142.2 4.3 %copy.21 = bf16[16,135,720]{2,0,1:T(8,128)(2,1)} copy(bf16[16,135,720]{2,1,0:T(8,128)(2,1)} %all-to-all-done) | data formatting | bytes 6220800 | tf_op jit(solution)/shard_map/optimization_barrier | solution.py:194
  146.5 8.0 %all-to-all-done.2 = bf16[16,3,2,45,96]{4,2,3,1,0:T(2,128)(2,1)S(1)} async-done(((bf16[16,3,2,45,96]{4,2,3,1,0:T(2,128)(2,1)}), bf16[16,3,2,45,96]{4,2,3,1,0:T(2,128)(2,1)S(1)}, u32[]{:S(2)}, u32[]{:S(2)}) %all-to-all-start.2) | async-done | bytes 829472 | tf_op jit(solution)/shard_map/all_to_all | solution.py:39
  154.5 0.8 copy.20
  155.3 0.7 reshape.319
  156.0 3.2 %fusion.22 = bf16[16,3,45,192]{3,2,0,1:T(8,128)(2,1)S(1)} fusion(bf16[3,720,192,1]{2,1,3,0:T(8,128)(2,1)S(1)} %reshape.319, bf16[16,3,45,720]{3,0,2,1:T(8,128)(2,1)} %bitcast.26), kind=kOutput, calls=%fused_computation.20 | convolution fusion | flops 597611520 | bytes 4769280 | tf_op jit(solution)/shard_map/ajlq,jqn->ajln/dot_general | solution.py:204
  159.2 1.1 copy.24
  160.3 4.4 %all-to-all-start.3 = ((bf16[16,3,45,192]{3,2,1,0:T(8,128)(2,1)}), bf16[16,3,45,192]{3,2,1,0:T(8,128)(2,1)S(1)}, u32[]{:S(2)}, u32[]{:S(2)}) async-start(bf16[16,3,45,192]{3,2,1,0:T(8,128)(2,1)} %copy.24), calls=%async_computation.4 | async-start | bytes 2359296 | tf_op jit(solution)/shard_map/all_to_all | solution.py:39
  164.7 0.2 all-gather.3.cloned.1.call-start
  165.0 0.0 copy-done.3
  165.0 1.9 slice_negate_fusion
  166.9 6.4 %fusion.18.table = bf16[464,768]{1,0:T(8,128)(2,1)} fusion(f32[768]{0:T(1024)S(1)} %broadcast_select_fusion, s32[768]{0:T(1024)S(1)} %broadcast_multiply_fusion, s32[464]{0:T(512)S(1)} %iota_add_fusion, s32[768]{0:T(1024)S(1)} %concatenate.23), kind=kLoop, calls=%fused_computation.15 | loop fusion | flops 4276224 | bytes 723776 | tf_op jit(solution)/shard_map/convert_element_type | solution.py:35
  173.3 4.1 %all-to-all-done.3 = bf16[16,3,45,192]{3,2,1,0:T(8,128)(2,1)S(1)} async-done(((bf16[16,3,45,192]{3,2,1,0:T(8,128)(2,1)}), bf16[16,3,45,192]{3,2,1,0:T(8,128)(2,1)S(1)}, u32[]{:S(2)}, u32[]{:S(2)}) %all-to-all-start.3) | async-done | bytes 829472 | tf_op jit(solution)/shard_map/all_to_all | solution.py:39
  177.3 3.0 %fusion.25 = bf16[48,45,192]{2,0,1:T(8,128)(2,1)S(1)} fusion(bf16[45,96,96]{2,1,0:T(8,128)(2,1)} %get-tuple-element.32, bf16[45,96,96]{2,1,0:T(8,128)(2,1)} %get-tuple-element.31, bf16[45,96,192]{2,1,0:T(8,128)(2,1)S(1)} %copy-done.3, bf16[48,45,192]{2,1,0:T(8,128)(2,1)S(1)} %bitcast.27), kind=kOutput, calls=%fused_computation.21 | convolution fusion | flops 169620480 | bytes 4976640 | tf_op jit(solution)/shard_map/mlt,ltu->mlu/dot_general | solution.py:223
  180.3 0.4 copy.26
  180.7 15.8 %all_to_all.30 = bf16[16,3,45,192]{3,2,1,0:T(8,128)(2,1)S(1)} all-to-all(bf16[16,3,45,192]{3,2,1,0:T(8,128)(2,1)S(1)} %bitcast.22), channel_id=1, replica_groups=mesh['lat'=16,'lon'=8] {'lat'}, dimensions={0} | all-to-all | bytes 1658880 | tf_op jit(solution)/shard_map/all_to_all | solution.py:39
  196.5 0.1 copy.27
  196.6 0.6 reshape.313.mixed
  197.1 4.4 %shard_map.47 = bf16[16,288,128]{2,1,0:T(8,128)(2,1)S(1)} custom-call(bf16[3,720,192]{2,1,0:T(8,128)(2,1)S(1)} %reshape.313.mixed, bf16[16,3,64,720]{3,2,1,0:T(8,128)(2,1)} %all-to-all-done.1.table), custom_call_target="tpu_custom_call" | custom-call | flops 849346560 | bytes 6000000 | tf_op jit(solution)/shard_map/pallas_call | solution.py:84
  201.5 15.6 %all_to_all.31.rows = bf16[16,288,128]{2,1,0:T(8,128)(2,1)S(1)} all-to-all(bf16[16,288,128]{2,1,0:T(8,128)(2,1)S(1)} %shard_map.47), channel_id=1, replica_groups=mesh['lat'=16,'lon'=8] {'lat'}, dimensions={0} | all-to-all | bytes 2359296 | tf_op jit(solution)/shard_map/all_to_all | solution.py:39
  217.2 3.3 %shard_map.48 = (bf16[48,64,128]{2,1,0:T(8,128)(2,1)}, bf16[48,32,128]{2,1,0:T(8,128)(2,1)S(1)}) custom-call(bf16[16,288,128]{2,1,0:T(8,128)(2,1)S(1)} %all_to_all.31.rows), custom_call_target="tpu_custom_call" | custom-call | tf_op jit(solution)/shard_map/pallas_call | solution.py:107
  220.5 0.0 all-gather.3.cloned.1.call-update
  220.5 1.3 collective-permute-start
  221.8 1.5 collective-permute-start.1
  223.2 9.7 %collective-permute-start.4 = (bf16[48,32,128]{2,1,0:T(8,128)(2,1)S(1)}, bf16[48,32,128]{2,1,0:T(8,128)(2,1)S(1)}, u32[]{:S(2)}, u32[]{:S(2)}) collective-permute-start(bf16[48,32,128]{2,1,0:T(8,128)(2,1)S(1)} %get-tuple-element.30.refs_1_), channel_id=1, source_target_pairs={{0,1},{1,0},{2,3},{3,2},{4,5},{5,4},{6,7},{7,6},{8,9},{9,8},{10,11... | collective-permute-start | bytes 1179656 | tf_op jit(solution)/shard_map/ppermute | solution.py:168
  233.0 0.0 collective-permute-done.refs_2_
  233.0 0.1 collective-permute-start.2
  233.1 0.0 collective-permute-done.1.refs_3_
  233.1 2.7 collective-permute-start.3
  235.8 8.6 %collective-permute-start.5 = (bf16[48,32,128]{2,1,0:T(8,128)(2,1)S(1)}, bf16[48,32,128]{2,1,0:T(8,128)(2,1)S(1)}, u32[]{:S(2)}, u32[]{:S(2)}) collective-permute-start(bf16[48,32,128]{2,1,0:T(8,128)(2,1)S(1)} %collective-permute-done.refs_2_), channel_id=1, source_target_pairs={{0,1},{1,0},{2,3},{3,2},{4,5},{5,4},{6,7},{7,6},{8,9},{9,8},{10,11... | collective-permute-start | bytes 1179656 | tf_op jit(solution)/shard_map/ppermute | solution.py:168
  244.4 0.0 collective-permute-start.6
  244.4 0.0 collective-permute-done.2.refs_4_
  244.4 6.7 %collective-permute-start.7 = (bf16[48,16,128]{2,1,0:T(8,128)(2,1)S(1)}, bf16[48,16,128]{2,1,0:T(8,128)(2,1)S(1)}, u32[]{:S(2)}, u32[]{:S(2)}) collective-permute-start(bf16[48,16,128]{2,1,0:T(8,128)(2,1)S(1)} %collective-permute-done.2.refs_4_), channel_id=1, source_target_pairs={{0,1},{1,0},{2,3},{3,2},{4,5},{5,4},{6,7},{7,6},{8,9},{9,8},{10,11... | collective-permute-start | bytes 589832 | tf_op jit(solution)/shard_map/ppermute | solution.py:168
  251.1 0.0 collective-permute-done.3.refs_5_
  251.2 0.7 collective-permute-start.8
  251.8 0.0 collective-permute-done.4.refs_6_
  251.8 0.4 collective-permute-done.7.refs_9_
  252.2 0.7 collective-permute-done.8.refs_10_
  252.9 0.0 collective-permute-done.5.refs_7_
  252.9 0.0 collective-permute-done.6.refs_8_
  252.9 17.6 %all-gather.3.cloned.1.call-done = bf16[384,64,128]{2,1,0:T(8,128)(2,1)} async-done(((bf16[48,64,128]{2,1,0:T(8,128)(2,1)}), bf16[384,64,128]{2,1,0:T(8,128)(2,1)}) %all-gather.3.cloned.1.call-update) | async-done | bytes 6291472 | tf_op jit(solution)/shard_map/all_gather | solution.py:227
  270.5 0.0 copy-done.5
  270.6 9.5 %shard_map.49 = bf16[2,48,64,450]{3,2,1,0:T(8,128)(2,1)} custom-call(bf16[464,768]{1,0:T(8,128)(2,1)} %fusion.18.table, bf16[8,48,64,128]{3,2,1,0:T(8,128)(2,1)} %bitcast.20, bf16[48,32,128]{2,1,0:T(8,128)(2,1)} %copy-done.2, bf16[48,32,128]{2,1,0:T(8,128)(2,1)} %copy-done.4, bf16[48,32,128]{2,1,0:T(8,128)(2,1)} %copy-done.5, ...), custom_call_target="tpu_custom_call" | custom-call | tf_op jit(solution)/shard_map/pallas_call | solution.py:144
  (45 shorter events, 0.2 us)
Async XLA Ops:
  12.9 51.2 %all-to-all-start = ((bf16[16,135,720]{2,1,0:T(8,128)(2,1)}), bf16[16,135,720]{2,1,0:T(8,128)(2,1)}, u32[]{:S(2)}, u32[]{:S(2)}) async-start(bf16[16,135,720]{2,1,0:T(8,128)(2,1)} %reshape.307), calls=%async_computation | async-start | bytes 6684672 | tf_op jit(solution)/shard_map/all_to_all | solution.py:39
  21.6 102.7 %reduce-scatter.2.cloned.1.call-start = ((), (), s32[]{:S(2)}) async-start(), calls=%async_computation.7 | async-start | bytes 9953280 | tf_op jit(solution)/shard_map/reduce_scatter | solution.py:195
  21.6 9.3 %copy-start.1 = (bf16[96,45,180]{0,2,1:T(8,128)(2,1)S(1)}, bf16[96,45,180]{0,2,1:T(8,128)(2,1)}, u32[]{:S(2)}) copy-start(bf16[96,45,180]{0,2,1:T(8,128)(2,1)} %param.4) | copy-start | bytes 4665604
  34.9 3.5 %copy-start = (bf16[8,45,96,96]{3,2,1,0:T(8,128)(2,1)}, bf16[8,45,96,96]{3,2,1,0:T(8,128)(2,1)S(1)}, u32[]{:S(2)}) copy-start(bf16[8,45,96,96]{3,2,1,0:T(8,128)(2,1)S(1)} %shard_map.46) | copy-start | bytes 19906564
  64.2 67.7 %all-to-all-start.1 = ((bf16[16,3,64,720]{3,2,1,0:T(8,128)(2,1)}), bf16[16,3,64,720]{3,2,1,0:T(8,128)(2,1)}, u32[]{:S(2)}, u32[]{:S(2)}) async-start(bf16[16,3,64,720]{3,2,1,0:T(8,128)(2,1)} %bitcast.19), calls=%async_computation.2 | async-start | bytes 9437184 | tf_op jit(solution)/shard_map/all_to_all | solution.py:39
  134.1 20.4 %all-to-all-start.2 = ((bf16[16,3,2,45,96]{4,2,3,1,0:T(2,128)(2,1)}), bf16[16,3,2,45,96]{4,2,3,1,0:T(2,128)(2,1)S(1)}, u32[]{:S(2)}, u32[]{:S(2)}) async-start(bf16[16,3,2,45,96]{4,2,3,1,0:T(2,128)(2,1)} %copy.19), calls=%async_computation.3 | async-start | bytes 2211840 | tf_op jit(solution)/shard_map/all_to_all | solution.py:39
  160.3 4.7 %copy-start.3 = (bf16[45,96,192]{2,1,0:T(8,128)(2,1)S(1)}, bf16[45,96,192]{2,1,0:T(8,128)(2,1)}, u32[]{:S(2)}) copy-start(bf16[45,96,192]{2,1,0:T(8,128)(2,1)} %param.6) | copy-start | bytes 4976644
  160.3 17.0 %all-to-all-start.3 = ((bf16[16,3,45,192]{3,2,1,0:T(8,128)(2,1)}), bf16[16,3,45,192]{3,2,1,0:T(8,128)(2,1)S(1)}, u32[]{:S(2)}, u32[]{:S(2)}) async-start(bf16[16,3,45,192]{3,2,1,0:T(8,128)(2,1)} %copy.24), calls=%async_computation.4 | async-start | bytes 2359296 | tf_op jit(solution)/shard_map/all_to_all | solution.py:39
  164.7 105.8 %all-gather.3.cloned.1.call-start = ((), (), s32[]{:S(2)}) async-start(), calls=%async_computation.8 | async-start | bytes 7077888 | tf_op jit(solution)/shard_map/all_gather | solution.py:227
  220.5 50.0 %copy-start.2 = (bf16[48,32,128]{2,1,0:T(8,128)(2,1)}, bf16[48,32,128]{2,1,0:T(8,128)(2,1)S(1)}, u32[]{:S(2)}) copy-start(bf16[48,32,128]{2,1,0:T(8,128)(2,1)S(1)} %get-tuple-element.30.refs_1_) | copy-start | bytes 1179652
  220.5 12.5 %collective-permute-start = (bf16[48,32,128]{2,1,0:T(8,128)(2,1)S(1)}, bf16[48,32,128]{2,1,0:T(8,128)(2,1)S(1)}, u32[]{:S(2)}, u32[]{:S(2)}) collective-permute-start(bf16[48,32,128]{2,1,0:T(8,128)(2,1)S(1)} %get-tuple-element.30.refs_1_), channel_id=1, source_target_pairs={{0,2},{1,3},{2,4},{3,5},{4,6},{5,7},{6,0},{7,1},{8,10},{9,11},{10,... | collective-permute-start | bytes 1179656 | tf_op jit(solution)/shard_map/ppermute | solution.py:165
  221.8 11.3 %collective-permute-start.1 = (bf16[48,32,128]{2,1,0:T(8,128)(2,1)S(1)}, bf16[48,32,128]{2,1,0:T(8,128)(2,1)S(1)}, u32[]{:S(2)}, u32[]{:S(2)}) collective-permute-start(bf16[48,32,128]{2,1,0:T(8,128)(2,1)S(1)} %get-tuple-element.30.refs_1_), channel_id=1, source_target_pairs={{0,6},{1,7},{2,0},{3,1},{4,2},{5,3},{6,4},{7,5},{8,14},{9,15},{10,... | collective-permute-start | bytes 1179656 | tf_op jit(solution)/shard_map/ppermute | solution.py:165
  223.2 28.6 %collective-permute-start.4 = (bf16[48,32,128]{2,1,0:T(8,128)(2,1)S(1)}, bf16[48,32,128]{2,1,0:T(8,128)(2,1)S(1)}, u32[]{:S(2)}, u32[]{:S(2)}) collective-permute-start(bf16[48,32,128]{2,1,0:T(8,128)(2,1)S(1)} %get-tuple-element.30.refs_1_), channel_id=1, source_target_pairs={{0,1},{1,0},{2,3},{3,2},{4,5},{5,4},{6,7},{7,6},{8,9},{9,8},{10,11... | collective-permute-start | bytes 1179656 | tf_op jit(solution)/shard_map/ppermute | solution.py:168
  233.0 37.5 %copy-start.4 = (bf16[48,32,128]{2,1,0:T(8,128)(2,1)}, bf16[48,32,128]{2,1,0:T(8,128)(2,1)S(1)}, u32[]{:S(2)}) copy-start(bf16[48,32,128]{2,1,0:T(8,128)(2,1)S(1)} %collective-permute-done.refs_2_) | copy-start | bytes 1179652
  233.0 11.4 %collective-permute-start.2 = (bf16[48,16,128]{2,1,0:T(8,128)(2,1)S(1)}, bf16[48,16,128]{2,1,0:T(8,128)(2,1)S(1)}, u32[]{:S(2)}, u32[]{:S(2)}) collective-permute-start(bf16[48,16,128]{2,1,0:T(8,128)(2,1)S(1)} %slice.16), channel_id=1, source_target_pairs={{0,2},{1,3},{2,4},{3,5},{4,6},{5,7},{6,0},{7,1},{8,10},{9,11},{10,... | collective-permute-start | bytes 589832 | tf_op jit(solution)/shard_map/ppermute | solution.py:165
  233.1 37.4 %copy-start.5 = (bf16[48,32,128]{2,1,0:T(8,128)(2,1)}, bf16[48,32,128]{2,1,0:T(8,128)(2,1)S(1)}, u32[]{:S(2)}) copy-start(bf16[48,32,128]{2,1,0:T(8,128)(2,1)S(1)} %collective-permute-done.1.refs_3_) | copy-start | bytes 1179652
  233.1 18.0 %collective-permute-start.3 = (bf16[48,16,128]{2,1,0:T(8,128)(2,1)S(1)}, bf16[48,16,128]{2,1,0:T(8,128)(2,1)S(1)}, u32[]{:S(2)}, u32[]{:S(2)}) collective-permute-start(bf16[48,16,128]{2,1,0:T(8,128)(2,1)S(1)} %slice.17), channel_id=1, source_target_pairs={{0,6},{1,7},{2,0},{3,1},{4,2},{5,3},{6,4},{7,5},{8,14},{9,15},{10,... | collective-permute-start | bytes 589832 | tf_op jit(solution)/shard_map/ppermute | solution.py:165
  235.8 17.1 %collective-permute-start.5 = (bf16[48,32,128]{2,1,0:T(8,128)(2,1)S(1)}, bf16[48,32,128]{2,1,0:T(8,128)(2,1)S(1)}, u32[]{:S(2)}, u32[]{:S(2)}) collective-permute-start(bf16[48,32,128]{2,1,0:T(8,128)(2,1)S(1)} %collective-permute-done.refs_2_), channel_id=1, source_target_pairs={{0,1},{1,0},{2,3},{3,2},{4,5},{5,4},{6,7},{7,6},{8,9},{9,8},{10,11... | collective-permute-start | bytes 1179656 | tf_op jit(solution)/shard_map/ppermute | solution.py:168
  244.4 8.5 %collective-permute-start.6 = (bf16[48,32,128]{2,1,0:T(8,128)(2,1)S(1)}, bf16[48,32,128]{2,1,0:T(8,128)(2,1)S(1)}, u32[]{:S(2)}, u32[]{:S(2)}) collective-permute-start(bf16[48,32,128]{2,1,0:T(8,128)(2,1)S(1)} %collective-permute-done.1.refs_3_), channel_id=1, source_target_pairs={{0,1},{1,0},{2,3},{3,2},{4,5},{5,4},{6,7},{7,6},{8,9},{9,8},{10,11... | collective-permute-start | bytes 1179656 | tf_op jit(solution)/shard_map/ppermute | solution.py:168
  244.4 26.1 %copy-start.9 = (bf16[48,16,128]{2,1,0:T(8,128)(2,1)}, bf16[48,16,128]{2,1,0:T(8,128)(2,1)S(1)}, u32[]{:S(2)}) copy-start(bf16[48,16,128]{2,1,0:T(8,128)(2,1)S(1)} %collective-permute-done.2.refs_4_) | copy-start | bytes 589828
  244.4 7.8 %collective-permute-start.7 = (bf16[48,16,128]{2,1,0:T(8,128)(2,1)S(1)}, bf16[48,16,128]{2,1,0:T(8,128)(2,1)S(1)}, u32[]{:S(2)}, u32[]{:S(2)}) collective-permute-start(bf16[48,16,128]{2,1,0:T(8,128)(2,1)S(1)} %collective-permute-done.2.refs_4_), channel_id=1, source_target_pairs={{0,1},{1,0},{2,3},{3,2},{4,5},{5,4},{6,7},{7,6},{8,9},{9,8},{10,11... | collective-permute-start | bytes 589832 | tf_op jit(solution)/shard_map/ppermute | solution.py:168
  251.2 19.3 %copy-start.10 = (bf16[48,16,128]{2,1,0:T(8,128)(2,1)}, bf16[48,16,128]{2,1,0:T(8,128)(2,1)S(1)}, u32[]{:S(2)}) copy-start(bf16[48,16,128]{2,1,0:T(8,128)(2,1)S(1)} %collective-permute-done.3.refs_5_) | copy-start | bytes 589828
  251.2 1.7 collective-permute-start.8
  251.8 18.7 %copy-start.6 = (bf16[48,32,128]{2,1,0:T(8,128)(2,1)}, bf16[48,32,128]{2,1,0:T(8,128)(2,1)S(1)}, u32[]{:S(2)}) copy-start(bf16[48,32,128]{2,1,0:T(8,128)(2,1)S(1)} %collective-permute-done.4.refs_6_) | copy-start | bytes 1179652
  252.2 18.3 %copy-start.11 = (bf16[48,16,128]{2,1,0:T(8,128)(2,1)}, bf16[48,16,128]{2,1,0:T(8,128)(2,1)S(1)}, u32[]{:S(2)}) copy-start(bf16[48,16,128]{2,1,0:T(8,128)(2,1)S(1)} %collective-permute-done.7.refs_9_) | copy-start | bytes 589828
  252.9 17.6 %copy-start.12 = (bf16[48,16,128]{2,1,0:T(8,128)(2,1)}, bf16[48,16,128]{2,1,0:T(8,128)(2,1)S(1)}, u32[]{:S(2)}) copy-start(bf16[48,16,128]{2,1,0:T(8,128)(2,1)S(1)} %collective-permute-done.8.refs_10_) | copy-start | bytes 589828
  252.9 17.7 %copy-start.7 = (bf16[48,32,128]{2,1,0:T(8,128)(2,1)}, bf16[48,32,128]{2,1,0:T(8,128)(2,1)S(1)}, u32[]{:S(2)}) copy-start(bf16[48,32,128]{2,1,0:T(8,128)(2,1)S(1)} %collective-permute-done.5.refs_7_) | copy-start | bytes 1179652
  252.9 17.7 %copy-start.8 = (bf16[48,32,128]{2,1,0:T(8,128)(2,1)}, bf16[48,32,128]{2,1,0:T(8,128)(2,1)S(1)}, u32[]{:S(2)}) copy-start(bf16[48,32,128]{2,1,0:T(8,128)(2,1)S(1)} %collective-permute-done.6.refs_8_) | copy-start | bytes 1179652
Sparse Core Ops, SparseCore 0:
  64.3 59.9 reduce-scatter.1
  220.6 49.8 all-gather.2

commit v6 on v5

--- a/solution.py
+++ b/solution.py
@@ -24,6 +24,7 @@
 OUT_COLS = 450
 WIDE = 464
 LANES = 128
+PAIRED, EIGHTS, PACKED = 960, 1056, 1088
 STEP = 16
 MIB = 1024 * 1024
 BF = jnp.bfloat16
@@ -65,11 +66,64 @@
     )(waves_in, field)
 
 
+def packing_kernel(*refs):
+    out = refs[-1]
+    ends = []
+    for k, table in enumerate(refs[:-1]):
+        for t in range(5):
+            at = (5 * k + t) * OUT_ROWS
+            out[0, at : at + OUT_ROWS] = table[0, :, t * LANES : (t + 1) * LANES]
+        rest = table[0, :, 640:704]
+        at = PAIRED + k * 32
+        out[0, at : at + 32] = jnp.concatenate([rest[:32], rest[32:]], axis=1)
+        rest = table[0, :, 704:].astype(jnp.float32)
+        ends.append(jnp.concatenate([rest[8 * g : 8 * g + 8] for g in range(8)], axis=1))
+    ends.append(jnp.zeros((8, LANES), jnp.float32))
+    out[0, EIGHTS:] = jnp.concatenate(ends, axis=0).astype(BF)
+
+    @pl.when(pl.program_id(0) == LATS - 1)
+    def _():
+        for k in range(OWN - (LATS - 1) * EACH, EACH):
+            out[0, 5 * k * OUT_ROWS : 5 * (k + 1) * OUT_ROWS] = jnp.zeros((5 * OUT_ROWS, LANES), BF)
+            out[0, PAIRED + k * 32 : PAIRED + (k + 1) * 32] = jnp.zeros((32, LANES), BF)
+        there = lax.broadcasted_iota(jnp.int32, (32, LANES), 0) < 8 * (OWN - (LATS - 1) * EACH)
+        last = jnp.where(there, jnp.concatenate(ends, axis=0), 0.0)
+        out[0, EIGHTS:] = last.astype(BF)
+
+
+def pack(table):
+    def spec(k):
+        return pl.BlockSpec(
+            (1, OUT_ROWS, 720), lambda a: (jnp.minimum(a * EACH + k, OWN - 1), 0, 0)
+        )
+
+    return pl.pallas_call(
+        packing_kernel,
+        grid=(LATS,),
+        in_specs=[spec(k) for k in range(EACH)],
+        out_specs=pl.BlockSpec((1, PACKED, LANES), lambda a: (a, 0, 0)),
+        out_shape=jax.ShapeDtypeStruct((LATS, PACKED, LANES), BF),
+        compiler_params=pltpu.CompilerParams(vmem_limit_bytes=10 * MIB),
+    )(*[table] * EACH)
+
+
+def unpack(table, k):
+    parts = []
+    for t in range(5):
+        at = (5 * k + t) * OUT_ROWS
+        parts.append(table[:, at : at + OUT_ROWS].reshape(LATS * OUT_ROWS, LANES))
+    pairs = table[:, PAIRED + k * 32 : PAIRED + (k + 1) * 32]
+    pairs = jnp.concatenate([pairs[:, :, :64], pairs[:, :, 64:]], axis=1)
+    ends = table[:, EIGHTS:].astype(jnp.float32)[:, 8 * k : 8 * k + 8]
+    ends = jnp.concatenate([ends[:, :, 16 * g : 16 * g + 16] for g in range(8)], axis=1)
+    ends = ends.reshape(LATS * OUT_ROWS, 16).astype(BF)
+    return jnp.concatenate(parts + [pairs.reshape(LATS * OUT_ROWS, 64), ends], axis=1)
+
+
 def synthesis_kernel(mixed, table, rows, lines):
     made = []
     for k in range(EACH):
-        t = table[:, k].reshape(LATS * OUT_ROWS, 720)
-        made.append(jnp.dot(t, mixed[k], preferred_element_type=jnp.float32))
+        made.append(jnp.dot(unpack(table, k), mixed[k], preferred_element_type=jnp.float32))
     for b in range(LATS):
         for k in range(EACH):
             one = made[k][b * OUT_ROWS : (b + 1) * OUT_ROWS].astype(BF).T.astype(jnp.float32)
@@ -85,7 +139,7 @@
         synthesis_kernel,
         out_shape=jax.ShapeDtypeStruct((LATS, HALF * LINES, LANES), BF),
         scratch_shapes=[pltpu.VMEM((HALF * LINES, LANES), jnp.float32)],
-        compiler_params=pltpu.CompilerParams(vmem_limit_bytes=20 * MIB),
+        compiler_params=pltpu.CompilerParams(vmem_limit_bytes=32 * MIB),
         cost_estimate=pl.CostEstimate(
             flops=2 * EACH * 1024 * 720 * 192, bytes_accessed=6000000, transcendentals=0
         ),
@@ -189,8 +243,7 @@
     waves_in = waves(ids, row // (SLOTS * LONS), slot < OWN, points, LON_IN, factor)
     spectrum = shares(waves_in, jnp.transpose(coarse_field, (1, 2, 0)))
 
-    wtab = jnp.transpose(synthesis_weight_table, (0, 2, 1))
-    wtab = jnp.pad(wtab, ((0, SLOTS - OWN), (0, 0), (0, 0))).reshape(LATS, EACH, OUT_ROWS, 720)
+    wtab = pack(jnp.transpose(synthesis_weight_table, (0, 2, 1)))
     spectrum, ftab, wtab, lon = lax.optimization_barrier((spectrum, ftab, wtab, lon))
     spectrum = lax.psum_scatter(spectrum, "lon", scatter_dimension=0)
     wtab = swap(wtab, "lat")

time: 288 us -> 283 us (0.983)
  waiting for transfers between devices: 112 us -> 108 us
    pad x1 -> x0, local copies, waits for them, and re-layouts: 5.43 us -> none  [local(): jnp.pad(wtab, ((0, SLOTS - OWN), (0, 0), (0, 0)))]
    unnamed x27 -> x31, local copies, waits for them, and re-layouts: 6.55 us -> 10.9 us
    all_to_all x4, waiting for transfers between devices: 43.7 us -> 39.7 us  [swap(): return lax.all_to_all(x, axis, split_axis=0, concat_axis=0, tiled=True)]
  transfers between devices with their start and end apart: 15 -> 15, of which waited for: 8 -> 8; matrix products, arithmetic and copies ran while one was open for 8% -> 7% of each run, Pallas kernels for 1% -> 2%
where the time goes in v6:
time: 283 us; the launch traced here: 282 us
  waiting for transfers between devices  108 us (38%)
  starting transfers between devices  61 us (22%)
  blocking collectives  31 us (11%)
  local copies, waits for them, and re-layouts  26.4 us (9%)
  Pallas kernels  23.4 us (8%)
  between operations  13.8 us (5%)
  other arithmetic  12.3 us (4%)
  matrix products  6.17 us (2%)
    reduce_scatter x1, waiting for transfers between devices, local(): spectrum = lax.psum_scatter(spectrum, 'lon', scatter_dimension=0)  49.6 us
    all_to_all x4, waiting for transfers between devices, swap(): return lax.all_to_all(x, axis, split_axis=0, concat_axis=0, tiled=True)  39.7 us
    all_to_all x2, blocking collectives, swap(): return lax.all_to_all(x, axis, split_axis=0, concat_axis=0, tiled=True)  31 us
    all_to_all x4, starting transfers between devices, swap(): return lax.all_to_all(x, axis, split_axis=0, concat_axis=0, tiled=True)  28.9 us
    ppermute x5, starting transfers between devices, across(): return lax.ppermute(u, 'lon', [(i, i ^ 1) for i in range(8)])  26.3 us
    all_gather x1, waiting for transfers between devices, local(): pieces = [lax.all_gather(rows, 'lon', axis=0)] + gather_lon(rest)  17.6 us
    unnamed x31, local copies, waits for them, and re-layouts  10.9 us
    convert_element_type x2, other arithmetic, waves(): return (jnp.cos(angles) * jnp.where(valid, factor, 0.0)).astype(BF)  10.2 us
  transfers between devices with their start and end apart: 15, of which 8 were waited for; matrix products, arithmetic and copies ran while one was open for 7% of the time, Pallas kernels for 2%

profile of v6, /device:TPU:1, one launch (start us, length us, event | category | flops | bytes accessed | tf_op | source)
XLA Modules:
  0.0 282.0 jit_solution(3556332689822474132)
XLA Ops:
  6.5 3.0 %copy.30 = bf16[46,45,720]{2,1,0:T(8,128)(2,1)S(1)} copy(bf16[46,45,720]{2,0,1:T(8,128)(2,1)} %param.5) | data formatting | bytes 5961600
  9.6 0.4 pad.4.clone
  10.0 3.0 %reshape.304 = bf16[16,135,720]{2,1,0:T(8,128)(2,1)} reshape(bf16[48,45,720]{2,1,0:T(8,128)(2,1)S(1)} %pad.4.clone) | data formatting | bytes 6220800 | tf_op jit(solution)/shard_map/reshape | solution.py:233
  12.9 8.6 %all-to-all-start = ((bf16[16,135,720]{2,1,0:T(8,128)(2,1)}), bf16[16,135,720]{2,1,0:T(8,128)(2,1)}, u32[]{:S(2)}, u32[]{:S(2)}) async-start(bf16[16,135,720]{2,1,0:T(8,128)(2,1)} %reshape.304), calls=%async_computation | async-start | bytes 6684672 | tf_op jit(solution)/shard_map/all_to_all | solution.py:40
  21.6 0.0 reduce-scatter.2.cloned.1.call-start
  21.6 0.0 copy-start
  21.6 2.3 copy-done
  23.9 2.3 shard_map.47
  26.2 0.0 copy-start.2
  26.2 2.1 copy-done.2
  28.3 3.8 %fusion.33.waves_in = bf16[768,180]{1,0:T(8,128)(2,1)S(1)} fusion(f32[768]{0:T(1024)S(1)} %fusion.52, s32[768]{0:T(1024)S(1)} %get-tuple-element.33, s32[180]{0:T(256)S(1)} %iota_add_fusion.1, s32[768]{0:T(1024)S(1)} %get-tuple-element.34), kind=kLoop, calls=%fused_computation.29 | loop fusion | flops 1658880 | bytes 286416 | tf_op jit(solution)/shard_map/convert_element_type | solution.py:36
  32.2 3.9 %shard_map.46 = bf16[8,45,96,96]{3,2,1,0:T(8,128)(2,1)S(1)} custom-call(bf16[768,180]{1,0:T(8,128)(2,1)S(1)} %fusion.33.waves_in, bf16[45,180,96]{2,1,0:T(8,128)(2,1)S(1)} %bitcast.20), custom_call_target="tpu_custom_call" | custom-call | tf_op jit(solution)/shard_map/pallas_call | solution.py:56
  36.1 3.5 %copy-done.1 = bf16[8,45,96,96]{3,2,1,0:T(8,128)(2,1)} copy-done((bf16[8,45,96,96]{3,2,1,0:T(8,128)(2,1)}, bf16[8,45,96,96]{3,2,1,0:T(8,128)(2,1)S(1)}, u32[]{:S(2)}) %copy-start.1) | copy-done | bytes 6635544
  39.6 24.5 %all-to-all-done = bf16[16,135,720]{2,1,0:T(8,128)(2,1)} async-done(((bf16[16,135,720]{2,1,0:T(8,128)(2,1)}), bf16[16,135,720]{2,1,0:T(8,128)(2,1)}, u32[]{:S(2)}, u32[]{:S(2)}) %all-to-all-start) | async-done | bytes 3110432 | tf_op jit(solution)/shard_map/all_to_all | solution.py:40
  64.2 0.0 reduce-scatter.2.cloned.1.call-update
  64.2 10.2 %all-to-all-start.1 = ((bf16[16,1088,128]{2,1,0:T(8,128)(2,1)}), bf16[16,1088,128]{2,1,0:T(8,128)(2,1)}, u32[]{:S(2)}, u32[]{:S(2)}) async-start(bf16[16,1088,128]{2,1,0:T(8,128)(2,1)} %copy-done.2), calls=%async_computation.2 | async-start | bytes 8912896 | tf_op jit(solution)/shard_map/all_to_all | solution.py:40
  74.5 0.1 concatenate.25
  74.6 0.1 concatenate.24
  74.8 49.6 %reduce-scatter.2.cloned.1.call-done = bf16[1,45,96,96]{3,2,1,0:T(8,128)(2,1)} async-done(((bf16[8,45,96,96]{3,2,1,0:T(8,128)(2,1)}), bf16[1,45,96,96]{3,2,1,0:T(8,128)(2,1)}) %reduce-scatter.2.cloned.1.call-update) | async-done | bytes 829456 | tf_op jit(solution)/shard_map/reduce_scatter | solution.py:248
  124.3 1.7 copy.18
  126.0 3.2 %all-to-all-done.1.table = bf16[16,1088,128]{2,1,0:T(8,128)(2,1)} async-done(((bf16[16,1088,128]{2,1,0:T(8,128)(2,1)}), bf16[16,1088,128]{2,1,0:T(8,128)(2,1)}, u32[]{:S(2)}, u32[]{:S(2)}) %all-to-all-start.1) | async-done | bytes 4456480 | tf_op jit(solution)/shard_map/all_to_all | solution.py:40
  129.2 2.2 copy.19
  131.4 5.9 %all-to-all-start.2 = ((bf16[16,3,2,45,96]{4,2,3,1,0:T(2,128)(2,1)}), bf16[16,3,2,45,96]{4,2,3,1,0:T(2,128)(2,1)S(1)}, u32[]{:S(2)}, u32[]{:S(2)}) async-start(bf16[16,3,2,45,96]{4,2,3,1,0:T(2,128)(2,1)} %copy.19), calls=%async_computation.3 | async-start | bytes 2211840 | tf_op jit(solution)/shard_map/all_to_all | solution.py:40
  137.4 0.1 concatenate.23
  137.5 4.3 %copy.21 = bf16[16,135,720]{2,0,1:T(8,128)(2,1)} copy(bf16[16,135,720]{2,1,0:T(8,128)(2,1)} %all-to-all-done) | data formatting | bytes 6220800 | tf_op jit(solution)/shard_map/optimization_barrier | solution.py:247
  141.8 7.9 %all-to-all-done.2 = bf16[16,3,2,45,96]{4,2,3,1,0:T(2,128)(2,1)S(1)} async-done(((bf16[16,3,2,45,96]{4,2,3,1,0:T(2,128)(2,1)}), bf16[16,3,2,45,96]{4,2,3,1,0:T(2,128)(2,1)S(1)}, u32[]{:S(2)}, u32[]{:S(2)}) %all-to-all-start.2) | async-done | bytes 829472 | tf_op jit(solution)/shard_map/all_to_all | solution.py:40
  149.6 0.8 copy.20
  150.4 0.7 reshape.315
  151.2 3.2 %fusion.22 = bf16[16,3,45,192]{3,2,0,1:T(8,128)(2,1)S(1)} fusion(bf16[3,720,192,1]{2,1,3,0:T(8,128)(2,1)S(1)} %reshape.315, bf16[16,3,45,720]{3,0,2,1:T(8,128)(2,1)} %bitcast.26), kind=kOutput, calls=%fused_computation.20 | convolution fusion | flops 597611520 | bytes 4769280 | tf_op jit(solution)/shard_map/ajlq,jqn->ajln/dot_general | solution.py:257
  154.4 1.1 copy.24
  155.5 4.1 %all-to-all-start.3 = ((bf16[16,3,45,192]{3,2,1,0:T(8,128)(2,1)}), bf16[16,3,45,192]{3,2,1,0:T(8,128)(2,1)S(1)}, u32[]{:S(2)}, u32[]{:S(2)}) async-start(bf16[16,3,45,192]{3,2,1,0:T(8,128)(2,1)} %copy.24), calls=%async_computation.4 | async-start | bytes 2359296 | tf_op jit(solution)/shard_map/all_to_all | solution.py:40
  159.6 0.2 all-gather.3.cloned.1.call-start
  159.8 1.9 slice_negate_fusion
  161.7 6.4 %fusion.18.table = bf16[464,768]{1,0:T(8,128)(2,1)} fusion(f32[768]{0:T(1024)S(1)} %broadcast_select_fusion, s32[768]{0:T(1024)S(1)} %broadcast_multiply_fusion, s32[464]{0:T(512)S(1)} %iota_add_fusion, s32[768]{0:T(1024)S(1)} %concatenate.23), kind=kLoop, calls=%fused_computation.15 | loop fusion | flops 4276224 | bytes 723776 | tf_op jit(solution)/shard_map/convert_element_type | solution.py:36
  168.1 4.1 %all-to-all-done.3 = bf16[16,3,45,192]{3,2,1,0:T(8,128)(2,1)S(1)} async-done(((bf16[16,3,45,192]{3,2,1,0:T(8,128)(2,1)}), bf16[16,3,45,192]{3,2,1,0:T(8,128)(2,1)S(1)}, u32[]{:S(2)}, u32[]{:S(2)}) %all-to-all-start.3) | async-done | bytes 829472 | tf_op jit(solution)/shard_map/all_to_all | solution.py:40
  172.2 3.0 %fusion.25 = bf16[48,45,192]{2,0,1:T(8,128)(2,1)S(1)} fusion(bf16[45,96,96]{2,1,0:T(8,128)(2,1)} %get-tuple-element.32, bf16[45,96,96]{2,1,0:T(8,128)(2,1)} %get-tuple-element.31, bf16[45,96,192]{2,1,0:T(8,128)(2,1)S(1)} %copy-done.5, bf16[48,45,192]{2,1,0:T(8,128)(2,1)S(1)} %bitcast.27), kind=kOutput, calls=%fused_computation.21 | convolution fusion | flops 169620480 | bytes 4976640 | tf_op jit(solution)/shard_map/mlt,ltu->mlu/dot_general | solution.py:276
  175.2 0.4 copy.26
  175.5 15.6 %all_to_all.30 = bf16[16,3,45,192]{3,2,1,0:T(8,128)(2,1)S(1)} all-to-all(bf16[16,3,45,192]{3,2,1,0:T(8,128)(2,1)S(1)} %bitcast.23), channel_id=1, replica_groups=mesh['lat'=16,'lon'=8] {'lat'}, dimensions={0} | all-to-all | bytes 1658880 | tf_op jit(solution)/shard_map/all_to_all | solution.py:40
  191.1 0.1 copy.27
  191.2 0.6 reshape.309.mixed
  191.8 4.5 %shard_map.48 = bf16[16,288,128]{2,1,0:T(8,128)(2,1)S(1)} custom-call(bf16[3,720,192]{2,1,0:T(8,128)(2,1)S(1)} %reshape.309.mixed, bf16[16,1088,128]{2,1,0:T(8,128)(2,1)} %all-to-all-done.1.table), custom_call_target="tpu_custom_call" | custom-call | flops 849346560 | bytes 6000000 | tf_op jit(solution)/shard_map/pallas_call | solution.py:138
  196.3 15.5 %all_to_all.31.rows = bf16[16,288,128]{2,1,0:T(8,128)(2,1)S(1)} all-to-all(bf16[16,288,128]{2,1,0:T(8,128)(2,1)S(1)} %shard_map.48), channel_id=1, replica_groups=mesh['lat'=16,'lon'=8] {'lat'}, dimensions={0} | all-to-all | bytes 2359296 | tf_op jit(solution)/shard_map/all_to_all | solution.py:40
  211.7 3.3 %shard_map.49 = (bf16[48,64,128]{2,1,0:T(8,128)(2,1)}, bf16[48,32,128]{2,1,0:T(8,128)(2,1)S(1)}) custom-call(bf16[16,288,128]{2,1,0:T(8,128)(2,1)S(1)} %all_to_all.31.rows), custom_call_target="tpu_custom_call" | custom-call | tf_op jit(solution)/shard_map/pallas_call | solution.py:161
  215.0 0.0 all-gather.3.cloned.1.call-update
  215.0 1.3 collective-permute-start
  216.3 1.5 collective-permute-start.1
  217.8 10.3 %collective-permute-start.4 = (bf16[48,32,128]{2,1,0:T(8,128)(2,1)S(1)}, bf16[48,32,128]{2,1,0:T(8,128)(2,1)S(1)}, u32[]{:S(2)}, u32[]{:S(2)}) collective-permute-start(bf16[48,32,128]{2,1,0:T(8,128)(2,1)S(1)} %get-tuple-element.30.refs_1_), channel_id=1, source_target_pairs={{0,1},{1,0},{2,3},{3,2},{4,5},{5,4},{6,7},{7,6},{8,9},{9,8},{10,11... | collective-permute-start | bytes 1179656 | tf_op jit(solution)/shard_map/ppermute | solution.py:222
  228.1 0.0 collective-permute-done.refs_2_
  228.1 0.1 collective-permute-start.2
  228.2 0.0 collective-permute-done.1.refs_3_
  228.2 2.7 collective-permute-start.3
  231.0 8.6 %collective-permute-start.5 = (bf16[48,32,128]{2,1,0:T(8,128)(2,1)S(1)}, bf16[48,32,128]{2,1,0:T(8,128)(2,1)S(1)}, u32[]{:S(2)}, u32[]{:S(2)}) collective-permute-start(bf16[48,32,128]{2,1,0:T(8,128)(2,1)S(1)} %collective-permute-done.refs_2_), channel_id=1, source_target_pairs={{0,1},{1,0},{2,3},{3,2},{4,5},{5,4},{6,7},{7,6},{8,9},{9,8},{10,11... | collective-permute-start | bytes 1179656 | tf_op jit(solution)/shard_map/ppermute | solution.py:222
  239.6 0.0 collective-permute-start.6
  239.6 0.0 collective-permute-done.2.refs_4_
  239.6 6.7 %collective-permute-start.7 = (bf16[48,16,128]{2,1,0:T(8,128)(2,1)S(1)}, bf16[48,16,128]{2,1,0:T(8,128)(2,1)S(1)}, u32[]{:S(2)}, u32[]{:S(2)}) collective-permute-start(bf16[48,16,128]{2,1,0:T(8,128)(2,1)S(1)} %collective-permute-done.2.refs_4_), channel_id=1, source_target_pairs={{0,1},{1,0},{2,3},{3,2},{4,5},{5,4},{6,7},{7,6},{8,9},{9,8},{10,11... | collective-permute-start | bytes 589832 | tf_op jit(solution)/shard_map/ppermute | solution.py:222
  246.3 0.0 collective-permute-done.3.refs_5_
  246.3 0.7 collective-permute-start.8
  246.9 0.0 collective-permute-done.4.refs_6_
  246.9 0.4 collective-permute-done.7.refs_9_
  247.3 0.7 collective-permute-done.8.refs_10_
  248.0 0.0 collective-permute-done.5.refs_7_
  248.0 0.0 collective-permute-done.6.refs_8_
  248.0 17.6 %all-gather.3.cloned.1.call-done = bf16[384,64,128]{2,1,0:T(8,128)(2,1)} async-done(((bf16[48,64,128]{2,1,0:T(8,128)(2,1)}), bf16[384,64,128]{2,1,0:T(8,128)(2,1)}) %all-gather.3.cloned.1.call-update) | async-done | bytes 6291472 | tf_op jit(solution)/shard_map/all_gather | solution.py:280
  265.7 9.5 %shard_map.50 = bf16[2,48,64,450]{3,2,1,0:T(8,128)(2,1)} custom-call(bf16[464,768]{1,0:T(8,128)(2,1)} %fusion.18.table, bf16[8,48,64,128]{3,2,1,0:T(8,128)(2,1)} %bitcast.21, bf16[48,32,128]{2,1,0:T(8,128)(2,1)} %copy-done.4, bf16[48,32,128]{2,1,0:T(8,128)(2,1)} %copy-done.6, bf16[48,32,128]{2,1,0:T(8,128)(2,1)} %copy-done.7, ...), custom_call_target="tpu_custom_call" | custom-call | tf_op jit(solution)/shard_map/pallas_call | solution.py:198
  (49 shorter events, 0.2 us)
Async XLA Ops:
  12.9 51.2 %all-to-all-start = ((bf16[16,135,720]{2,1,0:T(8,128)(2,1)}), bf16[16,135,720]{2,1,0:T(8,128)(2,1)}, u32[]{:S(2)}, u32[]{:S(2)}) async-start(bf16[16,135,720]{2,1,0:T(8,128)(2,1)} %reshape.304), calls=%async_computation | async-start | bytes 6684672 | tf_op jit(solution)/shard_map/all_to_all | solution.py:40
  21.6 102.7 %reduce-scatter.2.cloned.1.call-start = ((), (), s32[]{:S(2)}) async-start(), calls=%async_computation.7 | async-start | bytes 9953280 | tf_op jit(solution)/shard_map/reduce_scatter | solution.py:248
  21.6 2.3 copy-start
  23.9 8.3 %copy-start.3 = (bf16[96,45,180]{0,2,1:T(8,128)(2,1)S(1)}, bf16[96,45,180]{0,2,1:T(8,128)(2,1)}, u32[]{:S(2)}) copy-start(bf16[96,45,180]{0,2,1:T(8,128)(2,1)} %param.4) | copy-start | bytes 4665604
  26.2 2.1 copy-start.2
  36.1 3.5 %copy-start.1 = (bf16[8,45,96,96]{3,2,1,0:T(8,128)(2,1)}, bf16[8,45,96,96]{3,2,1,0:T(8,128)(2,1)S(1)}, u32[]{:S(2)}) copy-start(bf16[8,45,96,96]{3,2,1,0:T(8,128)(2,1)S(1)} %shard_map.46) | copy-start | bytes 19906564
  64.2 65.0 %all-to-all-start.1 = ((bf16[16,1088,128]{2,1,0:T(8,128)(2,1)}), bf16[16,1088,128]{2,1,0:T(8,128)(2,1)}, u32[]{:S(2)}, u32[]{:S(2)}) async-start(bf16[16,1088,128]{2,1,0:T(8,128)(2,1)} %copy-done.2), calls=%async_computation.2 | async-start | bytes 8912896 | tf_op jit(solution)/shard_map/all_to_all | solution.py:40
  131.4 18.3 %all-to-all-start.2 = ((bf16[16,3,2,45,96]{4,2,3,1,0:T(2,128)(2,1)}), bf16[16,3,2,45,96]{4,2,3,1,0:T(2,128)(2,1)S(1)}, u32[]{:S(2)}, u32[]{:S(2)}) async-start(bf16[16,3,2,45,96]{4,2,3,1,0:T(2,128)(2,1)} %copy.19), calls=%async_computation.3 | async-start | bytes 2211840 | tf_op jit(solution)/shard_map/all_to_all | solution.py:40
  155.4 4.4 %copy-start.5 = (bf16[45,96,192]{2,1,0:T(8,128)(2,1)S(1)}, bf16[45,96,192]{2,1,0:T(8,128)(2,1)}, u32[]{:S(2)}) copy-start(bf16[45,96,192]{2,1,0:T(8,128)(2,1)} %param.6) | copy-start | bytes 4976644
  155.5 16.7 %all-to-all-start.3 = ((bf16[16,3,45,192]{3,2,1,0:T(8,128)(2,1)}), bf16[16,3,45,192]{3,2,1,0:T(8,128)(2,1)S(1)}, u32[]{:S(2)}, u32[]{:S(2)}) async-start(bf16[16,3,45,192]{3,2,1,0:T(8,128)(2,1)} %copy.24), calls=%async_computation.4 | async-start | bytes 2359296 | tf_op jit(solution)/shard_map/all_to_all | solution.py:40
  159.6 106.0 %all-gather.3.cloned.1.call-start = ((), (), s32[]{:S(2)}) async-start(), calls=%async_computation.8 | async-start | bytes 7077888 | tf_op jit(solution)/shard_map/all_gather | solution.py:280
  215.0 50.6 %copy-start.4 = (bf16[48,32,128]{2,1,0:T(8,128)(2,1)}, bf16[48,32,128]{2,1,0:T(8,128)(2,1)S(1)}, u32[]{:S(2)}) copy-start(bf16[48,32,128]{2,1,0:T(8,128)(2,1)S(1)} %get-tuple-element.30.refs_1_) | copy-start | bytes 1179652
  215.0 13.1 %collective-permute-start = (bf16[48,32,128]{2,1,0:T(8,128)(2,1)S(1)}, bf16[48,32,128]{2,1,0:T(8,128)(2,1)S(1)}, u32[]{:S(2)}, u32[]{:S(2)}) collective-permute-start(bf16[48,32,128]{2,1,0:T(8,128)(2,1)S(1)} %get-tuple-element.30.refs_1_), channel_id=1, source_target_pairs={{0,2},{1,3},{2,4},{3,5},{4,6},{5,7},{6,0},{7,1},{8,10},{9,11},{10,... | collective-permute-start | bytes 1179656 | tf_op jit(solution)/shard_map/ppermute | solution.py:219
  216.3 11.9 %collective-permute-start.1 = (bf16[48,32,128]{2,1,0:T(8,128)(2,1)S(1)}, bf16[48,32,128]{2,1,0:T(8,128)(2,1)S(1)}, u32[]{:S(2)}, u32[]{:S(2)}) collective-permute-start(bf16[48,32,128]{2,1,0:T(8,128)(2,1)S(1)} %get-tuple-element.30.refs_1_), channel_id=1, source_target_pairs={{0,6},{1,7},{2,0},{3,1},{4,2},{5,3},{6,4},{7,5},{8,14},{9,15},{10,... | collective-permute-start | bytes 1179656 | tf_op jit(solution)/shard_map/ppermute | solution.py:219
  217.8 29.2 %collective-permute-start.4 = (bf16[48,32,128]{2,1,0:T(8,128)(2,1)S(1)}, bf16[48,32,128]{2,1,0:T(8,128)(2,1)S(1)}, u32[]{:S(2)}, u32[]{:S(2)}) collective-permute-start(bf16[48,32,128]{2,1,0:T(8,128)(2,1)S(1)} %get-tuple-element.30.refs_1_), channel_id=1, source_target_pairs={{0,1},{1,0},{2,3},{3,2},{4,5},{5,4},{6,7},{7,6},{8,9},{9,8},{10,11... | collective-permute-start | bytes 1179656 | tf_op jit(solution)/shard_map/ppermute | solution.py:222
  228.1 37.5 %copy-start.6 = (bf16[48,32,128]{2,1,0:T(8,128)(2,1)}, bf16[48,32,128]{2,1,0:T(8,128)(2,1)S(1)}, u32[]{:S(2)}) copy-start(bf16[48,32,128]{2,1,0:T(8,128)(2,1)S(1)} %collective-permute-done.refs_2_) | copy-start | bytes 1179652
  228.1 11.5 %collective-permute-start.2 = (bf16[48,16,128]{2,1,0:T(8,128)(2,1)S(1)}, bf16[48,16,128]{2,1,0:T(8,128)(2,1)S(1)}, u32[]{:S(2)}, u32[]{:S(2)}) collective-permute-start(bf16[48,16,128]{2,1,0:T(8,128)(2,1)S(1)} %slice.16), channel_id=1, source_target_pairs={{0,2},{1,3},{2,4},{3,5},{4,6},{5,7},{6,0},{7,1},{8,10},{9,11},{10,... | collective-permute-start | bytes 589832 | tf_op jit(solution)/shard_map/ppermute | solution.py:219
  228.2 37.4 %copy-start.7 = (bf16[48,32,128]{2,1,0:T(8,128)(2,1)}, bf16[48,32,128]{2,1,0:T(8,128)(2,1)S(1)}, u32[]{:S(2)}) copy-start(bf16[48,32,128]{2,1,0:T(8,128)(2,1)S(1)} %collective-permute-done.1.refs_3_) | copy-start | bytes 1179652
  228.2 18.0 %collective-permute-start.3 = (bf16[48,16,128]{2,1,0:T(8,128)(2,1)S(1)}, bf16[48,16,128]{2,1,0:T(8,128)(2,1)S(1)}, u32[]{:S(2)}, u32[]{:S(2)}) collective-permute-start(bf16[48,16,128]{2,1,0:T(8,128)(2,1)S(1)} %slice.17), channel_id=1, source_target_pairs={{0,6},{1,7},{2,0},{3,1},{4,2},{5,3},{6,4},{7,5},{8,14},{9,15},{10,... | collective-permute-start | bytes 589832 | tf_op jit(solution)/shard_map/ppermute | solution.py:219
  231.0 17.1 %collective-permute-start.5 = (bf16[48,32,128]{2,1,0:T(8,128)(2,1)S(1)}, bf16[48,32,128]{2,1,0:T(8,128)(2,1)S(1)}, u32[]{:S(2)}, u32[]{:S(2)}) collective-permute-start(bf16[48,32,128]{2,1,0:T(8,128)(2,1)S(1)} %collective-permute-done.refs_2_), channel_id=1, source_target_pairs={{0,1},{1,0},{2,3},{3,2},{4,5},{5,4},{6,7},{7,6},{8,9},{9,8},{10,11... | collective-permute-start | bytes 1179656 | tf_op jit(solution)/shard_map/ppermute | solution.py:222
  239.6 8.5 %collective-permute-start.6 = (bf16[48,32,128]{2,1,0:T(8,128)(2,1)S(1)}, bf16[48,32,128]{2,1,0:T(8,128)(2,1)S(1)}, u32[]{:S(2)}, u32[]{:S(2)}) collective-permute-start(bf16[48,32,128]{2,1,0:T(8,128)(2,1)S(1)} %collective-permute-done.1.refs_3_), channel_id=1, source_target_pairs={{0,1},{1,0},{2,3},{3,2},{4,5},{5,4},{6,7},{7,6},{8,9},{9,8},{10,11... | collective-permute-start | bytes 1179656 | tf_op jit(solution)/shard_map/ppermute | solution.py:222
  239.6 26.0 %copy-start.11 = (bf16[48,16,128]{2,1,0:T(8,128)(2,1)}, bf16[48,16,128]{2,1,0:T(8,128)(2,1)S(1)}, u32[]{:S(2)}) copy-start(bf16[48,16,128]{2,1,0:T(8,128)(2,1)S(1)} %collective-permute-done.2.refs_4_) | copy-start | bytes 589828
  239.6 7.8 %collective-permute-start.7 = (bf16[48,16,128]{2,1,0:T(8,128)(2,1)S(1)}, bf16[48,16,128]{2,1,0:T(8,128)(2,1)S(1)}, u32[]{:S(2)}, u32[]{:S(2)}) collective-permute-start(bf16[48,16,128]{2,1,0:T(8,128)(2,1)S(1)} %collective-permute-done.2.refs_4_), channel_id=1, source_target_pairs={{0,1},{1,0},{2,3},{3,2},{4,5},{5,4},{6,7},{7,6},{8,9},{9,8},{10,11... | collective-permute-start | bytes 589832 | tf_op jit(solution)/shard_map/ppermute | solution.py:222
  246.3 19.3 %copy-start.12 = (bf16[48,16,128]{2,1,0:T(8,128)(2,1)}, bf16[48,16,128]{2,1,0:T(8,128)(2,1)S(1)}, u32[]{:S(2)}) copy-start(bf16[48,16,128]{2,1,0:T(8,128)(2,1)S(1)} %collective-permute-done.3.refs_5_) | copy-start | bytes 589828
  246.3 1.7 collective-permute-start.8
  246.9 18.7 %copy-start.8 = (bf16[48,32,128]{2,1,0:T(8,128)(2,1)}, bf16[48,32,128]{2,1,0:T(8,128)(2,1)S(1)}, u32[]{:S(2)}) copy-start(bf16[48,32,128]{2,1,0:T(8,128)(2,1)S(1)} %collective-permute-done.4.refs_6_) | copy-start | bytes 1179652
  247.3 18.3 %copy-start.13 = (bf16[48,16,128]{2,1,0:T(8,128)(2,1)}, bf16[48,16,128]{2,1,0:T(8,128)(2,1)S(1)}, u32[]{:S(2)}) copy-start(bf16[48,16,128]{2,1,0:T(8,128)(2,1)S(1)} %collective-permute-done.7.refs_9_) | copy-start | bytes 589828
  248.0 17.6 %copy-start.14 = (bf16[48,16,128]{2,1,0:T(8,128)(2,1)}, bf16[48,16,128]{2,1,0:T(8,128)(2,1)S(1)}, u32[]{:S(2)}) copy-start(bf16[48,16,128]{2,1,0:T(8,128)(2,1)S(1)} %collective-permute-done.8.refs_10_) | copy-start | bytes 589828
  248.0 17.6 %copy-start.9 = (bf16[48,32,128]{2,1,0:T(8,128)(2,1)}, bf16[48,32,128]{2,1,0:T(8,128)(2,1)S(1)}, u32[]{:S(2)}) copy-start(bf16[48,32,128]{2,1,0:T(8,128)(2,1)S(1)} %collective-permute-done.5.refs_7_) | copy-start | bytes 1179652
  248.0 17.6 %copy-start.10 = (bf16[48,32,128]{2,1,0:T(8,128)(2,1)}, bf16[48,32,128]{2,1,0:T(8,128)(2,1)S(1)}, u32[]{:S(2)}) copy-start(bf16[48,32,128]{2,1,0:T(8,128)(2,1)S(1)} %collective-permute-done.6.refs_8_) | copy-start | bytes 1179652
Sparse Core Ops, SparseCore 0:
  64.3 59.9 reduce-scatter.1
  215.1 50.4 all-gather.2

commit v7 on v6

--- a/solution.py
+++ b/solution.py
@@ -250,13 +250,7 @@
     ftab = ftab.reshape(LATS, EACH, ROWS, 720)
     spectrum = spectrum.reshape(ROWS, 2, LATS, EACH, CHAN)
     spectrum = jnp.transpose(spectrum, (2, 3, 1, 0, 4))
-    spectrum, wtab, lon = lax.optimization_barrier((spectrum, wtab, lon))
-    spectrum = swap(spectrum, "lat")
-    spectrum = jnp.transpose(spectrum, (1, 0, 3, 2, 4)).reshape(EACH, 720, 2 * CHAN)
-
-    coef = jnp.einsum("ajlq,jqn->ajln", ftab, spectrum, preferred_element_type=jnp.float32)
-    coef = swap(coef.astype(BF), "lat").reshape(SLOTS, ROWS, 2 * CHAN)
-
+    spectrum = spectrum.reshape(LATS, 2 * EACH * ROWS, CHAN)
     ids, turns, real = [], [], []
     orders = [(column, 0, SPLIT) for column in range(LONS)]
     orders += lon_order(SPLIT, 2 * SLOTS)
@@ -268,11 +262,16 @@
     ids, turns, real = (jnp.concatenate(v)[None, :] for v in (ids, turns, real))
     points = (lon * OUT_COLS + jnp.arange(WIDE, dtype=jnp.int32))[:, None]
     table = waves(ids, turns, real, points, LON_OUT, KEPT_ORDERS ** (-0.5))
-    coef, table = lax.optimization_barrier((coef, table))
-
     w = degree_mixing_weight
     turned = jnp.concatenate([-w[..., CHAN:], w[..., :CHAN]], axis=-1)
     both = jnp.concatenate([w, turned], axis=1)
+    spectrum, wtab, table, both = lax.optimization_barrier((spectrum, wtab, table, both))
+    spectrum = swap(spectrum, "lat").reshape(LATS, EACH, 2, ROWS, CHAN)
+    spectrum = jnp.transpose(spectrum, (1, 0, 3, 2, 4)).reshape(EACH, 720, 2 * CHAN)
+
+    coef = jnp.einsum("ajlq,jqn->ajln", ftab, spectrum, preferred_element_type=jnp.float32)
+    coef = swap(coef.astype(BF), "lat").reshape(SLOTS, ROWS, 2 * CHAN)
+
     mixed = jnp.einsum("mlt,ltu->mlu", coef, both, preferred_element_type=jnp.float32)
     mixed = swap(mixed.astype(BF).reshape(LATS, EACH, ROWS, 2 * CHAN), "lat")
     mixed = jnp.transpose(mixed, (1, 0, 2, 3)).reshape(EACH, 720, 2 * CHAN)

time: 283 us -> 279 us (0.986)
  blocking collectives: 31 us -> 47.6 us
  waiting for transfers between devices: 108 us -> 91.6 us
  starting transfers between devices: 61 us -> 56.7 us
  other arithmetic: 12.3 us -> 15.7 us
    all_to_all x2 -> x3, blocking collectives: 31 us -> 47.6 us  [swap(): return lax.all_to_all(x, axis, split_axis=0, concat_axis=0, tiled=True)]
    reduce_scatter x1, waiting for transfers between devices: 49.6 us -> 37.5 us  [local(): spectrum = lax.psum_scatter(spectrum, 'lon', scatter_dimension=0)]
    concatenate x0 -> x1, other arithmetic: none -> 4.8 us  [local(): both = jnp.concatenate([w, turned], axis=1)]
    all_to_all x4 -> x3, waiting for transfers between devices: 39.7 us -> 35.4 us  [swap(): return lax.all_to_all(x, axis, split_axis=0, concat_axis=0, tiled=True)]
    all_to_all x4 -> x3, starting transfers between devices: 28.9 us -> 24.9 us  [swap(): return lax.all_to_all(x, axis, split_axis=0, concat_axis=0, tiled=True)]
    unnamed x31 -> x35, local copies, waits for them, and re-layouts: 10.9 us -> 10.9 us
  transfers between devices with their start and end apart: 15 -> 14, of which waited for: 8 -> 7; matrix products, arithmetic and copies ran while one was open for 7% -> 8% of each run, Pallas kernels for 2% -> 2%
where the time goes in v7:
time: 279 us; the launch traced here: 278 us
  waiting for transfers between devices  91.6 us (33%)
  starting transfers between devices  56.7 us (20%)
  blocking collectives  47.6 us (17%)
  local copies, waits for them, and re-layouts  25.1 us (9%)
  Pallas kernels  23.4 us (8%)
  other arithmetic  15.7 us (6%)
  between operations  13.9 us (5%)
  matrix products  4.14 us (1%)
    all_to_all x3, blocking collectives, swap(): return lax.all_to_all(x, axis, split_axis=0, concat_axis=0, tiled=True)  47.6 us
    reduce_scatter x1, waiting for transfers between devices, local(): spectrum = lax.psum_scatter(spectrum, 'lon', scatter_dimension=0)  37.5 us
    all_to_all x3, waiting for transfers between devices, swap(): return lax.all_to_all(x, axis, split_axis=0, concat_axis=0, tiled=True)  35.4 us
    ppermute x5, starting transfers between devices, across(): return lax.ppermute(u, 'lon', [(i, i ^ 1) for i in range(8)])  25.9 us
    all_to_all x3, starting transfers between devices, swap(): return lax.all_to_all(x, axis, split_axis=0, concat_axis=0, tiled=True)  24.9 us
    all_gather x1, waiting for transfers between devices, local(): pieces = [lax.all_gather(rows, 'lon', axis=0)] + gather_lon(rest)  17.6 us
    unnamed x35, local copies, waits for them, and re-layouts  10.9 us
    convert_element_type x2, other arithmetic, waves(): return (jnp.cos(angles) * jnp.where(valid, factor, 0.0)).astype(BF)  10.2 us
  transfers between devices with their start and end apart: 14, of which 7 were waited for; matrix products, arithmetic and copies ran while one was open for 8% of the time, Pallas kernels for 2%

profile of v7, /device:TPU:1, one launch (start us, length us, event | category | flops | bytes accessed | tf_op | source)
XLA Modules:
  0.0 278.1 jit_solution(16215795504807883598)
XLA Ops:
  6.5 3.0 %copy.32 = bf16[46,45,720]{2,1,0:T(8,128)(2,1)S(1)} copy(bf16[46,45,720]{2,0,1:T(8,128)(2,1)} %param.5) | data formatting | bytes 5961600
  9.6 0.4 pad.4.clone
  10.0 2.9 %reshape.310 = bf16[16,135,720]{2,1,0:T(8,128)(2,1)} reshape(bf16[48,45,720]{2,1,0:T(8,128)(2,1)S(1)} %pad.4.clone) | data formatting | bytes 6220800 | tf_op jit(solution)/shard_map/reshape | solution.py:233
  12.9 8.6 %all-to-all-start = ((bf16[16,135,720]{2,1,0:T(8,128)(2,1)}), bf16[16,135,720]{2,1,0:T(8,128)(2,1)}, u32[]{:S(2)}, u32[]{:S(2)}) async-start(bf16[16,135,720]{2,1,0:T(8,128)(2,1)} %reshape.310), calls=%async_computation | async-start | bytes 6684672 | tf_op jit(solution)/shard_map/all_to_all | solution.py:40
  21.6 0.0 reduce-scatter.2.cloned.1.call-start
  21.6 0.0 copy-start
  21.6 2.3 copy-done
  23.9 2.3 shard_map.47
  26.2 0.0 copy-start.2
  26.2 2.1 copy-done.2
  28.3 3.8 %fusion.22.waves_in = bf16[768,180]{1,0:T(8,128)(2,1)S(1)} fusion(f32[768]{0:T(1024)S(1)} %fusion.41, s32[768]{0:T(1024)S(1)} %get-tuple-element.31, s32[180]{0:T(256)S(1)} %iota_add_fusion.1, s32[768]{0:T(1024)S(1)} %get-tuple-element.32), kind=kLoop, calls=%fused_computation.24 | loop fusion | flops 1658880 | bytes 286416 | tf_op jit(solution)/shard_map/convert_element_type | solution.py:36
  32.2 3.9 %shard_map.46 = bf16[8,45,96,96]{3,2,1,0:T(8,128)(2,1)S(1)} custom-call(bf16[768,180]{1,0:T(8,128)(2,1)S(1)} %fusion.22.waves_in, bf16[45,180,96]{2,1,0:T(8,128)(2,1)S(1)} %bitcast.24), custom_call_target="tpu_custom_call" | custom-call | tf_op jit(solution)/shard_map/pallas_call | solution.py:56
  36.1 3.5 %copy-done.1 = bf16[8,45,96,96]{3,2,1,0:T(8,128)(2,1)} copy-done((bf16[8,45,96,96]{3,2,1,0:T(8,128)(2,1)}, bf16[8,45,96,96]{3,2,1,0:T(8,128)(2,1)S(1)}, u32[]{:S(2)}) %copy-start.1) | copy-done | bytes 6635544
  39.6 24.5 %all-to-all-done = bf16[16,135,720]{2,1,0:T(8,128)(2,1)} async-done(((bf16[16,135,720]{2,1,0:T(8,128)(2,1)}), bf16[16,135,720]{2,1,0:T(8,128)(2,1)}, u32[]{:S(2)}, u32[]{:S(2)}) %all-to-all-start) | async-done | bytes 3110432 | tf_op jit(solution)/shard_map/all_to_all | solution.py:40
  64.1 0.0 reduce-scatter.2.cloned.1.call-update
  64.2 0.0 copy-start.5
  64.2 10.3 %all-to-all-start.1 = ((bf16[16,1088,128]{2,1,0:T(8,128)(2,1)}), bf16[16,1088,128]{2,1,0:T(8,128)(2,1)}, u32[]{:S(2)}, u32[]{:S(2)}) async-start(bf16[16,1088,128]{2,1,0:T(8,128)(2,1)} %copy-done.2), calls=%async_computation.2 | async-start | bytes 8912896 | tf_op jit(solution)/shard_map/all_to_all | solution.py:40
  74.6 0.1 concatenate.25
  74.7 0.1 concatenate.24
  74.9 0.1 concatenate.23
  75.1 0.5 slice_negate_fusion
  75.6 4.8 %maximum_maximum_fusion = bf16[45,192,192]{2,1,0:T(8,128)(2,1)} fusion(bf16[45,96,96]{2,1,0:T(8,128)(2,1)S(1)} %get-tuple-element.30, bf16[45,96,96]{2,1,0:T(8,128)(2,1)S(1)} %get-tuple-element.29, bf16[45,96,192]{2,1,0:T(8,128)(2,1)S(1)} %copy-done.5), kind=kLoop, calls=%fused_computation | loop fusion | flops 9953280 | bytes 6635520 | tf_op jit(solution)/shard_map/concatenate | solution.py:267
  80.4 6.4 %fusion.9.table = bf16[464,768]{1,0:T(8,128)(2,1)} fusion(f32[768]{0:T(1024)S(1)} %broadcast_select_fusion, s32[768]{0:T(1024)S(1)} %broadcast_multiply_fusion, s32[464]{0:T(512)S(1)} %iota_add_fusion, s32[768]{0:T(1024)S(1)} %concatenate.23), kind=kLoop, calls=%fused_computation.10 | loop fusion | flops 4276224 | bytes 723776 | tf_op jit(solution)/shard_map/convert_element_type | solution.py:36
  86.8 37.5 %reduce-scatter.2.cloned.1.call-done = bf16[1,45,96,96]{3,2,1,0:T(8,128)(2,1)} async-done(((bf16[8,45,96,96]{3,2,1,0:T(8,128)(2,1)}), bf16[1,45,96,96]{3,2,1,0:T(8,128)(2,1)}) %reduce-scatter.2.cloned.1.call-update) | async-done | bytes 829456 | tf_op jit(solution)/shard_map/reduce_scatter | solution.py:248
  124.3 1.7 copy.18
  126.0 0.3 copy.19
  126.3 3.0 %all-to-all-done.1.table = bf16[16,1088,128]{2,1,0:T(8,128)(2,1)} async-done(((bf16[16,1088,128]{2,1,0:T(8,128)(2,1)}), bf16[16,1088,128]{2,1,0:T(8,128)(2,1)}, u32[]{:S(2)}, u32[]{:S(2)}) %all-to-all-start.1) | async-done | bytes 4456480 | tf_op jit(solution)/shard_map/all_to_all | solution.py:40
  129.3 1.3 copy.20
  130.6 5.9 %all-to-all-start.2 = ((bf16[16,270,96]{2,1,0:T(8,128)(2,1)}), bf16[16,270,96]{2,1,0:T(8,128)(2,1)S(1)}, u32[]{:S(2)}, u32[]{:S(2)}) async-start(bf16[16,270,96]{2,1,0:T(8,128)(2,1)} %copy.20), calls=%async_computation.3 | async-start | bytes 2228224 | tf_op jit(solution)/shard_map/all_to_all | solution.py:40
  136.5 0.2 all-gather.3.cloned.1.call-start
  136.8 4.3 %copy.23 = bf16[16,135,720]{2,0,1:T(8,128)(2,1)} copy(bf16[16,135,720]{2,1,0:T(8,128)(2,1)} %all-to-all-done) | data formatting | bytes 6220800 | tf_op jit(solution)/shard_map/optimization_barrier | solution.py:247
  141.1 7.9 %all-to-all-done.2 = bf16[16,270,96]{2,1,0:T(8,128)(2,1)S(1)} async-done(((bf16[16,270,96]{2,1,0:T(8,128)(2,1)}), bf16[16,270,96]{2,1,0:T(8,128)(2,1)S(1)}, u32[]{:S(2)}, u32[]{:S(2)}) %all-to-all-start.2) | async-done | bytes 829472 | tf_op jit(solution)/shard_map/all_to_all | solution.py:40
  149.0 0.3 copy.21
  149.2 0.9 copy.22
  150.1 0.7 reshape.323
  150.8 3.3 %fusion.13 = bf16[16,3,45,192]{3,2,0,1:T(8,128)(2,1)S(1)} fusion(bf16[3,720,192,1]{2,1,3,0:T(8,128)(2,1)S(1)} %reshape.323, bf16[16,3,45,720]{3,0,2,1:T(8,128)(2,1)} %bitcast.34), kind=kOutput, calls=%fused_computation.15 | convolution fusion | flops 597611520 | bytes 4769280 | tf_op jit(solution)/shard_map/ajlq,jqn->ajln/dot_general | solution.py:272
  154.2 0.1 copy.26
  154.3 16.3 %all_to_all.30 = bf16[16,3,45,192]{3,2,1,0:T(8,128)(2,1)S(1)} all-to-all(bf16[16,3,45,192]{3,2,1,0:T(8,128)(2,1)S(1)} %copy.26), channel_id=1, replica_groups=mesh['lat'=16,'lon'=8] {'lat'}, dimensions={0} | all-to-all | bytes 1658880 | tf_op jit(solution)/shard_map/all_to_all | solution.py:40
  170.6 0.8 fusion.16
  171.4 0.4 copy.28
  171.8 15.7 %all_to_all.31 = bf16[16,3,45,192]{3,2,1,0:T(8,128)(2,1)S(1)} all-to-all(bf16[16,3,45,192]{3,2,1,0:T(8,128)(2,1)S(1)} %bitcast.29), channel_id=1, replica_groups=mesh['lat'=16,'lon'=8] {'lat'}, dimensions={0} | all-to-all | bytes 1658880 | tf_op jit(solution)/shard_map/all_to_all | solution.py:40
  187.4 0.1 copy.29
  187.5 0.6 reshape.317.mixed
  188.1 4.5 %shard_map.48 = bf16[16,288,128]{2,1,0:T(8,128)(2,1)S(1)} custom-call(bf16[3,720,192]{2,1,0:T(8,128)(2,1)S(1)} %reshape.317.mixed, bf16[16,1088,128]{2,1,0:T(8,128)(2,1)} %all-to-all-done.1.table), custom_call_target="tpu_custom_call" | custom-call | flops 849346560 | bytes 6000000 | tf_op jit(solution)/shard_map/pallas_call | solution.py:138
  192.5 15.6 %all_to_all.32.rows = bf16[16,288,128]{2,1,0:T(8,128)(2,1)S(1)} all-to-all(bf16[16,288,128]{2,1,0:T(8,128)(2,1)S(1)} %shard_map.48), channel_id=1, replica_groups=mesh['lat'=16,'lon'=8] {'lat'}, dimensions={0} | all-to-all | bytes 2359296 | tf_op jit(solution)/shard_map/all_to_all | solution.py:40
  208.2 3.3 %shard_map.49 = (bf16[48,64,128]{2,1,0:T(8,128)(2,1)}, bf16[48,32,128]{2,1,0:T(8,128)(2,1)S(1)}) custom-call(bf16[16,288,128]{2,1,0:T(8,128)(2,1)S(1)} %all_to_all.32.rows), custom_call_target="tpu_custom_call" | custom-call | tf_op jit(solution)/shard_map/pallas_call | solution.py:161
  211.5 0.0 all-gather.3.cloned.1.call-update
  211.5 1.3 collective-permute-start
  212.8 1.5 collective-permute-start.1
  214.2 10.0 %collective-permute-start.4 = (bf16[48,32,128]{2,1,0:T(8,128)(2,1)S(1)}, bf16[48,32,128]{2,1,0:T(8,128)(2,1)S(1)}, u32[]{:S(2)}, u32[]{:S(2)}) collective-permute-start(bf16[48,32,128]{2,1,0:T(8,128)(2,1)S(1)} %get-tuple-element.28.refs_1_), channel_id=1, source_target_pairs={{0,1},{1,0},{2,3},{3,2},{4,5},{5,4},{6,7},{7,6},{8,9},{9,8},{10,11... | collective-permute-start | bytes 1179656 | tf_op jit(solution)/shard_map/ppermute | solution.py:222
  224.2 0.0 collective-permute-done.refs_2_
  224.2 0.1 collective-permute-start.2
  224.4 2.7 collective-permute-start.3
  227.1 8.6 %collective-permute-start.5 = (bf16[48,32,128]{2,1,0:T(8,128)(2,1)S(1)}, bf16[48,32,128]{2,1,0:T(8,128)(2,1)S(1)}, u32[]{:S(2)}, u32[]{:S(2)}) collective-permute-start(bf16[48,32,128]{2,1,0:T(8,128)(2,1)S(1)} %collective-permute-done.refs_2_), channel_id=1, source_target_pairs={{0,1},{1,0},{2,3},{3,2},{4,5},{5,4},{6,7},{7,6},{8,9},{9,8},{10,11... | collective-permute-start | bytes 1179656 | tf_op jit(solution)/shard_map/ppermute | solution.py:222
  235.7 0.0 collective-permute-start.6
  235.7 0.0 collective-permute-done.2.refs_4_
  235.7 6.7 %collective-permute-start.7 = (bf16[48,16,128]{2,1,0:T(8,128)(2,1)S(1)}, bf16[48,16,128]{2,1,0:T(8,128)(2,1)S(1)}, u32[]{:S(2)}, u32[]{:S(2)}) collective-permute-start(bf16[48,16,128]{2,1,0:T(8,128)(2,1)S(1)} %collective-permute-done.2.refs_4_), channel_id=1, source_target_pairs={{0,1},{1,0},{2,3},{3,2},{4,5},{5,4},{6,7},{7,6},{8,9},{9,8},{10,11... | collective-permute-start | bytes 589832 | tf_op jit(solution)/shard_map/ppermute | solution.py:222
  242.4 0.0 collective-permute-done.3.refs_5_
  242.4 0.7 collective-permute-start.8
  243.1 0.0 collective-permute-done.4.refs_6_
  243.1 0.4 collective-permute-done.7.refs_9_
  243.5 0.7 collective-permute-done.8.refs_10_
  244.2 17.6 %all-gather.3.cloned.1.call-done = bf16[384,64,128]{2,1,0:T(8,128)(2,1)} async-done(((bf16[48,64,128]{2,1,0:T(8,128)(2,1)}), bf16[384,64,128]{2,1,0:T(8,128)(2,1)}) %all-gather.3.cloned.1.call-update) | async-done | bytes 6291472 | tf_op jit(solution)/shard_map/all_gather | solution.py:279
  261.8 9.5 %shard_map.50 = bf16[2,48,64,450]{3,2,1,0:T(8,128)(2,1)} custom-call(bf16[464,768]{1,0:T(8,128)(2,1)} %fusion.9.table, bf16[8,48,64,128]{3,2,1,0:T(8,128)(2,1)} %bitcast.27, bf16[48,32,128]{2,1,0:T(8,128)(2,1)} %copy-done.4, bf16[48,32,128]{2,1,0:T(8,128)(2,1)} %copy-done.6, bf16[48,32,128]{2,1,0:T(8,128)(2,1)} %copy-done.7, ...), custom_call_target="tpu_custom_call" | custom-call | tf_op jit(solution)/shard_map/pallas_call | solution.py:198
  (56 shorter events, 0.2 us)
Async XLA Ops:
  12.9 51.2 %all-to-all-start = ((bf16[16,135,720]{2,1,0:T(8,128)(2,1)}), bf16[16,135,720]{2,1,0:T(8,128)(2,1)}, u32[]{:S(2)}, u32[]{:S(2)}) async-start(bf16[16,135,720]{2,1,0:T(8,128)(2,1)} %reshape.310), calls=%async_computation | async-start | bytes 6684672 | tf_op jit(solution)/shard_map/all_to_all | solution.py:40
  21.6 102.7 %reduce-scatter.2.cloned.1.call-start = ((), (), s32[]{:S(2)}) async-start(), calls=%async_computation.7 | async-start | bytes 9953280 | tf_op jit(solution)/shard_map/reduce_scatter | solution.py:248
  21.6 2.3 copy-start
  23.9 8.3 %copy-start.3 = (bf16[96,45,180]{0,2,1:T(8,128)(2,1)S(1)}, bf16[96,45,180]{0,2,1:T(8,128)(2,1)}, u32[]{:S(2)}) copy-start(bf16[96,45,180]{0,2,1:T(8,128)(2,1)} %param.4) | copy-start | bytes 4665604
  26.2 2.1 copy-start.2
  36.1 3.5 %copy-start.1 = (bf16[8,45,96,96]{3,2,1,0:T(8,128)(2,1)}, bf16[8,45,96,96]{3,2,1,0:T(8,128)(2,1)S(1)}, u32[]{:S(2)}) copy-start(bf16[8,45,96,96]{3,2,1,0:T(8,128)(2,1)S(1)} %shard_map.46) | copy-start | bytes 19906564
  64.2 10.9 %copy-start.5 = (bf16[45,96,192]{2,1,0:T(8,128)(2,1)S(1)}, bf16[45,96,192]{2,1,0:T(8,128)(2,1)}, u32[]{:S(2)}) copy-start(bf16[45,96,192]{2,1,0:T(8,128)(2,1)} %param.6) | copy-start | bytes 4976644
  64.2 65.1 %all-to-all-start.1 = ((bf16[16,1088,128]{2,1,0:T(8,128)(2,1)}), bf16[16,1088,128]{2,1,0:T(8,128)(2,1)}, u32[]{:S(2)}, u32[]{:S(2)}) async-start(bf16[16,1088,128]{2,1,0:T(8,128)(2,1)} %copy-done.2), calls=%async_computation.2 | async-start | bytes 8912896 | tf_op jit(solution)/shard_map/all_to_all | solution.py:40
  130.6 18.4 %all-to-all-start.2 = ((bf16[16,270,96]{2,1,0:T(8,128)(2,1)}), bf16[16,270,96]{2,1,0:T(8,128)(2,1)S(1)}, u32[]{:S(2)}, u32[]{:S(2)}) async-start(bf16[16,270,96]{2,1,0:T(8,128)(2,1)} %copy.20), calls=%async_computation.3 | async-start | bytes 2228224 | tf_op jit(solution)/shard_map/all_to_all | solution.py:40
  136.5 125.2 %all-gather.3.cloned.1.call-start = ((), (), s32[]{:S(2)}) async-start(), calls=%async_computation.8 | async-start | bytes 7077888 | tf_op jit(solution)/shard_map/all_gather | solution.py:279
  150.1 20.5 %slice-start = ((s8[4423680]{0:T(1024)(128)(4,1)}), s8[229376]{0:T(1024)(128)(4,1)S(1)}, s32[]{:S(2)}) async-start(s8[4423680]{0:T(1024)(128)(4,1)} %bitcast.25), calls=%async_computation.9 | async-start | bytes 458752
  150.8 19.8 %slice-start.1 = ((s8[4423680]{0:T(1024)(128)(4,1)}), s8[4194304]{0:T(1024)(128)(4,1)S(1)}, s32[]{:S(2)}) async-start(s8[4423680]{0:T(1024)(128)(4,1)} %bitcast.25), calls=%async_computation.10 | async-start | bytes 8388608
  211.5 50.2 %copy-start.4 = (bf16[48,32,128]{2,1,0:T(8,128)(2,1)}, bf16[48,32,128]{2,1,0:T(8,128)(2,1)S(1)}, u32[]{:S(2)}) copy-start(bf16[48,32,128]{2,1,0:T(8,128)(2,1)S(1)} %get-tuple-element.28.refs_1_) | copy-start | bytes 1179652
  211.5 12.7 %collective-permute-start = (bf16[48,32,128]{2,1,0:T(8,128)(2,1)S(1)}, bf16[48,32,128]{2,1,0:T(8,128)(2,1)S(1)}, u32[]{:S(2)}, u32[]{:S(2)}) collective-permute-start(bf16[48,32,128]{2,1,0:T(8,128)(2,1)S(1)} %get-tuple-element.28.refs_1_), channel_id=1, source_target_pairs={{0,2},{1,3},{2,4},{3,5},{4,6},{5,7},{6,0},{7,1},{8,10},{9,11},{10,... | collective-permute-start | bytes 1179656 | tf_op jit(solution)/shard_map/ppermute | solution.py:219
  212.8 11.5 %collective-permute-start.1 = (bf16[48,32,128]{2,1,0:T(8,128)(2,1)S(1)}, bf16[48,32,128]{2,1,0:T(8,128)(2,1)S(1)}, u32[]{:S(2)}, u32[]{:S(2)}) collective-permute-start(bf16[48,32,128]{2,1,0:T(8,128)(2,1)S(1)} %get-tuple-element.28.refs_1_), channel_id=1, source_target_pairs={{0,6},{1,7},{2,0},{3,1},{4,2},{5,3},{6,4},{7,5},{8,14},{9,15},{10,... | collective-permute-start | bytes 1179656 | tf_op jit(solution)/shard_map/ppermute | solution.py:219
  214.2 28.8 %collective-permute-start.4 = (bf16[48,32,128]{2,1,0:T(8,128)(2,1)S(1)}, bf16[48,32,128]{2,1,0:T(8,128)(2,1)S(1)}, u32[]{:S(2)}, u32[]{:S(2)}) collective-permute-start(bf16[48,32,128]{2,1,0:T(8,128)(2,1)S(1)} %get-tuple-element.28.refs_1_), channel_id=1, source_target_pairs={{0,1},{1,0},{2,3},{3,2},{4,5},{5,4},{6,7},{7,6},{8,9},{9,8},{10,11... | collective-permute-start | bytes 1179656 | tf_op jit(solution)/shard_map/ppermute | solution.py:222
  224.2 37.5 %copy-start.6 = (bf16[48,32,128]{2,1,0:T(8,128)(2,1)}, bf16[48,32,128]{2,1,0:T(8,128)(2,1)S(1)}, u32[]{:S(2)}) copy-start(bf16[48,32,128]{2,1,0:T(8,128)(2,1)S(1)} %collective-permute-done.refs_2_) | copy-start | bytes 1179652
  224.2 11.5 %collective-permute-start.2 = (bf16[48,16,128]{2,1,0:T(8,128)(2,1)S(1)}, bf16[48,16,128]{2,1,0:T(8,128)(2,1)S(1)}, u32[]{:S(2)}, u32[]{:S(2)}) collective-permute-start(bf16[48,16,128]{2,1,0:T(8,128)(2,1)S(1)} %slice.16), channel_id=1, source_target_pairs={{0,2},{1,3},{2,4},{3,5},{4,6},{5,7},{6,0},{7,1},{8,10},{9,11},{10,... | collective-permute-start | bytes 589832 | tf_op jit(solution)/shard_map/ppermute | solution.py:219
  224.3 37.4 %copy-start.7 = (bf16[48,32,128]{2,1,0:T(8,128)(2,1)}, bf16[48,32,128]{2,1,0:T(8,128)(2,1)S(1)}, u32[]{:S(2)}) copy-start(bf16[48,32,128]{2,1,0:T(8,128)(2,1)S(1)} %collective-permute-done.1.refs_3_) | copy-start | bytes 1179652
  224.4 18.0 %collective-permute-start.3 = (bf16[48,16,128]{2,1,0:T(8,128)(2,1)S(1)}, bf16[48,16,128]{2,1,0:T(8,128)(2,1)S(1)}, u32[]{:S(2)}, u32[]{:S(2)}) collective-permute-start(bf16[48,16,128]{2,1,0:T(8,128)(2,1)S(1)} %slice.17), channel_id=1, source_target_pairs={{0,6},{1,7},{2,0},{3,1},{4,2},{5,3},{6,4},{7,5},{8,14},{9,15},{10,... | collective-permute-start | bytes 589832 | tf_op jit(solution)/shard_map/ppermute | solution.py:219
  227.1 17.1 %collective-permute-start.5 = (bf16[48,32,128]{2,1,0:T(8,128)(2,1)S(1)}, bf16[48,32,128]{2,1,0:T(8,128)(2,1)S(1)}, u32[]{:S(2)}, u32[]{:S(2)}) collective-permute-start(bf16[48,32,128]{2,1,0:T(8,128)(2,1)S(1)} %collective-permute-done.refs_2_), channel_id=1, source_target_pairs={{0,1},{1,0},{2,3},{3,2},{4,5},{5,4},{6,7},{7,6},{8,9},{9,8},{10,11... | collective-permute-start | bytes 1179656 | tf_op jit(solution)/shard_map/ppermute | solution.py:222
  235.7 8.5 %collective-permute-start.6 = (bf16[48,32,128]{2,1,0:T(8,128)(2,1)S(1)}, bf16[48,32,128]{2,1,0:T(8,128)(2,1)S(1)}, u32[]{:S(2)}, u32[]{:S(2)}) collective-permute-start(bf16[48,32,128]{2,1,0:T(8,128)(2,1)S(1)} %collective-permute-done.1.refs_3_), channel_id=1, source_target_pairs={{0,1},{1,0},{2,3},{3,2},{4,5},{5,4},{6,7},{7,6},{8,9},{9,8},{10,11... | collective-permute-start | bytes 1179656 | tf_op jit(solution)/shard_map/ppermute | solution.py:222
  235.7 26.0 %copy-start.11 = (bf16[48,16,128]{2,1,0:T(8,128)(2,1)}, bf16[48,16,128]{2,1,0:T(8,128)(2,1)S(1)}, u32[]{:S(2)}) copy-start(bf16[48,16,128]{2,1,0:T(8,128)(2,1)S(1)} %collective-permute-done.2.refs_4_) | copy-start | bytes 589828
  235.7 7.8 %collective-permute-start.7 = (bf16[48,16,128]{2,1,0:T(8,128)(2,1)S(1)}, bf16[48,16,128]{2,1,0:T(8,128)(2,1)S(1)}, u32[]{:S(2)}, u32[]{:S(2)}) collective-permute-start(bf16[48,16,128]{2,1,0:T(8,128)(2,1)S(1)} %collective-permute-done.2.refs_4_), channel_id=1, source_target_pairs={{0,1},{1,0},{2,3},{3,2},{4,5},{5,4},{6,7},{7,6},{8,9},{9,8},{10,11... | collective-permute-start | bytes 589832 | tf_op jit(solution)/shard_map/ppermute | solution.py:222
  242.4 19.3 %copy-start.12 = (bf16[48,16,128]{2,1,0:T(8,128)(2,1)}, bf16[48,16,128]{2,1,0:T(8,128)(2,1)S(1)}, u32[]{:S(2)}) copy-start(bf16[48,16,128]{2,1,0:T(8,128)(2,1)S(1)} %collective-permute-done.3.refs_5_) | copy-start | bytes 589828
  242.4 1.7 collective-permute-start.8
  243.1 18.7 %copy-start.8 = (bf16[48,32,128]{2,1,0:T(8,128)(2,1)}, bf16[48,32,128]{2,1,0:T(8,128)(2,1)S(1)}, u32[]{:S(2)}) copy-start(bf16[48,32,128]{2,1,0:T(8,128)(2,1)S(1)} %collective-permute-done.4.refs_6_) | copy-start | bytes 1179652
  243.5 18.3 %copy-start.13 = (bf16[48,16,128]{2,1,0:T(8,128)(2,1)}, bf16[48,16,128]{2,1,0:T(8,128)(2,1)S(1)}, u32[]{:S(2)}) copy-start(bf16[48,16,128]{2,1,0:T(8,128)(2,1)S(1)} %collective-permute-done.7.refs_9_) | copy-start | bytes 589828
  244.1 17.6 %copy-start.14 = (bf16[48,16,128]{2,1,0:T(8,128)(2,1)}, bf16[48,16,128]{2,1,0:T(8,128)(2,1)S(1)}, u32[]{:S(2)}) copy-start(bf16[48,16,128]{2,1,0:T(8,128)(2,1)S(1)} %collective-permute-done.8.refs_10_) | copy-start | bytes 589828
  244.1 17.6 %copy-start.9 = (bf16[48,32,128]{2,1,0:T(8,128)(2,1)}, bf16[48,32,128]{2,1,0:T(8,128)(2,1)S(1)}, u32[]{:S(2)}) copy-start(bf16[48,32,128]{2,1,0:T(8,128)(2,1)S(1)} %collective-permute-done.5.refs_7_) | copy-start | bytes 1179652
  244.1 17.6 %copy-start.10 = (bf16[48,32,128]{2,1,0:T(8,128)(2,1)}, bf16[48,32,128]{2,1,0:T(8,128)(2,1)S(1)}, u32[]{:S(2)}) copy-start(bf16[48,32,128]{2,1,0:T(8,128)(2,1)S(1)} %collective-permute-done.6.refs_8_) | copy-start | bytes 1179652
Sparse Core Ops, SparseCore 0:
  64.3 59.9 reduce-scatter.1
  211.6 50.0 all-gather.2

commit v8 on v7

--- a/solution.py
+++ b/solution.py
@@ -265,7 +265,9 @@
     w = degree_mixing_weight
     turned = jnp.concatenate([-w[..., CHAN:], w[..., :CHAN]], axis=-1)
     both = jnp.concatenate([w, turned], axis=1)
-    spectrum, wtab, table, both = lax.optimization_barrier((spectrum, wtab, table, both))
+    spectrum, wtab, ftab, table, both = lax.optimization_barrier(
+        (spectrum, wtab, ftab, table, both)
+    )
     spectrum = swap(spectrum, "lat").reshape(LATS, EACH, 2, ROWS, CHAN)
     spectrum = jnp.transpose(spectrum, (1, 0, 3, 2, 4)).reshape(EACH, 720, 2 * CHAN)
 

time: 279 us -> 277 us (level)
  blocking collectives: 47.6 us -> 65.3 us
  waiting for transfers between devices: 91.6 us -> 79.2 us
  starting transfers between devices: 56.7 us -> 51 us
    all_to_all x3 -> x4, blocking collectives: 47.6 us -> 65.3 us  [swap(): return lax.all_to_all(x, axis, split_axis=0, concat_axis=0, tiled=True)]
    all_to_all x3 -> x2, waiting for transfers between devices: 35.4 us -> 27.6 us  [swap(): return lax.all_to_all(x, axis, split_axis=0, concat_axis=0, tiled=True)]
    all_to_all x3 -> x2, starting transfers between devices: 24.9 us -> 19 us  [swap(): return lax.all_to_all(x, axis, split_axis=0, concat_axis=0, tiled=True)]
    reduce_scatter x1, waiting for transfers between devices: 37.5 us -> 33 us  [local(): spectrum = lax.psum_scatter(spectrum, 'lon', scatter_dimension=0)]
  transfers between devices with their start and end apart: 14 -> 13, of which waited for: 7 -> 6; matrix products, arithmetic and copies ran while one was open for 8% -> 8% of each run, Pallas kernels for 2% -> 2%
where the time goes in v8:
time: 277 us
  waiting for transfers between devices  79.2 us (29%)
  blocking collectives  65.3 us (24%)
  starting transfers between devices  51 us (18%)
  local copies, waits for them, and re-layouts  24.1 us (9%)
  Pallas kernels  23.4 us (8%)
  other arithmetic  15.7 us (6%)
  between operations  13.9 us (5%)
  matrix products  4.14 us (1%)
    all_to_all x4, blocking collectives, swap(): return lax.all_to_all(x, axis, split_axis=0, concat_axis=0, tiled=True)  65.3 us
    reduce_scatter x1, waiting for transfers between devices, local(): spectrum = lax.psum_scatter(spectrum, 'lon', scatter_dimension=0)  33 us
    all_to_all x2, waiting for transfers between devices, swap(): return lax.all_to_all(x, axis, split_axis=0, concat_axis=0, tiled=True)  27.6 us
    ppermute x5, starting transfers between devices, across(): return lax.ppermute(u, 'lon', [(i, i ^ 1) for i in range(8)])  26.2 us
    all_to_all x2, starting transfers between devices, swap(): return lax.all_to_all(x, axis, split_axis=0, concat_axis=0, tiled=True)  19 us
    all_gather x1, waiting for transfers between devices, local(): pieces = [lax.all_gather(rows, 'lon', axis=0)] + gather_lon(rest)  17.6 us
    unnamed x35, local copies, waits for them, and re-layouts  10.9 us
    convert_element_type x2, other arithmetic, waves(): return (jnp.cos(angles) * jnp.where(valid, factor, 0.0)).astype(BF)  10.2 us
  transfers between devices with their start and end apart: 13, of which 6 were waited for; matrix products, arithmetic and copies ran while one was open for 8% of the time, Pallas kernels for 2%

profile of v8, /device:TPU:1, one launch (start us, length us, event | category | flops | bytes accessed | tf_op | source)
XLA Modules:
  0.0 276.7 jit_solution(11252806873440325001)
XLA Ops:
  6.5 3.0 %copy.32 = bf16[46,45,720]{2,1,0:T(8,128)(2,1)S(1)} copy(bf16[46,45,720]{2,0,1:T(8,128)(2,1)} %param.5) | data formatting | bytes 5961600
  9.6 0.4 pad.4.clone
  10.0 3.0 %reshape.310 = bf16[16,135,720]{2,1,0:T(8,128)(2,1)} reshape(bf16[48,45,720]{2,1,0:T(8,128)(2,1)S(1)} %pad.4.clone) | data formatting | bytes 6220800 | tf_op jit(solution)/shard_map/reshape | solution.py:233
  12.9 8.6 %all-to-all-start = ((bf16[16,135,720]{2,1,0:T(8,128)(2,1)}), bf16[16,135,720]{2,1,0:T(8,128)(2,1)}, u32[]{:S(2)}, u32[]{:S(2)}) async-start(bf16[16,135,720]{2,1,0:T(8,128)(2,1)} %reshape.310), calls=%async_computation | async-start | bytes 6684672 | tf_op jit(solution)/shard_map/all_to_all | solution.py:40
  21.6 0.0 reduce-scatter.2.cloned.1.call-start
  21.6 0.0 copy-start
  21.6 2.3 copy-done
  23.9 2.3 shard_map.47
  26.2 0.0 copy-start.2
  26.2 2.1 copy-done.2
  28.3 3.8 %fusion.22.waves_in = bf16[768,180]{1,0:T(8,128)(2,1)S(1)} fusion(f32[768]{0:T(1024)S(1)} %fusion.41, s32[768]{0:T(1024)S(1)} %get-tuple-element.33, s32[180]{0:T(256)S(1)} %iota_add_fusion.1, s32[768]{0:T(1024)S(1)} %get-tuple-element.34), kind=kLoop, calls=%fused_computation.24 | loop fusion | flops 1658880 | bytes 286416 | tf_op jit(solution)/shard_map/convert_element_type | solution.py:36
  32.2 3.9 %shard_map.46 = bf16[8,45,96,96]{3,2,1,0:T(8,128)(2,1)S(1)} custom-call(bf16[768,180]{1,0:T(8,128)(2,1)S(1)} %fusion.22.waves_in, bf16[45,180,96]{2,1,0:T(8,128)(2,1)S(1)} %bitcast.24), custom_call_target="tpu_custom_call" | custom-call | tf_op jit(solution)/shard_map/pallas_call | solution.py:56
  36.1 3.5 %copy-done.1 = bf16[8,45,96,96]{3,2,1,0:T(8,128)(2,1)} copy-done((bf16[8,45,96,96]{3,2,1,0:T(8,128)(2,1)}, bf16[8,45,96,96]{3,2,1,0:T(8,128)(2,1)S(1)}, u32[]{:S(2)}) %copy-start.1) | copy-done | bytes 6635544
  39.6 24.5 %all-to-all-done = bf16[16,135,720]{2,1,0:T(8,128)(2,1)} async-done(((bf16[16,135,720]{2,1,0:T(8,128)(2,1)}), bf16[16,135,720]{2,1,0:T(8,128)(2,1)}, u32[]{:S(2)}, u32[]{:S(2)}) %all-to-all-start) | async-done | bytes 3110432 | tf_op jit(solution)/shard_map/all_to_all | solution.py:40
  64.2 0.0 reduce-scatter.2.cloned.1.call-update
  64.2 0.0 copy-start.5
  64.2 10.3 %all-to-all-start.1 = ((bf16[16,1088,128]{2,1,0:T(8,128)(2,1)}), bf16[16,1088,128]{2,1,0:T(8,128)(2,1)}, u32[]{:S(2)}, u32[]{:S(2)}) async-start(bf16[16,1088,128]{2,1,0:T(8,128)(2,1)} %copy-done.2), calls=%async_computation.2 | async-start | bytes 8912896 | tf_op jit(solution)/shard_map/all_to_all | solution.py:40
  74.5 0.2 all-gather.3.cloned.1.call-start
  74.8 0.1 concatenate.25
  75.0 0.1 concatenate.24
  75.2 0.1 concatenate.23
  75.3 0.5 slice_negate_fusion
  75.8 4.8 %maximum_maximum_fusion = bf16[45,192,192]{2,1,0:T(8,128)(2,1)} fusion(bf16[45,96,96]{2,1,0:T(8,128)(2,1)S(1)} %get-tuple-element.32, bf16[45,96,96]{2,1,0:T(8,128)(2,1)S(1)} %get-tuple-element.31, bf16[45,96,192]{2,1,0:T(8,128)(2,1)S(1)} %copy-done.5), kind=kLoop, calls=%fused_computation | loop fusion | flops 9953280 | bytes 6635520 | tf_op jit(solution)/shard_map/concatenate | solution.py:267
  80.7 4.3 %copy.20 = bf16[16,135,720]{2,0,1:T(8,128)(2,1)} copy(bf16[16,135,720]{2,1,0:T(8,128)(2,1)} %all-to-all-done) | data formatting | bytes 6220800 | tf_op jit(solution)/shard_map/optimization_barrier | solution.py:247
  85.0 6.4 %fusion.9.table = bf16[464,768]{1,0:T(8,128)(2,1)} fusion(f32[768]{0:T(1024)S(1)} %broadcast_select_fusion, s32[768]{0:T(1024)S(1)} %broadcast_multiply_fusion, s32[464]{0:T(512)S(1)} %iota_add_fusion, s32[768]{0:T(1024)S(1)} %concatenate.23), kind=kLoop, calls=%fused_computation.10 | loop fusion | flops 4276224 | bytes 723776 | tf_op jit(solution)/shard_map/convert_element_type | solution.py:36
  91.4 33.0 %reduce-scatter.2.cloned.1.call-done = bf16[1,45,96,96]{3,2,1,0:T(8,128)(2,1)} async-done(((bf16[8,45,96,96]{3,2,1,0:T(8,128)(2,1)}), bf16[1,45,96,96]{3,2,1,0:T(8,128)(2,1)}) %reduce-scatter.2.cloned.1.call-update) | async-done | bytes 829456 | tf_op jit(solution)/shard_map/reduce_scatter | solution.py:248
  124.3 1.7 copy.18
  126.0 0.3 copy.19
  126.3 3.0 %all-to-all-done.1.table = bf16[16,1088,128]{2,1,0:T(8,128)(2,1)} async-done(((bf16[16,1088,128]{2,1,0:T(8,128)(2,1)}), bf16[16,1088,128]{2,1,0:T(8,128)(2,1)}, u32[]{:S(2)}, u32[]{:S(2)}) %all-to-all-start.1) | async-done | bytes 4456480 | tf_op jit(solution)/shard_map/all_to_all | solution.py:40
  129.3 0.3 copy.21
  129.6 18.4 %all_to_all.30 = bf16[16,270,96]{2,1,0:T(8,128)(2,1)S(1)} all-to-all(bf16[16,270,96]{2,1,0:T(8,128)(2,1)S(1)} %copy.21), channel_id=1, replica_groups=mesh['lat'=16,'lon'=8] {'lat'}, dimensions={0} | all-to-all | bytes 1658880 | tf_op jit(solution)/shard_map/all_to_all | solution.py:40
  148.0 0.3 copy.22
  148.3 0.9 copy.23
  149.2 0.0 slice-start
  149.2 0.7 reshape.323
  149.9 0.0 slice-start.1
  149.9 3.4 %fusion.13 = bf16[16,3,45,192]{3,2,0,1:T(8,128)(2,1)S(1)} fusion(bf16[3,720,192,1]{2,1,3,0:T(8,128)(2,1)S(1)} %reshape.323, bf16[16,3,45,720]{3,0,2,1:T(8,128)(2,1)} %bitcast.34), kind=kOutput, calls=%fused_computation.15 | convolution fusion | flops 597611520 | bytes 4769280 | tf_op jit(solution)/shard_map/ajlq,jqn->ajln/dot_general | solution.py:274
  153.3 0.1 copy.26
  153.4 15.7 %all_to_all.31 = bf16[16,3,45,192]{3,2,1,0:T(8,128)(2,1)S(1)} all-to-all(bf16[16,3,45,192]{3,2,1,0:T(8,128)(2,1)S(1)} %copy.26), channel_id=1, replica_groups=mesh['lat'=16,'lon'=8] {'lat'}, dimensions={0} | all-to-all | bytes 1658880 | tf_op jit(solution)/shard_map/all_to_all | solution.py:40
  169.1 0.8 fusion.16
  169.9 0.4 copy.28
  170.2 15.7 %all_to_all.32 = bf16[16,3,45,192]{3,2,1,0:T(8,128)(2,1)S(1)} all-to-all(bf16[16,3,45,192]{3,2,1,0:T(8,128)(2,1)S(1)} %bitcast.29), channel_id=1, replica_groups=mesh['lat'=16,'lon'=8] {'lat'}, dimensions={0} | all-to-all | bytes 1658880 | tf_op jit(solution)/shard_map/all_to_all | solution.py:40
  185.9 0.1 copy.29
  186.0 0.6 reshape.317.mixed
  186.6 4.5 %shard_map.48 = bf16[16,288,128]{2,1,0:T(8,128)(2,1)S(1)} custom-call(bf16[3,720,192]{2,1,0:T(8,128)(2,1)S(1)} %reshape.317.mixed, bf16[16,1088,128]{2,1,0:T(8,128)(2,1)} %all-to-all-done.1.table), custom_call_target="tpu_custom_call" | custom-call | flops 849346560 | bytes 6000000 | tf_op jit(solution)/shard_map/pallas_call | solution.py:138
  191.1 15.5 %all_to_all.33.rows = bf16[16,288,128]{2,1,0:T(8,128)(2,1)S(1)} all-to-all(bf16[16,288,128]{2,1,0:T(8,128)(2,1)S(1)} %shard_map.48), channel_id=1, replica_groups=mesh['lat'=16,'lon'=8] {'lat'}, dimensions={0} | all-to-all | bytes 2359296 | tf_op jit(solution)/shard_map/all_to_all | solution.py:40
  206.5 3.3 %shard_map.49 = (bf16[48,64,128]{2,1,0:T(8,128)(2,1)}, bf16[48,32,128]{2,1,0:T(8,128)(2,1)S(1)}) custom-call(bf16[16,288,128]{2,1,0:T(8,128)(2,1)S(1)} %all_to_all.33.rows), custom_call_target="tpu_custom_call" | custom-call | tf_op jit(solution)/shard_map/pallas_call | solution.py:161
  209.8 0.0 all-gather.3.cloned.1.call-update
  209.8 1.3 collective-permute-start
  211.1 1.5 collective-permute-start.1
  212.6 10.2 %collective-permute-start.4 = (bf16[48,32,128]{2,1,0:T(8,128)(2,1)S(1)}, bf16[48,32,128]{2,1,0:T(8,128)(2,1)S(1)}, u32[]{:S(2)}, u32[]{:S(2)}) collective-permute-start(bf16[48,32,128]{2,1,0:T(8,128)(2,1)S(1)} %get-tuple-element.30.refs_1_), channel_id=1, source_target_pairs={{0,1},{1,0},{2,3},{3,2},{4,5},{5,4},{6,7},{7,6},{8,9},{9,8},{10,11... | collective-permute-start | bytes 1179656 | tf_op jit(solution)/shard_map/ppermute | solution.py:222
  222.8 0.0 collective-permute-done.refs_2_
  222.8 0.1 collective-permute-start.2
  222.9 2.7 collective-permute-start.3
  225.7 8.6 %collective-permute-start.5 = (bf16[48,32,128]{2,1,0:T(8,128)(2,1)S(1)}, bf16[48,32,128]{2,1,0:T(8,128)(2,1)S(1)}, u32[]{:S(2)}, u32[]{:S(2)}) collective-permute-start(bf16[48,32,128]{2,1,0:T(8,128)(2,1)S(1)} %collective-permute-done.refs_2_), channel_id=1, source_target_pairs={{0,1},{1,0},{2,3},{3,2},{4,5},{5,4},{6,7},{7,6},{8,9},{9,8},{10,11... | collective-permute-start | bytes 1179656 | tf_op jit(solution)/shard_map/ppermute | solution.py:222
  234.3 0.0 collective-permute-start.6
  234.3 0.0 collective-permute-done.2.refs_4_
  234.3 6.7 %collective-permute-start.7 = (bf16[48,16,128]{2,1,0:T(8,128)(2,1)S(1)}, bf16[48,16,128]{2,1,0:T(8,128)(2,1)S(1)}, u32[]{:S(2)}, u32[]{:S(2)}) collective-permute-start(bf16[48,16,128]{2,1,0:T(8,128)(2,1)S(1)} %collective-permute-done.2.refs_4_), channel_id=1, source_target_pairs={{0,1},{1,0},{2,3},{3,2},{4,5},{5,4},{6,7},{7,6},{8,9},{9,8},{10,11... | collective-permute-start | bytes 589832 | tf_op jit(solution)/shard_map/ppermute | solution.py:222
  241.0 0.7 collective-permute-start.8
  241.6 0.0 collective-permute-done.4.refs_6_
  241.6 0.4 collective-permute-done.7.refs_9_
  242.0 0.7 collective-permute-done.8.refs_10_
  242.7 17.6 %all-gather.3.cloned.1.call-done = bf16[384,64,128]{2,1,0:T(8,128)(2,1)} async-done(((bf16[48,64,128]{2,1,0:T(8,128)(2,1)}), bf16[384,64,128]{2,1,0:T(8,128)(2,1)}) %all-gather.3.cloned.1.call-update) | async-done | bytes 6291472 | tf_op jit(solution)/shard_map/all_gather | solution.py:281
  260.4 9.5 %shard_map.50 = bf16[2,48,64,450]{3,2,1,0:T(8,128)(2,1)} custom-call(bf16[464,768]{1,0:T(8,128)(2,1)} %fusion.9.table, bf16[8,48,64,128]{3,2,1,0:T(8,128)(2,1)} %bitcast.27, bf16[48,32,128]{2,1,0:T(8,128)(2,1)} %copy-done.4, bf16[48,32,128]{2,1,0:T(8,128)(2,1)} %copy-done.6, bf16[48,32,128]{2,1,0:T(8,128)(2,1)} %copy-done.7, ...), custom_call_target="tpu_custom_call" | custom-call | tf_op jit(solution)/shard_map/pallas_call | solution.py:198
  (55 shorter events, 0.2 us)
Async XLA Ops:
  12.9 51.2 %all-to-all-start = ((bf16[16,135,720]{2,1,0:T(8,128)(2,1)}), bf16[16,135,720]{2,1,0:T(8,128)(2,1)}, u32[]{:S(2)}, u32[]{:S(2)}) async-start(bf16[16,135,720]{2,1,0:T(8,128)(2,1)} %reshape.310), calls=%async_computation | async-start | bytes 6684672 | tf_op jit(solution)/shard_map/all_to_all | solution.py:40
  21.6 102.7 %reduce-scatter.2.cloned.1.call-start = ((), (), s32[]{:S(2)}) async-start(), calls=%async_computation.7 | async-start | bytes 9953280 | tf_op jit(solution)/shard_map/reduce_scatter | solution.py:248
  21.6 2.3 copy-start
  23.9 8.3 %copy-start.3 = (bf16[96,45,180]{0,2,1:T(8,128)(2,1)S(1)}, bf16[96,45,180]{0,2,1:T(8,128)(2,1)}, u32[]{:S(2)}) copy-start(bf16[96,45,180]{0,2,1:T(8,128)(2,1)} %param.4) | copy-start | bytes 4665604
  26.2 2.1 copy-start.2
  36.1 3.5 %copy-start.1 = (bf16[8,45,96,96]{3,2,1,0:T(8,128)(2,1)}, bf16[8,45,96,96]{3,2,1,0:T(8,128)(2,1)S(1)}, u32[]{:S(2)}) copy-start(bf16[8,45,96,96]{3,2,1,0:T(8,128)(2,1)S(1)} %shard_map.46) | copy-start | bytes 19906564
  64.2 11.1 %copy-start.5 = (bf16[45,96,192]{2,1,0:T(8,128)(2,1)S(1)}, bf16[45,96,192]{2,1,0:T(8,128)(2,1)}, u32[]{:S(2)}) copy-start(bf16[45,96,192]{2,1,0:T(8,128)(2,1)} %param.6) | copy-start | bytes 4976644
  64.2 65.1 %all-to-all-start.1 = ((bf16[16,1088,128]{2,1,0:T(8,128)(2,1)}), bf16[16,1088,128]{2,1,0:T(8,128)(2,1)}, u32[]{:S(2)}, u32[]{:S(2)}) async-start(bf16[16,1088,128]{2,1,0:T(8,128)(2,1)} %copy-done.2), calls=%async_computation.2 | async-start | bytes 8912896 | tf_op jit(solution)/shard_map/all_to_all | solution.py:40
  74.5 185.8 %all-gather.3.cloned.1.call-start = ((), (), s32[]{:S(2)}) async-start(), calls=%async_computation.8 | async-start | bytes 7077888 | tf_op jit(solution)/shard_map/all_gather | solution.py:281
  149.2 19.9 %slice-start = ((s8[4423680]{0:T(1024)(128)(4,1)}), s8[229376]{0:T(1024)(128)(4,1)S(1)}, s32[]{:S(2)}) async-start(s8[4423680]{0:T(1024)(128)(4,1)} %bitcast.25), calls=%async_computation.9 | async-start | bytes 458752
  149.9 19.1 %slice-start.1 = ((s8[4423680]{0:T(1024)(128)(4,1)}), s8[4194304]{0:T(1024)(128)(4,1)S(1)}, s32[]{:S(2)}) async-start(s8[4423680]{0:T(1024)(128)(4,1)} %bitcast.25), calls=%async_computation.10 | async-start | bytes 8388608
  209.8 50.5 %copy-start.4 = (bf16[48,32,128]{2,1,0:T(8,128)(2,1)}, bf16[48,32,128]{2,1,0:T(8,128)(2,1)S(1)}, u32[]{:S(2)}) copy-start(bf16[48,32,128]{2,1,0:T(8,128)(2,1)S(1)} %get-tuple-element.30.refs_1_) | copy-start | bytes 1179652
  209.8 13.0 %collective-permute-start = (bf16[48,32,128]{2,1,0:T(8,128)(2,1)S(1)}, bf16[48,32,128]{2,1,0:T(8,128)(2,1)S(1)}, u32[]{:S(2)}, u32[]{:S(2)}) collective-permute-start(bf16[48,32,128]{2,1,0:T(8,128)(2,1)S(1)} %get-tuple-element.30.refs_1_), channel_id=1, source_target_pairs={{0,2},{1,3},{2,4},{3,5},{4,6},{5,7},{6,0},{7,1},{8,10},{9,11},{10,... | collective-permute-start | bytes 1179656 | tf_op jit(solution)/shard_map/ppermute | solution.py:219
  211.1 11.8 %collective-permute-start.1 = (bf16[48,32,128]{2,1,0:T(8,128)(2,1)S(1)}, bf16[48,32,128]{2,1,0:T(8,128)(2,1)S(1)}, u32[]{:S(2)}, u32[]{:S(2)}) collective-permute-start(bf16[48,32,128]{2,1,0:T(8,128)(2,1)S(1)} %get-tuple-element.30.refs_1_), channel_id=1, source_target_pairs={{0,6},{1,7},{2,0},{3,1},{4,2},{5,3},{6,4},{7,5},{8,14},{9,15},{10,... | collective-permute-start | bytes 1179656 | tf_op jit(solution)/shard_map/ppermute | solution.py:219
  212.6 29.1 %collective-permute-start.4 = (bf16[48,32,128]{2,1,0:T(8,128)(2,1)S(1)}, bf16[48,32,128]{2,1,0:T(8,128)(2,1)S(1)}, u32[]{:S(2)}, u32[]{:S(2)}) collective-permute-start(bf16[48,32,128]{2,1,0:T(8,128)(2,1)S(1)} %get-tuple-element.30.refs_1_), channel_id=1, source_target_pairs={{0,1},{1,0},{2,3},{3,2},{4,5},{5,4},{6,7},{7,6},{8,9},{9,8},{10,11... | collective-permute-start | bytes 1179656 | tf_op jit(solution)/shard_map/ppermute | solution.py:222
  222.8 37.5 %copy-start.6 = (bf16[48,32,128]{2,1,0:T(8,128)(2,1)}, bf16[48,32,128]{2,1,0:T(8,128)(2,1)S(1)}, u32[]{:S(2)}) copy-start(bf16[48,32,128]{2,1,0:T(8,128)(2,1)S(1)} %collective-permute-done.refs_2_) | copy-start | bytes 1179652
  222.8 11.5 %collective-permute-start.2 = (bf16[48,16,128]{2,1,0:T(8,128)(2,1)S(1)}, bf16[48,16,128]{2,1,0:T(8,128)(2,1)S(1)}, u32[]{:S(2)}, u32[]{:S(2)}) collective-permute-start(bf16[48,16,128]{2,1,0:T(8,128)(2,1)S(1)} %slice.16), channel_id=1, source_target_pairs={{0,2},{1,3},{2,4},{3,5},{4,6},{5,7},{6,0},{7,1},{8,10},{9,11},{10,... | collective-permute-start | bytes 589832 | tf_op jit(solution)/shard_map/ppermute | solution.py:219
  222.9 37.4 %copy-start.7 = (bf16[48,32,128]{2,1,0:T(8,128)(2,1)}, bf16[48,32,128]{2,1,0:T(8,128)(2,1)S(1)}, u32[]{:S(2)}) copy-start(bf16[48,32,128]{2,1,0:T(8,128)(2,1)S(1)} %collective-permute-done.1.refs_3_) | copy-start | bytes 1179652
  222.9 18.0 %collective-permute-start.3 = (bf16[48,16,128]{2,1,0:T(8,128)(2,1)S(1)}, bf16[48,16,128]{2,1,0:T(8,128)(2,1)S(1)}, u32[]{:S(2)}, u32[]{:S(2)}) collective-permute-start(bf16[48,16,128]{2,1,0:T(8,128)(2,1)S(1)} %slice.17), channel_id=1, source_target_pairs={{0,6},{1,7},{2,0},{3,1},{4,2},{5,3},{6,4},{7,5},{8,14},{9,15},{10,... | collective-permute-start | bytes 589832 | tf_op jit(solution)/shard_map/ppermute | solution.py:219
  225.7 17.1 %collective-permute-start.5 = (bf16[48,32,128]{2,1,0:T(8,128)(2,1)S(1)}, bf16[48,32,128]{2,1,0:T(8,128)(2,1)S(1)}, u32[]{:S(2)}, u32[]{:S(2)}) collective-permute-start(bf16[48,32,128]{2,1,0:T(8,128)(2,1)S(1)} %collective-permute-done.refs_2_), channel_id=1, source_target_pairs={{0,1},{1,0},{2,3},{3,2},{4,5},{5,4},{6,7},{7,6},{8,9},{9,8},{10,11... | collective-permute-start | bytes 1179656 | tf_op jit(solution)/shard_map/ppermute | solution.py:222
  234.3 8.5 %collective-permute-start.6 = (bf16[48,32,128]{2,1,0:T(8,128)(2,1)S(1)}, bf16[48,32,128]{2,1,0:T(8,128)(2,1)S(1)}, u32[]{:S(2)}, u32[]{:S(2)}) collective-permute-start(bf16[48,32,128]{2,1,0:T(8,128)(2,1)S(1)} %collective-permute-done.1.refs_3_), channel_id=1, source_target_pairs={{0,1},{1,0},{2,3},{3,2},{4,5},{5,4},{6,7},{7,6},{8,9},{9,8},{10,11... | collective-permute-start | bytes 1179656 | tf_op jit(solution)/shard_map/ppermute | solution.py:222
  234.3 26.0 %copy-start.11 = (bf16[48,16,128]{2,1,0:T(8,128)(2,1)}, bf16[48,16,128]{2,1,0:T(8,128)(2,1)S(1)}, u32[]{:S(2)}) copy-start(bf16[48,16,128]{2,1,0:T(8,128)(2,1)S(1)} %collective-permute-done.2.refs_4_) | copy-start | bytes 589828
  234.3 7.8 %collective-permute-start.7 = (bf16[48,16,128]{2,1,0:T(8,128)(2,1)S(1)}, bf16[48,16,128]{2,1,0:T(8,128)(2,1)S(1)}, u32[]{:S(2)}, u32[]{:S(2)}) collective-permute-start(bf16[48,16,128]{2,1,0:T(8,128)(2,1)S(1)} %collective-permute-done.2.refs_4_), channel_id=1, source_target_pairs={{0,1},{1,0},{2,3},{3,2},{4,5},{5,4},{6,7},{7,6},{8,9},{9,8},{10,11... | collective-permute-start | bytes 589832 | tf_op jit(solution)/shard_map/ppermute | solution.py:222
  241.0 19.3 %copy-start.12 = (bf16[48,16,128]{2,1,0:T(8,128)(2,1)}, bf16[48,16,128]{2,1,0:T(8,128)(2,1)S(1)}, u32[]{:S(2)}) copy-start(bf16[48,16,128]{2,1,0:T(8,128)(2,1)S(1)} %collective-permute-done.3.refs_5_) | copy-start | bytes 589828
  241.0 1.7 collective-permute-start.8
  241.6 18.7 %copy-start.8 = (bf16[48,32,128]{2,1,0:T(8,128)(2,1)}, bf16[48,32,128]{2,1,0:T(8,128)(2,1)S(1)}, u32[]{:S(2)}) copy-start(bf16[48,32,128]{2,1,0:T(8,128)(2,1)S(1)} %collective-permute-done.4.refs_6_) | copy-start | bytes 1179652
  242.0 18.3 %copy-start.13 = (bf16[48,16,128]{2,1,0:T(8,128)(2,1)}, bf16[48,16,128]{2,1,0:T(8,128)(2,1)S(1)}, u32[]{:S(2)}) copy-start(bf16[48,16,128]{2,1,0:T(8,128)(2,1)S(1)} %collective-permute-done.7.refs_9_) | copy-start | bytes 589828
  242.7 17.6 %copy-start.14 = (bf16[48,16,128]{2,1,0:T(8,128)(2,1)}, bf16[48,16,128]{2,1,0:T(8,128)(2,1)S(1)}, u32[]{:S(2)}) copy-start(bf16[48,16,128]{2,1,0:T(8,128)(2,1)S(1)} %collective-permute-done.8.refs_10_) | copy-start | bytes 589828
  242.7 17.6 %copy-start.9 = (bf16[48,32,128]{2,1,0:T(8,128)(2,1)}, bf16[48,32,128]{2,1,0:T(8,128)(2,1)S(1)}, u32[]{:S(2)}) copy-start(bf16[48,32,128]{2,1,0:T(8,128)(2,1)S(1)} %collective-permute-done.5.refs_7_) | copy-start | bytes 1179652
  242.7 17.6 %copy-start.10 = (bf16[48,32,128]{2,1,0:T(8,128)(2,1)}, bf16[48,32,128]{2,1,0:T(8,128)(2,1)S(1)}, u32[]{:S(2)}) copy-start(bf16[48,32,128]{2,1,0:T(8,128)(2,1)S(1)} %collective-permute-done.6.refs_8_) | copy-start | bytes 1179652
Sparse Core Ops, SparseCore 0:
  64.3 59.9 reduce-scatter.1
  209.9 50.3 all-gather.2

commit v9 on v8

--- a/solution.py
+++ b/solution.py
@@ -272,7 +272,8 @@
     spectrum = jnp.transpose(spectrum, (1, 0, 3, 2, 4)).reshape(EACH, 720, 2 * CHAN)
 
     coef = jnp.einsum("ajlq,jqn->ajln", ftab, spectrum, preferred_element_type=jnp.float32)
-    coef = swap(coef.astype(BF), "lat").reshape(SLOTS, ROWS, 2 * CHAN)
+    coef = coef.astype(BF).reshape(LATS, EACH * ROWS, 2 * CHAN)
+    coef = swap(coef, "lat").reshape(SLOTS, ROWS, 2 * CHAN)
 
     mixed = jnp.einsum("mlt,ltu->mlu", coef, both, preferred_element_type=jnp.float32)
     mixed = swap(mixed.astype(BF).reshape(LATS, EACH, ROWS, 2 * CHAN), "lat")

time: 277 us -> 280 us (1.011)
    unnamed x35 -> x31, local copies, waits for them, and re-layouts: 10.9 us -> 10.9 us
where the time goes in v9:
time: 280 us
  waiting for transfers between devices  79.2 us (28%)
  blocking collectives  64.9 us (23%)
  starting transfers between devices  51 us (18%)
  local copies, waits for them, and re-layouts  25.2 us (9%)
  Pallas kernels  23.4 us (8%)
  other arithmetic  15.7 us (6%)
  between operations  13.9 us (5%)
  matrix products  6.24 us (2%)
    all_to_all x4, blocking collectives, swap(): return lax.all_to_all(x, axis, split_axis=0, concat_axis=0, tiled=True)  64.9 us
    reduce_scatter x1, waiting for transfers between devices, local(): spectrum = lax.psum_scatter(spectrum, 'lon', scatter_dimension=0)  33 us
    all_to_all x2, waiting for transfers between devices, swap(): return lax.all_to_all(x, axis, split_axis=0, concat_axis=0, tiled=True)  27.6 us
    ppermute x5, starting transfers between devices, across(): return lax.ppermute(u, 'lon', [(i, i ^ 1) for i in range(8)])  26.2 us
    all_to_all x2, starting transfers between devices, swap(): return lax.all_to_all(x, axis, split_axis=0, concat_axis=0, tiled=True)  19 us
    all_gather x1, waiting for transfers between devices, local(): pieces = [lax.all_gather(rows, 'lon', axis=0)] + gather_lon(rest)  17.6 us
    unnamed x31, local copies, waits for them, and re-layouts  10.9 us
    convert_element_type x2, other arithmetic, waves(): return (jnp.cos(angles) * jnp.where(valid, factor, 0.0)).astype(BF)  10.2 us
  transfers between devices with their start and end apart: 13, of which 6 were waited for; matrix products, arithmetic and copies ran while one was open for 8% of the time, Pallas kernels for 2%

profile of v9, /device:TPU:1, one launch (start us, length us, event | category | flops | bytes accessed | tf_op | source)
XLA Modules:
  0.0 279.5 jit_solution(14849440258159252475)
XLA Ops:
  6.5 3.0 %copy.34 = bf16[46,45,720]{2,1,0:T(8,128)(2,1)S(1)} copy(bf16[46,45,720]{2,0,1:T(8,128)(2,1)} %param.5) | data formatting | bytes 5961600
  9.6 0.4 pad.4.clone
  10.0 3.0 %reshape.313 = bf16[16,135,720]{2,1,0:T(8,128)(2,1)} reshape(bf16[48,45,720]{2,1,0:T(8,128)(2,1)S(1)} %pad.4.clone) | data formatting | bytes 6220800 | tf_op jit(solution)/shard_map/reshape | solution.py:233
  12.9 8.6 %all-to-all-start = ((bf16[16,135,720]{2,1,0:T(8,128)(2,1)}), bf16[16,135,720]{2,1,0:T(8,128)(2,1)}, u32[]{:S(2)}, u32[]{:S(2)}) async-start(bf16[16,135,720]{2,1,0:T(8,128)(2,1)} %reshape.313), calls=%async_computation | async-start | bytes 6684672 | tf_op jit(solution)/shard_map/all_to_all | solution.py:40
  21.6 0.0 reduce-scatter.2.cloned.1.call-start
  21.6 0.0 copy-start
  21.6 2.3 copy-done
  23.9 2.3 shard_map.47
  26.2 0.0 copy-start.2
  26.2 2.1 copy-done.2
  28.3 3.8 %fusion.22.waves_in = bf16[768,180]{1,0:T(8,128)(2,1)S(1)} fusion(f32[768]{0:T(1024)S(1)} %fusion.41, s32[768]{0:T(1024)S(1)} %get-tuple-element.33, s32[180]{0:T(256)S(1)} %iota_add_fusion.1, s32[768]{0:T(1024)S(1)} %get-tuple-element.34), kind=kLoop, calls=%fused_computation.24 | loop fusion | flops 1658880 | bytes 286416 | tf_op jit(solution)/shard_map/convert_element_type | solution.py:36
  32.2 3.9 %shard_map.46 = bf16[8,45,96,96]{3,2,1,0:T(8,128)(2,1)S(1)} custom-call(bf16[768,180]{1,0:T(8,128)(2,1)S(1)} %fusion.22.waves_in, bf16[45,180,96]{2,1,0:T(8,128)(2,1)S(1)} %bitcast.24), custom_call_target="tpu_custom_call" | custom-call | tf_op jit(solution)/shard_map/pallas_call | solution.py:56
  36.1 3.4 %copy-done.1 = bf16[8,45,96,96]{3,2,1,0:T(8,128)(2,1)} copy-done((bf16[8,45,96,96]{3,2,1,0:T(8,128)(2,1)}, bf16[8,45,96,96]{3,2,1,0:T(8,128)(2,1)S(1)}, u32[]{:S(2)}) %copy-start.1) | copy-done | bytes 6635544
  39.6 24.6 %all-to-all-done = bf16[16,135,720]{2,1,0:T(8,128)(2,1)} async-done(((bf16[16,135,720]{2,1,0:T(8,128)(2,1)}), bf16[16,135,720]{2,1,0:T(8,128)(2,1)}, u32[]{:S(2)}, u32[]{:S(2)}) %all-to-all-start) | async-done | bytes 3110432 | tf_op jit(solution)/shard_map/all_to_all | solution.py:40
  64.1 0.0 reduce-scatter.2.cloned.1.call-update
  64.2 0.0 copy-start.5
  64.2 10.3 %all-to-all-start.1 = ((bf16[16,1088,128]{2,1,0:T(8,128)(2,1)}), bf16[16,1088,128]{2,1,0:T(8,128)(2,1)}, u32[]{:S(2)}, u32[]{:S(2)}) async-start(bf16[16,1088,128]{2,1,0:T(8,128)(2,1)} %copy-done.2), calls=%async_computation.2 | async-start | bytes 8912896 | tf_op jit(solution)/shard_map/all_to_all | solution.py:40
  74.5 0.2 all-gather.3.cloned.1.call-start
  74.8 0.1 concatenate.25
  75.0 0.1 concatenate.24
  75.2 0.1 concatenate.23
  75.3 0.5 slice_negate_fusion
  75.8 4.8 %maximum_maximum_fusion = bf16[45,192,192]{2,1,0:T(8,128)(2,1)} fusion(bf16[45,96,96]{2,1,0:T(8,128)(2,1)S(1)} %get-tuple-element.32, bf16[45,96,96]{2,1,0:T(8,128)(2,1)S(1)} %get-tuple-element.31, bf16[45,96,192]{2,1,0:T(8,128)(2,1)S(1)} %copy-done.5), kind=kLoop, calls=%fused_computation | loop fusion | flops 9953280 | bytes 6635520 | tf_op jit(solution)/shard_map/concatenate | solution.py:267
  80.6 4.3 %copy.21 = bf16[16,135,720]{2,0,1:T(8,128)(2,1)} copy(bf16[16,135,720]{2,1,0:T(8,128)(2,1)} %all-to-all-done) | data formatting | bytes 6220800 | tf_op jit(solution)/shard_map/optimization_barrier | solution.py:247
  84.9 6.4 %fusion.9.table = bf16[464,768]{1,0:T(8,128)(2,1)} fusion(f32[768]{0:T(1024)S(1)} %broadcast_select_fusion, s32[768]{0:T(1024)S(1)} %broadcast_multiply_fusion, s32[464]{0:T(512)S(1)} %iota_add_fusion, s32[768]{0:T(1024)S(1)} %concatenate.23), kind=kLoop, calls=%fused_computation.10 | loop fusion | flops 4276224 | bytes 723776 | tf_op jit(solution)/shard_map/convert_element_type | solution.py:36
  91.4 33.0 %reduce-scatter.2.cloned.1.call-done = bf16[1,45,96,96]{3,2,1,0:T(8,128)(2,1)} async-done(((bf16[8,45,96,96]{3,2,1,0:T(8,128)(2,1)}), bf16[1,45,96,96]{3,2,1,0:T(8,128)(2,1)}) %reduce-scatter.2.cloned.1.call-update) | async-done | bytes 829456 | tf_op jit(solution)/shard_map/reduce_scatter | solution.py:248
  124.3 1.7 copy.19
  126.0 0.3 copy.20
  126.3 3.0 %all-to-all-done.1.table = bf16[16,1088,128]{2,1,0:T(8,128)(2,1)} async-done(((bf16[16,1088,128]{2,1,0:T(8,128)(2,1)}), bf16[16,1088,128]{2,1,0:T(8,128)(2,1)}, u32[]{:S(2)}, u32[]{:S(2)}) %all-to-all-start.1) | async-done | bytes 4456480 | tf_op jit(solution)/shard_map/all_to_all | solution.py:40
  129.3 0.3 copy.22
  129.6 18.4 %all_to_all.30 = bf16[16,270,96]{2,1,0:T(8,128)(2,1)S(1)} all-to-all(bf16[16,270,96]{2,1,0:T(8,128)(2,1)S(1)} %copy.22), channel_id=1, replica_groups=mesh['lat'=16,'lon'=8] {'lat'}, dimensions={0} | all-to-all | bytes 1658880 | tf_op jit(solution)/shard_map/all_to_all | solution.py:40
  148.0 0.3 copy.23
  148.3 0.9 copy.24
  149.2 0.7 reshape.327
  149.9 3.2 %fusion.13 = bf16[16,3,45,192]{3,2,0,1:T(8,128)(2,1)S(1)} fusion(bf16[3,720,192,1]{2,1,3,0:T(8,128)(2,1)S(1)} %reshape.327, bf16[16,3,45,720]{3,0,2,1:T(8,128)(2,1)} %bitcast.32), kind=kOutput, calls=%fused_computation.15 | convolution fusion | flops 597611520 | bytes 4769280 | tf_op jit(solution)/shard_map/ajlq,jqn->ajln/dot_general | solution.py:274
  153.1 0.4 copy.27
  153.5 0.4 copy.28
  153.9 15.5 %all_to_all.31 = bf16[16,135,192]{2,1,0:T(8,128)(2,1)S(1)} all-to-all(bf16[16,135,192]{2,1,0:T(8,128)(2,1)S(1)} %copy.28), channel_id=1, replica_groups=mesh['lat'=16,'lon'=8] {'lat'}, dimensions={0} | all-to-all | bytes 1658880 | tf_op jit(solution)/shard_map/all_to_all | solution.py:40
  169.3 0.5 reshape.319
  169.8 3.0 %fusion.16 = bf16[48,45,192]{2,0,1:T(8,128)(2,1)S(1)} fusion(bf16[45,192,192]{2,1,0:T(8,128)(2,1)} %maximum_maximum_fusion, bf16[48,45,192]{2,1,0:T(8,128)(2,1)S(1)} %reshape.319), kind=kOutput, calls=%fused_computation.16 | convolution fusion | flops 159667200 | bytes 4976640 | tf_op jit(solution)/shard_map/mlt,ltu->mlu/dot_general | solution.py:278
  172.9 0.4 copy.30
  173.2 15.6 %all_to_all.32 = bf16[16,3,45,192]{3,2,1,0:T(8,128)(2,1)S(1)} all-to-all(bf16[16,3,45,192]{3,2,1,0:T(8,128)(2,1)S(1)} %bitcast.27), channel_id=1, replica_groups=mesh['lat'=16,'lon'=8] {'lat'}, dimensions={0} | all-to-all | bytes 1658880 | tf_op jit(solution)/shard_map/all_to_all | solution.py:40
  188.8 0.1 copy.31
  188.9 0.6 reshape.321.mixed
  189.5 4.5 %shard_map.48 = bf16[16,288,128]{2,1,0:T(8,128)(2,1)S(1)} custom-call(bf16[3,720,192]{2,1,0:T(8,128)(2,1)S(1)} %reshape.321.mixed, bf16[16,1088,128]{2,1,0:T(8,128)(2,1)} %all-to-all-done.1.table), custom_call_target="tpu_custom_call" | custom-call | flops 849346560 | bytes 6000000 | tf_op jit(solution)/shard_map/pallas_call | solution.py:138
  193.9 15.5 %all_to_all.33.rows = bf16[16,288,128]{2,1,0:T(8,128)(2,1)S(1)} all-to-all(bf16[16,288,128]{2,1,0:T(8,128)(2,1)S(1)} %shard_map.48), channel_id=1, replica_groups=mesh['lat'=16,'lon'=8] {'lat'}, dimensions={0} | all-to-all | bytes 2359296 | tf_op jit(solution)/shard_map/all_to_all | solution.py:40
  209.4 3.3 %shard_map.49 = (bf16[48,64,128]{2,1,0:T(8,128)(2,1)}, bf16[48,32,128]{2,1,0:T(8,128)(2,1)S(1)}) custom-call(bf16[16,288,128]{2,1,0:T(8,128)(2,1)S(1)} %all_to_all.33.rows), custom_call_target="tpu_custom_call" | custom-call | tf_op jit(solution)/shard_map/pallas_call | solution.py:161
  212.7 0.0 all-gather.3.cloned.1.call-update
  212.7 1.3 collective-permute-start
  214.0 1.5 collective-permute-start.1
  215.4 10.2 %collective-permute-start.4 = (bf16[48,32,128]{2,1,0:T(8,128)(2,1)S(1)}, bf16[48,32,128]{2,1,0:T(8,128)(2,1)S(1)}, u32[]{:S(2)}, u32[]{:S(2)}) collective-permute-start(bf16[48,32,128]{2,1,0:T(8,128)(2,1)S(1)} %get-tuple-element.30.refs_1_), channel_id=1, source_target_pairs={{0,1},{1,0},{2,3},{3,2},{4,5},{5,4},{6,7},{7,6},{8,9},{9,8},{10,11... | collective-permute-start | bytes 1179656 | tf_op jit(solution)/shard_map/ppermute | solution.py:222
  225.7 0.0 collective-permute-done.refs_2_
  225.7 0.1 collective-permute-start.2
  225.8 0.0 collective-permute-done.1.refs_3_
  225.8 2.7 collective-permute-start.3
  228.5 8.6 %collective-permute-start.5 = (bf16[48,32,128]{2,1,0:T(8,128)(2,1)S(1)}, bf16[48,32,128]{2,1,0:T(8,128)(2,1)S(1)}, u32[]{:S(2)}, u32[]{:S(2)}) collective-permute-start(bf16[48,32,128]{2,1,0:T(8,128)(2,1)S(1)} %collective-permute-done.refs_2_), channel_id=1, source_target_pairs={{0,1},{1,0},{2,3},{3,2},{4,5},{5,4},{6,7},{7,6},{8,9},{9,8},{10,11... | collective-permute-start | bytes 1179656 | tf_op jit(solution)/shard_map/ppermute | solution.py:222
  237.1 0.0 collective-permute-start.6
  237.1 0.0 collective-permute-done.2.refs_4_
  237.1 6.7 %collective-permute-start.7 = (bf16[48,16,128]{2,1,0:T(8,128)(2,1)S(1)}, bf16[48,16,128]{2,1,0:T(8,128)(2,1)S(1)}, u32[]{:S(2)}, u32[]{:S(2)}) collective-permute-start(bf16[48,16,128]{2,1,0:T(8,128)(2,1)S(1)} %collective-permute-done.2.refs_4_), channel_id=1, source_target_pairs={{0,1},{1,0},{2,3},{3,2},{4,5},{5,4},{6,7},{7,6},{8,9},{9,8},{10,11... | collective-permute-start | bytes 589832 | tf_op jit(solution)/shard_map/ppermute | solution.py:222
  243.8 0.7 collective-permute-start.8
  244.5 0.4 collective-permute-done.7.refs_9_
  244.9 0.7 collective-permute-done.8.refs_10_
  245.6 17.6 %all-gather.3.cloned.1.call-done = bf16[384,64,128]{2,1,0:T(8,128)(2,1)} async-done(((bf16[48,64,128]{2,1,0:T(8,128)(2,1)}), bf16[384,64,128]{2,1,0:T(8,128)(2,1)}) %all-gather.3.cloned.1.call-update) | async-done | bytes 6291472 | tf_op jit(solution)/shard_map/all_gather | solution.py:282
  263.2 9.5 %shard_map.50 = bf16[2,48,64,450]{3,2,1,0:T(8,128)(2,1)} custom-call(bf16[464,768]{1,0:T(8,128)(2,1)} %fusion.9.table, bf16[8,48,64,128]{3,2,1,0:T(8,128)(2,1)} %bitcast.25, bf16[48,32,128]{2,1,0:T(8,128)(2,1)} %copy-done.4, bf16[48,32,128]{2,1,0:T(8,128)(2,1)} %copy-done.6, bf16[48,32,128]{2,1,0:T(8,128)(2,1)} %copy-done.7, ...), custom_call_target="tpu_custom_call" | custom-call | tf_op jit(solution)/shard_map/pallas_call | solution.py:198
  (52 shorter events, 0.2 us)
Async XLA Ops:
  12.9 51.2 %all-to-all-start = ((bf16[16,135,720]{2,1,0:T(8,128)(2,1)}), bf16[16,135,720]{2,1,0:T(8,128)(2,1)}, u32[]{:S(2)}, u32[]{:S(2)}) async-start(bf16[16,135,720]{2,1,0:T(8,128)(2,1)} %reshape.313), calls=%async_computation | async-start | bytes 6684672 | tf_op jit(solution)/shard_map/all_to_all | solution.py:40
  21.6 102.7 %reduce-scatter.2.cloned.1.call-start = ((), (), s32[]{:S(2)}) async-start(), calls=%async_computation.7 | async-start | bytes 9953280 | tf_op jit(solution)/shard_map/reduce_scatter | solution.py:248
  21.6 2.3 copy-start
  23.9 8.3 %copy-start.3 = (bf16[96,45,180]{0,2,1:T(8,128)(2,1)S(1)}, bf16[96,45,180]{0,2,1:T(8,128)(2,1)}, u32[]{:S(2)}) copy-start(bf16[96,45,180]{0,2,1:T(8,128)(2,1)} %param.4) | copy-start | bytes 4665604
  26.2 2.1 copy-start.2
  36.1 3.5 %copy-start.1 = (bf16[8,45,96,96]{3,2,1,0:T(8,128)(2,1)}, bf16[8,45,96,96]{3,2,1,0:T(8,128)(2,1)S(1)}, u32[]{:S(2)}) copy-start(bf16[8,45,96,96]{3,2,1,0:T(8,128)(2,1)S(1)} %shard_map.46) | copy-start | bytes 19906564
  64.2 11.1 %copy-start.5 = (bf16[45,96,192]{2,1,0:T(8,128)(2,1)S(1)}, bf16[45,96,192]{2,1,0:T(8,128)(2,1)}, u32[]{:S(2)}) copy-start(bf16[45,96,192]{2,1,0:T(8,128)(2,1)} %param.6) | copy-start | bytes 4976644
  64.2 65.1 %all-to-all-start.1 = ((bf16[16,1088,128]{2,1,0:T(8,128)(2,1)}), bf16[16,1088,128]{2,1,0:T(8,128)(2,1)}, u32[]{:S(2)}, u32[]{:S(2)}) async-start(bf16[16,1088,128]{2,1,0:T(8,128)(2,1)} %copy-done.2), calls=%async_computation.2 | async-start | bytes 8912896 | tf_op jit(solution)/shard_map/all_to_all | solution.py:40
  74.5 188.6 %all-gather.3.cloned.1.call-start = ((), (), s32[]{:S(2)}) async-start(), calls=%async_computation.8 | async-start | bytes 7077888 | tf_op jit(solution)/shard_map/all_gather | solution.py:282
  212.7 50.5 %copy-start.4 = (bf16[48,32,128]{2,1,0:T(8,128)(2,1)}, bf16[48,32,128]{2,1,0:T(8,128)(2,1)S(1)}, u32[]{:S(2)}) copy-start(bf16[48,32,128]{2,1,0:T(8,128)(2,1)S(1)} %get-tuple-element.30.refs_1_) | copy-start | bytes 1179652
  212.7 13.0 %collective-permute-start = (bf16[48,32,128]{2,1,0:T(8,128)(2,1)S(1)}, bf16[48,32,128]{2,1,0:T(8,128)(2,1)S(1)}, u32[]{:S(2)}, u32[]{:S(2)}) collective-permute-start(bf16[48,32,128]{2,1,0:T(8,128)(2,1)S(1)} %get-tuple-element.30.refs_1_), channel_id=1, source_target_pairs={{0,2},{1,3},{2,4},{3,5},{4,6},{5,7},{6,0},{7,1},{8,10},{9,11},{10,... | collective-permute-start | bytes 1179656 | tf_op jit(solution)/shard_map/ppermute | solution.py:219
  214.0 11.8 %collective-permute-start.1 = (bf16[48,32,128]{2,1,0:T(8,128)(2,1)S(1)}, bf16[48,32,128]{2,1,0:T(8,128)(2,1)S(1)}, u32[]{:S(2)}, u32[]{:S(2)}) collective-permute-start(bf16[48,32,128]{2,1,0:T(8,128)(2,1)S(1)} %get-tuple-element.30.refs_1_), channel_id=1, source_target_pairs={{0,6},{1,7},{2,0},{3,1},{4,2},{5,3},{6,4},{7,5},{8,14},{9,15},{10,... | collective-permute-start | bytes 1179656 | tf_op jit(solution)/shard_map/ppermute | solution.py:219
  215.4 29.1 %collective-permute-start.4 = (bf16[48,32,128]{2,1,0:T(8,128)(2,1)S(1)}, bf16[48,32,128]{2,1,0:T(8,128)(2,1)S(1)}, u32[]{:S(2)}, u32[]{:S(2)}) collective-permute-start(bf16[48,32,128]{2,1,0:T(8,128)(2,1)S(1)} %get-tuple-element.30.refs_1_), channel_id=1, source_target_pairs={{0,1},{1,0},{2,3},{3,2},{4,5},{5,4},{6,7},{7,6},{8,9},{9,8},{10,11... | collective-permute-start | bytes 1179656 | tf_op jit(solution)/shard_map/ppermute | solution.py:222
  225.7 37.5 %copy-start.6 = (bf16[48,32,128]{2,1,0:T(8,128)(2,1)}, bf16[48,32,128]{2,1,0:T(8,128)(2,1)S(1)}, u32[]{:S(2)}) copy-start(bf16[48,32,128]{2,1,0:T(8,128)(2,1)S(1)} %collective-permute-done.refs_2_) | copy-start | bytes 1179652
  225.7 11.5 %collective-permute-start.2 = (bf16[48,16,128]{2,1,0:T(8,128)(2,1)S(1)}, bf16[48,16,128]{2,1,0:T(8,128)(2,1)S(1)}, u32[]{:S(2)}, u32[]{:S(2)}) collective-permute-start(bf16[48,16,128]{2,1,0:T(8,128)(2,1)S(1)} %slice.16), channel_id=1, source_target_pairs={{0,2},{1,3},{2,4},{3,5},{4,6},{5,7},{6,0},{7,1},{8,10},{9,11},{10,... | collective-permute-start | bytes 589832 | tf_op jit(solution)/shard_map/ppermute | solution.py:219
  225.8 37.4 %copy-start.7 = (bf16[48,32,128]{2,1,0:T(8,128)(2,1)}, bf16[48,32,128]{2,1,0:T(8,128)(2,1)S(1)}, u32[]{:S(2)}) copy-start(bf16[48,32,128]{2,1,0:T(8,128)(2,1)S(1)} %collective-permute-done.1.refs_3_) | copy-start | bytes 1179652
  225.8 18.0 %collective-permute-start.3 = (bf16[48,16,128]{2,1,0:T(8,128)(2,1)S(1)}, bf16[48,16,128]{2,1,0:T(8,128)(2,1)S(1)}, u32[]{:S(2)}, u32[]{:S(2)}) collective-permute-start(bf16[48,16,128]{2,1,0:T(8,128)(2,1)S(1)} %slice.17), channel_id=1, source_target_pairs={{0,6},{1,7},{2,0},{3,1},{4,2},{5,3},{6,4},{7,5},{8,14},{9,15},{10,... | collective-permute-start | bytes 589832 | tf_op jit(solution)/shard_map/ppermute | solution.py:219
  228.5 17.1 %collective-permute-start.5 = (bf16[48,32,128]{2,1,0:T(8,128)(2,1)S(1)}, bf16[48,32,128]{2,1,0:T(8,128)(2,1)S(1)}, u32[]{:S(2)}, u32[]{:S(2)}) collective-permute-start(bf16[48,32,128]{2,1,0:T(8,128)(2,1)S(1)} %collective-permute-done.refs_2_), channel_id=1, source_target_pairs={{0,1},{1,0},{2,3},{3,2},{4,5},{5,4},{6,7},{7,6},{8,9},{9,8},{10,11... | collective-permute-start | bytes 1179656 | tf_op jit(solution)/shard_map/ppermute | solution.py:222
  237.1 8.5 %collective-permute-start.6 = (bf16[48,32,128]{2,1,0:T(8,128)(2,1)S(1)}, bf16[48,32,128]{2,1,0:T(8,128)(2,1)S(1)}, u32[]{:S(2)}, u32[]{:S(2)}) collective-permute-start(bf16[48,32,128]{2,1,0:T(8,128)(2,1)S(1)} %collective-permute-done.1.refs_3_), channel_id=1, source_target_pairs={{0,1},{1,0},{2,3},{3,2},{4,5},{5,4},{6,7},{7,6},{8,9},{9,8},{10,11... | collective-permute-start | bytes 1179656 | tf_op jit(solution)/shard_map/ppermute | solution.py:222
  237.1 26.0 %copy-start.11 = (bf16[48,16,128]{2,1,0:T(8,128)(2,1)}, bf16[48,16,128]{2,1,0:T(8,128)(2,1)S(1)}, u32[]{:S(2)}) copy-start(bf16[48,16,128]{2,1,0:T(8,128)(2,1)S(1)} %collective-permute-done.2.refs_4_) | copy-start | bytes 589828
  237.1 7.8 %collective-permute-start.7 = (bf16[48,16,128]{2,1,0:T(8,128)(2,1)S(1)}, bf16[48,16,128]{2,1,0:T(8,128)(2,1)S(1)}, u32[]{:S(2)}, u32[]{:S(2)}) collective-permute-start(bf16[48,16,128]{2,1,0:T(8,128)(2,1)S(1)} %collective-permute-done.2.refs_4_), channel_id=1, source_target_pairs={{0,1},{1,0},{2,3},{3,2},{4,5},{5,4},{6,7},{7,6},{8,9},{9,8},{10,11... | collective-permute-start | bytes 589832 | tf_op jit(solution)/shard_map/ppermute | solution.py:222
  243.8 19.3 %copy-start.12 = (bf16[48,16,128]{2,1,0:T(8,128)(2,1)}, bf16[48,16,128]{2,1,0:T(8,128)(2,1)S(1)}, u32[]{:S(2)}) copy-start(bf16[48,16,128]{2,1,0:T(8,128)(2,1)S(1)} %collective-permute-done.3.refs_5_) | copy-start | bytes 589828
  243.8 1.7 collective-permute-start.8
  244.5 18.7 %copy-start.8 = (bf16[48,32,128]{2,1,0:T(8,128)(2,1)}, bf16[48,32,128]{2,1,0:T(8,128)(2,1)S(1)}, u32[]{:S(2)}) copy-start(bf16[48,32,128]{2,1,0:T(8,128)(2,1)S(1)} %collective-permute-done.4.refs_6_) | copy-start | bytes 1179652
  244.9 18.3 %copy-start.13 = (bf16[48,16,128]{2,1,0:T(8,128)(2,1)}, bf16[48,16,128]{2,1,0:T(8,128)(2,1)S(1)}, u32[]{:S(2)}) copy-start(bf16[48,16,128]{2,1,0:T(8,128)(2,1)S(1)} %collective-permute-done.7.refs_9_) | copy-start | bytes 589828
  245.6 17.6 %copy-start.14 = (bf16[48,16,128]{2,1,0:T(8,128)(2,1)}, bf16[48,16,128]{2,1,0:T(8,128)(2,1)S(1)}, u32[]{:S(2)}) copy-start(bf16[48,16,128]{2,1,0:T(8,128)(2,1)S(1)} %collective-permute-done.8.refs_10_) | copy-start | bytes 589828
  245.6 17.6 %copy-start.9 = (bf16[48,32,128]{2,1,0:T(8,128)(2,1)}, bf16[48,32,128]{2,1,0:T(8,128)(2,1)S(1)}, u32[]{:S(2)}) copy-start(bf16[48,32,128]{2,1,0:T(8,128)(2,1)S(1)} %collective-permute-done.5.refs_7_) | copy-start | bytes 1179652
  245.6 17.6 %copy-start.10 = (bf16[48,32,128]{2,1,0:T(8,128)(2,1)}, bf16[48,32,128]{2,1,0:T(8,128)(2,1)S(1)}, u32[]{:S(2)}) copy-start(bf16[48,32,128]{2,1,0:T(8,128)(2,1)S(1)} %collective-permute-done.6.refs_8_) | copy-start | bytes 1179652
Sparse Core Ops, SparseCore 0:
  64.3 59.9 reduce-scatter.1
  212.8 50.3 all-gather.2
